TPU v7x, 32 devices: a whole 2x2x4 slice. The times are simulated.
32 devices in a mesh: col: 8 (over y, x, core), sub: 4 (over z).
Axes of the slice: x: 2, y: 2, z: 4, core: 2. Of those that a mesh axis runs over, the one named last changes fastest.
Arguments:
- vectors: bfloat16 [131072, 128], P(('col', 'sub')), may hold values from -6 to 6
- near_blocks: bfloat16 [512, 4, 256, 256], P(('col', 'sub')), may hold values from -0.1875 to 0.1875
- near_index: int32 [512, 4], P(('col', 'sub')), may hold values from 0 to 511, as said below
- leaf_basis: bfloat16 [512, 32, 256], P(('col', 'sub')), may hold values from -0.375 to 0.375
- leaf_transfer: float32 [512, 32, 32], P(('col', 'sub')), may hold values from -0.25 to 0.25
- leaf_coupling: float32 [512, 8, 32, 32], P(('col', 'sub')), may hold values from -0.375 to 0.375
- leaf_far: int32 [512, 8], P(('col', 'sub')), may hold values from 0 to 511, as said below
- cluster_transfer: float32 [32, 32, 32], P(('col', 'sub')), may hold values from -0.5 to 0.5
- cluster_coupling: float32 [32, 4, 32, 32], P(('col', 'sub')), may hold values from -0.5 to 0.5
- cluster_partner: int32 [32, 4], P(('col', 'sub')), may hold values from 0 to 3
- top_coupling: float32 [8, 8, 32, 32], P('col'), may hold values from -0.375 to 0.375
- top_partner: int32 [8, 8], P('col'), may hold values from 0 to 7
Outputs:
- products: bfloat16 [131072, 128], P(('col', 'sub'))
Inputs may be any that keep to these rules, and one draw needn't show every extreme that they name: `near_index`: slot 0 of leaf i is i itself; every entry lies within 16 leaves of i; slot 1 is exactly 16 leaves away from i. `leaf_far`: every entry lies within 16 leaves of its row leaf i; slots 0 and 1 are exactly 16 leaves away from i.
All inputs are finite; a program needn't handle non-finite values.
Results may differ from a plain program's by a relative error of at most 0.0034.
Values may be sent and summed in bfloat16 or wider, within the bound.
No kernel may reach another device: no remote copies, remote signals or barrier semaphores. Data moves between devices by JAX's collectives and lax.ppermute only.
A program may use at most 64 MiB of HBM per device.

v0:
```python
import jax
import jax.numpy as jnp
from jax import lax
from jax.sharding import PartitionSpec as P

HIGHEST = lax.Precision.HIGHEST


def with_halo(block, sides, width):
    for axis, dim in sides:
        count = lax.axis_size(axis)
        forward = [(i, i + 1) for i in range(count - 1)]
        backward = [(target, source) for source, target in forward]
        low = lax.ppermute(
            lax.slice_in_dim(block, block.shape[dim] - width, None, axis=dim), axis, forward
        )
        high = lax.ppermute(lax.slice_in_dim(block, 0, width, axis=dim), axis, backward)
        block = jnp.concatenate([low, block, high], axis=dim)
    return block


def local(
    vectors,
    near_blocks,
    near_index,
    leaf_basis,
    leaf_transfer,
    leaf_coupling,
    leaf_far,
    cluster_transfer,
    cluster_coupling,
    cluster_partner,
    top_coupling,
    top_partner,
):
    leaves_here = leaf_basis.shape[0]
    leaf_rows = leaf_basis.shape[2]
    columns = vectors.shape[1]
    window_start = lax.axis_index(("col", "sub")) * leaves_here - leaves_here
    widened = with_halo(vectors, ((("col", "sub"), 0),), leaves_here * leaf_rows)
    window_vec = widened.reshape(3 * leaves_here, leaf_rows, columns)
    own_vec = vectors.reshape(leaves_here, leaf_rows, columns)
    leaf_coefs = jnp.einsum("lrp,lpc->lrc", leaf_basis, own_vec, preferred_element_type=jnp.float32)
    window_coefs = with_halo(leaf_coefs, ((("col", "sub"), 0),), leaves_here)
    cluster_coef = jnp.einsum("lrs,lrc->sc", leaf_transfer, leaf_coefs, precision=HIGHEST)
    sub_coefs = lax.all_gather(cluster_coef[None], "sub", axis=0, tiled=True)
    cluster_field = jnp.einsum(
        "krs,ksc->rc", cluster_coupling[0], sub_coefs[cluster_partner[0]], precision=HIGHEST
    )
    upward = jnp.dot(cluster_transfer[0].T, cluster_coef, precision=HIGHEST)
    top_coef = lax.psum(upward, "sub")
    col_coefs = lax.all_gather(top_coef[None], "col", axis=0, tiled=True)
    top_field = jnp.einsum(
        "krs,ksc->rc", top_coupling[0], col_coefs[top_partner[0]], precision=HIGHEST
    )
    cluster_field = cluster_field + jnp.dot(cluster_transfer[0], top_field, precision=HIGHEST)
    far_coefs = window_coefs[leaf_far - window_start]
    leaf_field = jnp.einsum("lkrs,lksc->lrc", leaf_coupling, far_coefs, precision=HIGHEST)
    leaf_field = leaf_field + jnp.einsum(
        "lrs,sc->lrc", leaf_transfer, cluster_field, precision=HIGHEST
    )
    rounded = leaf_field.astype(jnp.bfloat16)
    picked = window_vec[near_index - window_start]
    near_part = jnp.einsum(
        "lkij,lkjc->lic", near_blocks, picked, preferred_element_type=jnp.float32
    )
    far_part = jnp.einsum("lrp,lrc->lpc", leaf_basis, rounded, preferred_element_type=jnp.float32)
    return (near_part + far_part).astype(jnp.bfloat16).reshape(leaves_here * leaf_rows, columns)


def solution(mesh):
    in_specs = (
        P(("col", "sub"), None),
        P(("col", "sub"), None, None, None),
        P(("col", "sub"), None),
        P(("col", "sub"), None, None),
        P(("col", "sub"), None, None),
        P(("col", "sub"), None, None, None),
        P(("col", "sub"), None),
        P(("col", "sub"), None, None),
        P(("col", "sub"), None, None, None),
        P(("col", "sub"), None),
        P("col", None, None, None),
        P("col", None),
    )
    out_specs = P(("col", "sub"), None)
    return jax.shard_map(local, mesh=mesh, in_specs=in_specs, out_specs=out_specs, check_vma=False)
```

profile of v0, /device:TPU:0, one launch (start us, length us, event | category | flops | bytes accessed | tf_op | source)
XLA Modules:
  0.0 138.5 jit_solution(11745126108896459472)
XLA Ops:
  0.0 0.0 copy-start
  0.0 0.0 copy-start.4
  0.0 1.7 %fusion.12 = f32[16,32,128]{2,1,0:T(8,128)S(1)} fusion(bf16[16,32,256]{2,1,0:T(8,128)(2,1)} %param.15, bf16[16,256,128]{2,1,0:T(8,128)(2,1)} %bitcast.79), kind=kOutput, calls=%fused_computation.33 | convolution fusion | flops 33554432 | bytes 1572864 | tf_op jit(solution)/shard_map/lrp,lpc->lrc/dot_general | solution.py:43
  1.7 1.3 collective-permute-start.3
  3.0 6.3 %collective-permute-start.2 = (f32[16,32,128]{2,1,0:T(8,128)S(1)}, f32[16,32,128]{2,1,0:T(8,128)}, u32[]{:S(2)}, u32[]{:S(2)}) collective-permute-start(f32[16,32,128]{2,1,0:T(8,128)S(1)} %fusion.12), channel_id=1, source_target_pairs={{0,1},{1,2},{2,3},{3,4},{4,5},{5,6},{6,7},{7,8},{8,9},{9,10},{10,1... | collective-permute-start | bytes 786440 | tf_op jit(solution)/shard_map/ppermute | solution.py:14
  9.3 1.3 collective-permute-start.1
  10.6 5.6 %collective-permute-start = (bf16[4096,128]{1,0:T(8,128)(2,1)}, bf16[4096,128]{1,0:T(8,128)(2,1)}, u32[]{:S(2)}, u32[]{:S(2)}) collective-permute-start(bf16[4096,128]{1,0:T(8,128)(2,1)} %param.12), channel_id=1, source_target_pairs={{0,1},{1,2},{2,3},{3,4},{4,5},{5,6},{6,7},{7,8},{8,9},{9,10},{10,1... | collective-permute-start | bytes 3145736 | tf_op jit(solution)/shard_map/ppermute | solution.py:14
  16.1 0.7 fusion.10
  16.8 0.7 fusion.11
  17.5 0.7 compare_select_fusion.1
  18.1 0.7 compare_select_fusion
  18.9 0.1 copy.24
  18.9 0.1 reshape.78
  19.0 1.5 %fusion.13 = f32[128,32,1]{0,1,2:T(8,128)S(1)} fusion(f32[16,32,128]{2,1,0:T(8,128)S(1)} %fusion.12, f32[16,32,32]{2,1,0:T(8,128)} %param.16), kind=kOutput, calls=%fused_computation.34 | convolution fusion | flops 25165824 | bytes 344064 | tf_op jit(solution)/shard_map/lrs,lrc->sc/dot_general | solution.py:45
  20.5 0.9 convolution_bitcast_fusion.3
  21.5 53.2 %psum.7 = f32[1,32,128]{2,1,0:T(8,128)S(1)} all-reduce(f32[1,32,128]{2,1,0:T(8,128)S(1)} %convolution_bitcast_fusion.3), channel_id=1, replica_groups=mesh['col'=8,'sub'=4] {'sub'}, use_global_device_ids=true, to_apply=%region_0.0 | all-reduce | flops 4096 | bytes 32768 | tf_op jit(solution)/shard_map/psum | solution.py:51
  74.7 13.1 %all-gather = f32[128,128]{1,0:T(8,128)S(1)} all-gather(f32[32,128]{1,0:T(8,128)S(1)} %bitcast.81), channel_id=2, replica_groups=mesh['col'=8,'sub'=4] {'sub'}, dimensions={0}, use_global_device_ids=true | all-gather | bytes 81920 | tf_op jit(solution)/shard_map/all_gather | solution.py:46
  87.8 13.1 %all_gather.7 = f32[8,32,128]{2,1,0:T(8,128)S(1)} all-gather(f32[1,32,128]{2,1,0:T(8,128)S(1)} %psum.7), channel_id=1, replica_groups=mesh['col'=8,'sub'=4] {'col'}, dimensions={0}, use_global_device_ids=true | all-gather | bytes 147456 | tf_op jit(solution)/shard_map/all_gather | solution.py:52
  100.9 0.6 gather_fusion.2
  101.5 1.1 convolution_bitcast_fusion.4
  102.6 0.6 gather_fusion.3
  103.1 1.2 convolution_bitcast_fusion.2
  104.4 0.1 copy.22
  104.5 0.1 reshape.70
  104.6 0.0 copy-done.4
  104.6 0.1 fusion.4
  104.7 0.0 collective-permute-done.3
  104.7 0.0 collective-permute-done.2
  104.8 1.0 pad_maximum_fusion.1
  105.8 2.1 %gather_fusion.1 = f32[128,32,128]{2,1,0:T(8,128)} fusion(f32[48,32,128]{2,1,0:T(8,128)S(1)} %pad_maximum_fusion.1, s32[1024]{0:T(1024)S(1)} %pad_clamp_fusion.2), kind=kCustom, calls=%fused_computation.1 | custom fusion | bytes 4194816 | tf_op jit(solution)/shard_map/gather | solution.py:57
  107.9 0.0 copy-start.3
  107.9 0.0 copy-start.2
  107.9 0.0 copy-done
  107.9 0.0 copy-start.1
  107.9 4.4 %convolution_bitcast_fusion.1 = f32[16,32,128]{2,1,0:T(8,128)S(1)} fusion(f32[16,8,32,128]{3,2,1,0:T(8,128)} %bitcast.78, f32[16,8,32,32]{3,2,1,0:T(8,128)S(1)} %copy-done), kind=kOutput, calls=%fused_computation.10 | convolution fusion | flops 201326592 | bytes 2883584 | tf_op jit(solution)/shard_map/lkrs,lksc->lrc/dot_general | solution.py:58
  112.3 0.0 copy-done.3
  112.4 0.4 fusion.3
  112.7 0.0 copy-done.2
  112.7 1.9 %fusion.14 = f32[16,128,256]{2,1,0:T(8,128)} fusion(bf16[16,32,128]{2,1,0:T(8,128)(2,1)S(1)} %fusion.3, bf16[16,32,256]{2,1,0:T(8,128)(2,1)S(1)} %copy-done.2), kind=kOutput, calls=%fused_computation.35 | convolution fusion | flops 33554432 | bytes 2490368 | tf_op jit(solution)/shard_map/lrp,lrc->lpc/dot_general | solution.py:67
  114.6 0.0 collective-permute-done.1
  114.6 0.0 collective-permute-done
  114.6 0.0 copy-done.1
  114.6 9.6 %pad_maximum_fusion = bf16[12288,128]{1,0:T(8,128)(2,1)} fusion(bf16[4096,128]{1,0:T(8,128)(2,1)} %collective-permute-done.1, bf16[4096,128]{1,0:T(8,128)(2,1)S(1)} %copy-done.1, bf16[4096,128]{1,0:T(8,128)(2,1)} %collective-permute-done), kind=kLoop, calls=%fused_computation.4 | loop fusion | flops 9437184 | bytes 6291456 | tf_op jit(solution)/shard_map/concatenate | solution.py:18
  124.2 4.9 %gather_fusion = bf16[64,256,128]{2,1,0:T(8,128)(2,1)} fusion(bf16[48,256,128]{2,1,0:T(8,128)(2,1)} %bitcast.76, s32[1024]{0:T(1024)S(1)} %pad_clamp_fusion.3), kind=kCustom, calls=%fused_computation | custom fusion | bytes 8388864 | tf_op jit(solution)/shard_map/gather | solution.py:63
  129.1 8.1 %fusion.1 = bf16[16,256,128]{1,2,0:T(8,128)(2,1)S(1)} fusion(f32[16,128,256]{2,1,0:T(8,128)} %fusion.14, bf16[16,4,256,128]{3,2,1,0:T(8,128)(2,1)} %bitcast.77, bf16[16,4,256,256]{3,2,1,0:T(8,128)(2,1)} %param.13), kind=kOutput, calls=%fused_computation.7 | convolution fusion | flops 1074790400 | bytes 15728640 | tf_op jit(solution)/shard_map/lkij,lkjc->lic/dot_general | solution.py:64
  137.2 1.3 copy.26
  (4 shorter events, 0.0 us)
Async XLA Ops:
  0.0 107.9 %copy-start = (f32[16,8,32,32]{3,2,1,0:T(8,128)S(1)}, f32[16,8,32,32]{3,2,1,0:T(8,128)}, u32[]{:S(2)}) copy-start(f32[16,8,32,32]{3,2,1,0:T(8,128)} %param.17) | copy-start | bytes 1572868
  0.0 104.6 %copy-start.4 = (f32[1,32,32]{2,1,0:T(8,128)S(1)}, f32[1,32,32]{2,1,0:T(8,128)}, u32[]{:S(2)}) copy-start(f32[1,32,32]{2,1,0:T(8,128)} %param.19) | copy-start | bytes 12292
  1.7 103.0 %collective-permute-start.3 = (f32[16,32,128]{2,1,0:T(8,128)S(1)}, f32[16,32,128]{2,1,0:T(8,128)S(1)}, u32[]{:S(2)}, u32[]{:S(2)}) collective-permute-start(f32[16,32,128]{2,1,0:T(8,128)S(1)} %fusion.12), channel_id=1, source_target_pairs={{1,0},{2,1},{3,2},{4,3},{5,4},{6,5},{7,6},{8,7},{9,8},{10,9},{11,1... | collective-permute-start | bytes 786440 | tf_op jit(solution)/shard_map/ppermute | solution.py:17
  3.0 101.7 %collective-permute-start.2 = (f32[16,32,128]{2,1,0:T(8,128)S(1)}, f32[16,32,128]{2,1,0:T(8,128)}, u32[]{:S(2)}, u32[]{:S(2)}) collective-permute-start(f32[16,32,128]{2,1,0:T(8,128)S(1)} %fusion.12), channel_id=1, source_target_pairs={{0,1},{1,2},{2,3},{3,4},{4,5},{5,6},{6,7},{7,8},{8,9},{9,10},{10,1... | collective-permute-start | bytes 786440 | tf_op jit(solution)/shard_map/ppermute | solution.py:14
  9.3 105.3 %collective-permute-start.1 = (bf16[4096,128]{1,0:T(8,128)(2,1)}, bf16[4096,128]{1,0:T(8,128)(2,1)}, u32[]{:S(2)}, u32[]{:S(2)}) collective-permute-start(bf16[4096,128]{1,0:T(8,128)(2,1)} %param.12), channel_id=1, source_target_pairs={{1,0},{2,1},{3,2},{4,3},{5,4},{6,5},{7,6},{8,7},{9,8},{10,9},{11,1... | collective-permute-start | bytes 3145736 | tf_op jit(solution)/shard_map/ppermute | solution.py:17
  10.6 104.0 %collective-permute-start = (bf16[4096,128]{1,0:T(8,128)(2,1)}, bf16[4096,128]{1,0:T(8,128)(2,1)}, u32[]{:S(2)}, u32[]{:S(2)}) collective-permute-start(bf16[4096,128]{1,0:T(8,128)(2,1)} %param.12), channel_id=1, source_target_pairs={{0,1},{1,2},{2,3},{3,4},{4,5},{5,6},{6,7},{7,8},{8,9},{9,10},{10,1... | collective-permute-start | bytes 3145736 | tf_op jit(solution)/shard_map/ppermute | solution.py:14
  107.9 4.4 %copy-start.3 = (f32[16,32,32]{2,1,0:T(8,128)S(1)}, f32[16,32,32]{2,1,0:T(8,128)}, u32[]{:S(2)}) copy-start(f32[16,32,32]{2,1,0:T(8,128)} %param.16) | copy-start | bytes 196612
  107.9 4.8 %copy-start.2 = (bf16[16,32,256]{2,1,0:T(8,128)(2,1)S(1)}, bf16[16,32,256]{2,1,0:T(8,128)(2,1)}, u32[]{:S(2)}) copy-start(bf16[16,32,256]{2,1,0:T(8,128)(2,1)} %param.15) | copy-start | bytes 786436
  107.9 6.7 %copy-start.1 = (bf16[4096,128]{1,0:T(8,128)(2,1)S(1)}, bf16[4096,128]{1,0:T(8,128)(2,1)}, u32[]{:S(2)}) copy-start(bf16[4096,128]{1,0:T(8,128)(2,1)} %param.12) | copy-start | bytes 3145732
where the time goes:
time: 139 us
  blocking collectives  79.4 us (57%)
  matrix products  21.4 us (15%)
  starting transfers between devices  14.4 us (10%)
  other arithmetic  13.3 us (10%)
  local copies, waits for them, and re-layouts  9.83 us (7%)
    psum x1, blocking collectives, local(): top_coef = lax.psum(upward, 'sub')  53.2 us
    all_gather x1, blocking collectives, local(): sub_coefs = lax.all_gather(cluster_coef[None], 'sub', axis=0, tiled=True)  13.1 us
    all_gather x1, blocking collectives, local(): col_coefs = lax.all_gather(top_coef[None], 'col', axis=0, tiled=True)  13.1 us
    ppermute x2, starting transfers between devices, with_halo(): lax.ppermute(lax.slice_in_dim(block, block.shape[dim] - width, None, axis...  11.8 us
    concatenate x2, other arithmetic, with_halo(): block = jnp.concatenate([low, block, high], axis=dim)  10.6 us
    dot_general x1, matrix products, local(): jnp.einsum('lkij,lkjc->lic', near_blocks, picked, preferred_element_type=...  8.07 us
    gather x1, local copies, waits for them, and re-layouts, local(): picked = window_vec[near_index - window_start]  4.92 us
    dot_general x1, matrix products, local(): jnp.einsum('lkrs,lksc->lrc', leaf_coupling, far_coefs, precision=HIGHEST)  4.43 us
  transfers between devices with their start and end apart: 4, of which 0 were waited for; matrix products, arithmetic and copies ran while one was open for 14% of the time, Pallas kernels for 0%

commit v1 on v0

v1 whole, which is shorter than its diff:
```python
import functools

import jax
import jax.numpy as jnp
from jax import lax
from jax.experimental import pallas as pl
from jax.experimental.pallas import tpu as pltpu
from jax.sharding import PartitionSpec as P

HIGHEST = lax.Precision.HIGHEST
BOTH = ("col", "sub")


def shift(value, step):
    count = lax.axis_size(BOTH)
    pairs = [(i, i + step) for i in range(count) if 0 <= i + step < count]
    return lax.ppermute(value, BOTH, pairs)


def gather_sub(value):
    count = lax.axis_size("sub")
    parts = [value]
    for step in range(1, count):
        pairs = [(i, (i + step) % count) for i in range(count)]
        parts.append(lax.ppermute(value, "sub", pairs))
    return jnp.stack(parts)


def gather_col(value):
    count = lax.axis_size("col")
    if count & (count - 1):
        return lax.all_gather(value, "col", axis=0), jnp.arange(count)
    stack = value[None]
    width = 1
    while width < count:
        pairs = [(i, i ^ width) for i in range(count)]
        stack = jnp.concatenate([stack, lax.ppermute(stack, "col", pairs)], axis=0)
        width *= 2
    return stack, jnp.arange(count) ^ lax.axis_index("col")


def near_first_body(leaves, slots, place_ref, blocks_ref, own_ref, high_ref, acc_ref):
    leaf = pl.program_id(0)
    rows = acc_ref.shape[0]
    acc_ref[...] = jnp.zeros_like(acc_ref)
    for k in range(slots):
        place = place_ref[leaf, k]

        def add(vec_ref, at, k=k):
            start = pl.multiple_of(at * rows, rows)
            acc_ref[...] += jnp.dot(
                blocks_ref[0, k], vec_ref[pl.ds(start, rows), :], preferred_element_type=jnp.float32
            )

        pl.when((place >= leaves) & (place < 2 * leaves))(lambda: add(own_ref, place - leaves))
        pl.when(place >= 2 * leaves)(lambda: add(high_ref, place - 2 * leaves))


def near_first(place, blocks, own, high):
    leaves, slots, rows, _ = blocks.shape
    columns = own.shape[1]
    whole = pl.BlockSpec((leaves * rows, columns), lambda i, p: (0, 0))
    return pl.pallas_call(
        functools.partial(near_first_body, leaves, slots),
        grid_spec=pltpu.PrefetchScalarGridSpec(
            num_scalar_prefetch=1,
            grid=(leaves,),
            in_specs=[
                pl.BlockSpec((1, slots, rows, rows), lambda i, p: (i, 0, 0, 0)),
                whole,
                whole,
            ],
            out_specs=pl.BlockSpec((rows, columns), lambda i, p: (i, 0)),
        ),
        out_shape=jax.ShapeDtypeStruct((leaves * rows, columns), jnp.float32),
        compiler_params=pltpu.CompilerParams(vmem_limit_bytes=24 * 2**20),
        cost_estimate=pl.CostEstimate(
            flops=2 * leaves * slots * rows * rows * columns,
            bytes_accessed=2 * leaves * slots * rows * rows,
            transcendentals=0,
        ),
        name="near_own_high",
    )(place, blocks, own, high)


def near_last_body(leaves, slots, place_ref, blocks_ref, low_ref, acc_ref, out_ref, held, sems):
    rows = held.shape[1]

    def copy(at):
        return pltpu.make_async_copy(
            blocks_ref.at[at // slots, lax.rem(at, slots)], held.at[at], sems.at[at]
        )

    @pl.loop(0, leaves * slots)
    def _(at):
        @pl.when(place_ref[at] < leaves)
        def _():
            copy(at).start()

    @pl.loop(0, leaves)
    def _(leaf):
        here = pl.ds(pl.multiple_of(leaf * rows, rows), rows)
        for k in range(slots):
            at = leaf * slots + k
            place = place_ref[at]

            @pl.when(place < leaves)
            def _():
                copy(at).wait()
                start = pl.multiple_of(place * rows, rows)
                acc_ref[here, :] += jnp.dot(
                    held[at], low_ref[pl.ds(start, rows), :], preferred_element_type=jnp.float32
                )

        out_ref[here, :] = acc_ref[here, :].astype(out_ref.dtype)


def near_last(place, blocks, low, acc):
    leaves, slots, rows, _ = blocks.shape
    columns = low.shape[1]
    return pl.pallas_call(
        functools.partial(near_last_body, leaves, slots),
        in_specs=[
            pl.BlockSpec(memory_space=pltpu.SMEM),
            pl.BlockSpec(memory_space=pl.ANY),
            pl.BlockSpec(memory_space=pltpu.VMEM),
            pl.BlockSpec(memory_space=pltpu.VMEM),
        ],
        out_specs=pl.BlockSpec(memory_space=pltpu.VMEM),
        out_shape=jax.ShapeDtypeStruct((leaves * rows, columns), low.dtype),
        scratch_shapes=[
            pltpu.VMEM((leaves * slots, rows, rows), blocks.dtype),
            pltpu.SemaphoreType.DMA((leaves * slots,)),
        ],
        compiler_params=pltpu.CompilerParams(vmem_limit_bytes=24 * 2**20),
        cost_estimate=pl.CostEstimate(
            flops=leaves * rows * rows * columns, bytes_accessed=4 * 2**20, transcendentals=0
        ),
        name="near_low",
    )(place.reshape(-1), blocks, low, acc)


def local(
    vectors,
    near_blocks,
    near_index,
    leaf_basis,
    leaf_transfer,
    leaf_coupling,
    leaf_far,
    cluster_transfer,
    cluster_coupling,
    cluster_partner,
    top_coupling,
    top_partner,
):
    leaves, rank, rows = leaf_basis.shape
    columns = vectors.shape[1]
    sub = lax.axis_index("sub")
    subs = lax.axis_size("sub")
    window_start = lax.axis_index(BOTH) * leaves - leaves

    high_vec = shift(vectors, -1)

    own_vec = vectors.reshape(leaves, rows, columns)
    leaf_coefs = jnp.einsum("lrp,lpc->lrc", leaf_basis, own_vec, preferred_element_type=jnp.float32)
    cluster_coef = jnp.einsum("lrs,lrc->sc", leaf_transfer, leaf_coefs, precision=HIGHEST)
    upward = jnp.dot(cluster_transfer[0].T, cluster_coef, precision=HIGHEST)
    gathered = gather_sub(jnp.stack([cluster_coef, upward]))

    low_coefs = shift(leaf_coefs, 1)
    high_coefs = shift(leaf_coefs, -1)
    later_vec, _ = lax.optimization_barrier((vectors, upward))
    low_vec = shift(later_vec, 1)

    col_coefs, col_place = gather_col(gathered[:, 1].sum(axis=0))
    sub_place = lax.rem(sub - cluster_partner[0] + subs, subs)
    cluster_field = jnp.einsum(
        "krs,ksc->rc", cluster_coupling[0], gathered[sub_place, 0], precision=HIGHEST
    )
    top_field = jnp.einsum(
        "krs,ksc->rc", top_coupling[0], col_coefs[col_place[top_partner[0]]], precision=HIGHEST
    )
    cluster_field = cluster_field + jnp.dot(cluster_transfer[0], top_field, precision=HIGHEST)

    near_place = jnp.clip(near_index - window_start, 0, 3 * leaves - 1)
    acc = near_first(near_place, near_blocks, vectors, high_vec)

    window_coefs = jnp.concatenate([low_coefs, leaf_coefs, high_coefs], axis=0)
    far_coefs = window_coefs[leaf_far - window_start]
    leaf_field = jnp.einsum("lkrs,lksc->lrc", leaf_coupling, far_coefs, precision=HIGHEST)
    leaf_field = leaf_field + jnp.einsum(
        "lrs,sc->lrc", leaf_transfer, cluster_field, precision=HIGHEST
    )
    rounded = leaf_field.astype(jnp.bfloat16)
    far_part = jnp.einsum("lrp,lrc->lpc", leaf_basis, rounded, preferred_element_type=jnp.float32)
    acc = acc + far_part.reshape(leaves * rows, columns)
    return near_last(near_place, near_blocks, low_vec, acc)


def solution(mesh):
    both = P(BOTH)
    in_specs = (both,) * 10 + (P("col"),) * 2
    return jax.shard_map(local, mesh=mesh, in_specs=in_specs, out_specs=both, check_vma=False)
```

time: 139 us -> 89.8 us (0.65)
  the two profiles are of different devices: /device:TPU:0 before, /device:TPU:4 now
where the time goes in v1:
time: 89.8 us; the launch traced here: 89 us
  starting transfers between devices  21.1 us (23%)
  Pallas kernels  20.2 us (22%)
  local copies, waits for them, and re-layouts  16.3 us (18%)
  matrix products  15.1 us (17%)
  other arithmetic  11.6 us (13%)
  waiting for transfers between devices  4.41 us (5%)
    ppermute x4, starting transfers between devices, shift(): return lax.ppermute(value, BOTH, pairs)  15 us
    pallas_call x1, Pallas kernels, near_first(): pl.pallas_call(functools.partial(near_first_body, leaves, slots), grid_sp...  12.1 us
    pallas_call x1, Pallas kernels, near_last(): pl.pallas_call(functools.partial(near_last_body, leaves, slots), in_specs...  8.17 us
    ppermute x3, starting transfers between devices, gather_sub(): parts.append(lax.ppermute(value, 'sub', pairs))  5.51 us
    unnamed x25, local copies, waits for them, and re-layouts  4.77 us
    ppermute x3, waiting for transfers between devices, gather_col(): stack = jnp.concatenate([stack, lax.ppermute(stack, 'col', pairs)], axis=0)  4.39 us
    dot_general x1, matrix products, local(): jnp.einsum('lkrs,lksc->lrc', leaf_coupling, far_coefs, precision=HIGHEST)  4.37 us
    gather x1, local copies, waits for them, and re-layouts, local(): far_coefs = window_coefs[leaf_far - window_start]  3.15 us
  transfers between devices with their start and end apart: 10, of which 2 were waited for; matrix products, arithmetic and copies ran while one was open for 39% of the time, Pallas kernels for 14%

profile of v1, /device:TPU:4, one launch (start us, length us, event | category | flops | bytes accessed | tf_op | source)
XLA Modules:
  0.0 89.0 jit_solution(4965293921298360320)
XLA Ops:
  0.0 1.7 %fusion.15 = f32[16,32,128]{2,1,0:T(8,128)S(1)} fusion(bf16[16,32,256]{2,1,0:T(8,128)(2,1)} %param.15, bf16[16,256,128]{2,1,0:T(8,128)(2,1)} %bitcast.76), kind=kOutput, calls=%fused_computation.45 | convolution fusion | flops 33554432 | bytes 1572864 | tf_op jit(solution)/shard_map/lrp,lpc->lrc/dot_general | solution.py:166
  1.7 1.5 %fusion.16 = f32[128,32,1]{0,1,2:T(8,128)S(1)} fusion(f32[16,32,128]{2,1,0:T(8,128)S(1)} %fusion.15, f32[16,32,32]{2,1,0:T(8,128)} %param.16), kind=kOutput, calls=%fused_computation.46 | convolution fusion | flops 25165824 | bytes 344064 | tf_op jit(solution)/shard_map/lrs,lrc->sc/dot_general | solution.py:167
  3.3 0.0 copy-done.10
  3.3 0.2 convolution_bitcast_fusion.5
  3.5 0.6 fusion.14
  4.1 1.6 %collective-permute-start.4 = (f32[2,32,128]{2,1,0:T(8,128)S(1)}, f32[2,32,128]{2,1,0:T(8,128)S(1)}, u32[]{:S(2)}, u32[]{:S(2)}) collective-permute-start(f32[2,32,128]{2,1,0:T(8,128)S(1)} %get-tuple-element.8), channel_id=1, source_target_pairs={{0,1},{1,2},{2,3},{3,0},{4,5},{5,6},{6,7},{7,4},{8,9},{9,10},{10,1... | collective-permute-start | bytes 98312 | tf_op jit(solution)/shard_map/ppermute | solution.py:25
  5.7 2.6 %collective-permute-start.5 = (f32[2,32,128]{2,1,0:T(8,128)S(1)}, f32[2,32,128]{2,1,0:T(8,128)S(1)}, u32[]{:S(2)}, u32[]{:S(2)}) collective-permute-start(f32[2,32,128]{2,1,0:T(8,128)S(1)} %get-tuple-element.8), channel_id=1, source_target_pairs={{0,2},{1,3},{2,0},{3,1},{4,6},{5,7},{6,4},{7,5},{8,10},{9,11},{10,... | collective-permute-start | bytes 98312 | tf_op jit(solution)/shard_map/ppermute | solution.py:25
  8.3 1.3 %collective-permute-start.6 = (f32[2,32,128]{2,1,0:T(8,128)S(1)}, f32[2,32,128]{2,1,0:T(8,128)S(1)}, u32[]{:S(2)}, u32[]{:S(2)}) collective-permute-start(f32[2,32,128]{2,1,0:T(8,128)S(1)} %get-tuple-element.8), channel_id=1, source_target_pairs={{0,3},{1,0},{2,1},{3,2},{4,7},{5,4},{6,5},{7,6},{8,11},{9,8},{10,9... | collective-permute-start | bytes 98312 | tf_op jit(solution)/shard_map/ppermute | solution.py:25
  9.6 2.6 %collective-permute-start.2 = (f32[16,32,128]{2,1,0:T(8,128)S(1)}, f32[16,32,128]{2,1,0:T(8,128)}, u32[]{:S(2)}, u32[]{:S(2)}) collective-permute-start(f32[16,32,128]{2,1,0:T(8,128)S(1)} %fusion.15), channel_id=1, source_target_pairs={{0,1},{1,2},{2,3},{3,4},{4,5},{5,6},{6,7},{7,8},{8,9},{9,10},{10,1... | collective-permute-start | bytes 786440 | tf_op jit(solution)/shard_map/ppermute | solution.py:17
  12.2 6.6 %collective-permute-start.3 = (f32[16,32,128]{2,1,0:T(8,128)S(1)}, f32[16,32,128]{2,1,0:T(8,128)}, u32[]{:S(2)}, u32[]{:S(2)}) collective-permute-start(f32[16,32,128]{2,1,0:T(8,128)S(1)} %fusion.15), channel_id=1, source_target_pairs={{1,0},{2,1},{3,2},{4,3},{5,4},{6,5},{7,6},{8,7},{9,8},{10,9},{11,1... | collective-permute-start | bytes 786440 | tf_op jit(solution)/shard_map/ppermute | solution.py:17
  18.8 0.6 gather_fusion.2
  19.5 0.6 fusion.13
  20.1 0.8 copy.17
  20.8 1.3 %compare_select_fusion = s32[16,8]{0,1:T(8,128)} fusion(s32[16,8]{0,1:T(8,128)} %param.18, s32[]{:T(128)S(6)} %sub.29), kind=kLoop, calls=%fused_computation.27 | loop fusion | flops 512 | bytes 1028 | tf_op jit(solution)/shard_map/select_n | solution.py:190
  22.1 1.3 %fusion.11 = s32[4]{0:T(128)} fusion(s32[1,4]{1,0:T(1,128)} %param.21, s32[]{:T(128)S(6)} %axis_index.14), kind=kLoop, calls=%fused_computation.40 | loop fusion | flops 52 | bytes 36 | tf_op jit(solution)/shard_map/concatenate | solution.py:179
  23.4 1.9 %collective-permute-start.1 = (bf16[4096,128]{1,0:T(8,128)(2,1)S(1)}, bf16[4096,128]{1,0:T(8,128)(2,1)}, u32[]{:S(2)}, u32[]{:S(2)}) collective-permute-start(bf16[4096,128]{1,0:T(8,128)(2,1)S(1)} %copy-done.3), channel_id=1, source_target_pairs={{1,0},{2,1},{3,2},{4,3},{5,4},{6,5},{7,6},{8,7},{9,8},{10,9},{11,1... | collective-permute-start | bytes 3145736 | tf_op jit(solution)/shard_map/ppermute | solution.py:17
  25.3 3.9 %collective-permute-start = (bf16[4096,128]{1,0:T(8,128)(2,1)S(1)}, bf16[4096,128]{1,0:T(8,128)(2,1)}, u32[]{:S(2)}, u32[]{:S(2)}) collective-permute-start(bf16[4096,128]{1,0:T(8,128)(2,1)S(1)} %copy-done.3), channel_id=1, source_target_pairs={{0,1},{1,2},{2,3},{3,4},{4,5},{5,6},{6,7},{7,8},{8,9},{9,10},{10,1... | collective-permute-start | bytes 3145736 | tf_op jit(solution)/shard_map/ppermute | solution.py:17
  29.3 0.6 copy-done.9
  29.9 0.8 pad_maximum_fusion.1
  30.7 0.6 slice_reduce_fusion
  31.3 1.3 %pad_clamp_fusion = s32[1024]{0:T(1024)} fusion(s32[8]{0:T(128)} %fusion.13), kind=kLoop, calls=%fused_computation.29 | loop fusion | flops 1024 | bytes 4128 | tf_op jit(solution)/shard_map/gather | solution.py:182
  32.6 1.3 %copy.19 = s32[16,8]{1,0:T(8,128)} copy(s32[16,8]{0,1:T(8,128)} %compare_select_fusion) | data formatting | bytes 1024 | tf_op jit(solution)/shard_map/select_n | solution.py:190
  33.9 0.8 reshape.99
  34.7 0.0 collective-permute-done.7
  34.7 1.4 %pad_maximum_fusion.5 = f32[2,32,128]{2,1,0:T(8,128)} fusion(f32[1,32,128]{2,1,0:T(8,128)} %collective-permute-done.7, f32[1,32,128]{2,1,0:T(8,128)} %bitcast.19), kind=kLoop, calls=%fused_computation.23 | loop fusion | flops 8192 | bytes 65536 | tf_op jit(solution)/shard_map/concatenate | solution.py:37
  36.1 0.6 collective-permute-start.8
  36.7 0.1 reshape.94.place_ref
  36.8 1.3 %gather_fusion.1 = f32[4,32,128]{2,1,0:T(8,128)} fusion(f32[4,2,32,128]{3,2,1,0:T(8,128)S(1)} %pad_maximum_fusion.1, s32[4]{0:T(128)} %fusion.11), kind=kCustom, calls=%fused_computation.1 | custom fusion | bytes 131104 | tf_op jit(solution)/shard_map/gather | solution.py:179
  38.1 2.2 %collective-permute-done.8 = f32[2,32,128]{2,1,0:T(8,128)} collective-permute-done((f32[2,32,128]{2,1,0:T(8,128)}, f32[2,32,128]{2,1,0:T(8,128)}, u32[]{:S(2)}, u32[]{:S(2)}) %collective-permute-start.8) | collective-permute-done | bytes 32800 | tf_op jit(solution)/shard_map/ppermute | solution.py:37
  40.3 0.8 pad_maximum_fusion.3
  41.1 2.1 %convolution_bitcast_fusion.4 = f32[128,32]{1,0:T(8,128)} fusion(f32[4,32,128]{2,1,0:T(8,128)} %gather_fusion.1, f32[1,4,32,32]{3,2,1,0:T(8,128)} %param.20), kind=kOutput, calls=%fused_computation.13 | convolution fusion | flops 6291456 | bytes 98304 | tf_op jit(solution)/shard_map/krs,ksc->rc/dot_general | solution.py:178
  43.2 2.2 %collective-permute-done.9 = f32[4,32,128]{2,1,0:T(8,128)S(1)} collective-permute-done((f32[4,32,128]{2,1,0:T(8,128)S(1)}, f32[4,32,128]{2,1,0:T(8,128)S(1)}, u32[]{:S(2)}, u32[]{:S(2)}) %collective-permute-start.9) | collective-permute-done | bytes 65568 | tf_op jit(solution)/shard_map/ppermute | solution.py:37
  45.4 0.8 pad_maximum_fusion.2
  46.2 1.3 %gather_fusion.3 = f32[8,32,128]{2,1,0:T(8,128)} fusion(f32[8,32,128]{2,1,0:T(8,128)S(1)} %pad_maximum_fusion.2, s32[1024]{0:T(1024)} %pad_clamp_fusion), kind=kCustom, calls=%fused_computation.3 | custom fusion | bytes 262176 | tf_op jit(solution)/shard_map/gather | solution.py:182
  47.5 2.0 %convolution_bitcast_fusion.3 = f32[128,32]{1,0:T(8,128)S(1)} fusion(f32[8,32,128]{2,1,0:T(8,128)} %gather_fusion.3, f32[1,8,32,32]{3,2,1,0:T(8,128)} %param.22), kind=kOutput, calls=%fused_computation.12 | convolution fusion | flops 12582912 | bytes 180224 | tf_op jit(solution)/shard_map/krs,ksc->rc/dot_general | solution.py:181
  49.5 1.1 %fusion.2 = f32[128,32,1]{1,0,2:T(8,128)S(1)} fusion(f32[128,32]{1,0:T(8,128)} %convolution_bitcast_fusion.4, f32[128,32]{1,0:T(8,128)S(1)} %convolution_bitcast_fusion.3, f32[1,32,32]{2,1,0:T(8,128)} %param.19), kind=kOutput, calls=%fused_computation.11 | convolution fusion | flops 1576960 | bytes 53248 | tf_op jit(solution)/shard_map/dot_general | solution.py:184
  50.5 2.0 %pad_maximum_fusion = f32[48,32,128]{2,1,0:T(8,128)} fusion(f32[16,32,128]{2,1,0:T(8,128)} %collective-permute-done.3, f32[16,32,128]{2,1,0:T(8,128)S(1)} %fusion.15, f32[16,32,128]{2,1,0:T(8,128)} %collective-permute-done.2), kind=kLoop, calls=%fused_computation.15 | loop fusion | flops 393216 | bytes 1572864 | tf_op jit(solution)/shard_map/concatenate | solution.py:189
  52.5 3.1 %gather_fusion = f32[128,32,128]{2,1,0:T(8,128)} fusion(f32[48,32,128]{2,1,0:T(8,128)} %pad_maximum_fusion, s32[1024]{0:T(1024)S(1)} %pad_clamp_fusion.2), kind=kCustom, calls=%fused_computation | custom fusion | bytes 4194816 | tf_op jit(solution)/shard_map/gather | solution.py:190
  55.7 4.4 %convolution_bitcast_fusion.2 = f32[16,32,128]{2,1,0:T(8,128)S(1)} fusion(f32[16,8,32,128]{3,2,1,0:T(8,128)} %bitcast.77, f32[16,8,32,32]{3,2,1,0:T(8,128)S(1)} %copy-done), kind=kOutput, calls=%fused_computation.8 | convolution fusion | flops 201326592 | bytes 2883584 | tf_op jit(solution)/shard_map/lkrs,lksc->lrc/dot_general | solution.py:191
  60.0 0.4 fusion.1
  60.5 1.8 %convolution_bitcast_fusion = f32[16,256,128]{1,2,0:T(8,128)} fusion(bf16[16,32,128]{2,1,0:T(8,128)(2,1)S(1)} %fusion.1, bf16[16,32,256]{2,1,0:T(8,128)(2,1)S(1)} %copy-done.5), kind=kOutput, calls=%fused_computation.5 | convolution fusion | flops 33554432 | bytes 2490368 | tf_op jit(solution)/shard_map/lrp,lrc->lpc/dot_general | solution.py:196
  62.3 2.9 %copy.20 = f32[16,256,128]{2,1,0:T(8,128)} copy(f32[16,256,128]{1,2,0:T(8,128)} %convolution_bitcast_fusion) | data formatting | bytes 4194304 | tf_op jit(solution)/shard_map/lrp,lrc->lpc/dot_general | solution.py:196
  65.2 0.0 collective-permute-done.1.high_ref
  65.2 3.4 %copy-done.1 = bf16[16,4,256,256]{3,2,1,0:T(8,128)(2,1)S(1)} copy-done((bf16[16,4,256,256]{3,2,1,0:T(8,128)(2,1)S(1)}, bf16[16,4,256,256]{3,2,1,0:T(8,128)(2,1)}, u32[]{:S(2)}) %copy-start.1) | copy-done | bytes 8388632
  68.5 12.1 %near_own_high.1 = f32[4096,128]{1,0:T(8,128)S(1)} custom-call(s32[16,4]{1,0:T(8,128)S(1)} %subtract_clamp_fusion.place_ref, bf16[16,4,256,256]{3,2,1,0:T(8,128)(2,1)S(1)} %copy-done.1, bf16[4096,128]{1,0:T(8,128)(2,1)S(1)} %copy-done.3, bf16[4096,128]{1,0:T(8,128)(2,1)} %collective-permute-done.1.high_ref), custom_call_target="tpu_custom_call" | custom-call | flops 1073741824 | bytes 8388608 | tf_op jit(solution)/shard_map/near_own_high/pallas_call | solution.py:63
  80.6 0.2 bitcast_add_fusion.acc_ref
  80.8 0.0 collective-permute-done.low_ref
  80.9 8.2 %near_low.1 = bf16[4096,128]{1,0:T(8,128)(2,1)} custom-call(s32[64]{0:T(128)S(1)} %reshape.94.place_ref, bf16[16,4,256,256]{3,2,1,0:T(8,128)(2,1)S(1)} %copy-done.2, bf16[4096,128]{1,0:T(8,128)(2,1)} %collective-permute-done.low_ref, f32[4096,128]{1,0:T(8,128)S(1)} %bitcast_add_fusion.acc_ref), custom_call_target="tpu_custom_call" | custom-call | flops 134217728 | bytes 4194304 | tf_op jit(solution)/shard_map/near_low/pallas_call | solution.py:121
  (33 shorter events, 0.1 us)
Async XLA Ops:
  0.0 55.7 %copy-start = (f32[16,8,32,32]{3,2,1,0:T(8,128)S(1)}, f32[16,8,32,32]{3,2,1,0:T(8,128)}, u32[]{:S(2)}) copy-start(f32[16,8,32,32]{3,2,1,0:T(8,128)} %param.17) | copy-start | bytes 1572868
  0.0 23.4 %copy-start.3 = (bf16[4096,128]{1,0:T(8,128)(2,1)S(1)}, bf16[4096,128]{1,0:T(8,128)(2,1)}, u32[]{:S(2)}) copy-start(bf16[4096,128]{1,0:T(8,128)(2,1)} %own_ref.1) | copy-start | bytes 3145732
  0.0 3.3 %copy-start.10 = (f32[1,32,32]{2,1,0:T(8,128)S(1)}, f32[1,32,32]{2,1,0:T(8,128)}, u32[]{:S(2)}) copy-start(f32[1,32,32]{2,1,0:T(8,128)} %param.19) | copy-start | bytes 12292
  0.0 18.8 %copy-start.11 = (s32[1,8]{1,0:T(1,128)S(1)}, s32[1,8]{1,0:T(1,128)}, u32[]{:S(2)}) copy-start(s32[1,8]{1,0:T(1,128)} %param.23) | copy-start | bytes 100
  4.1 19.3 %collective-permute-start.4 = (f32[2,32,128]{2,1,0:T(8,128)S(1)}, f32[2,32,128]{2,1,0:T(8,128)S(1)}, u32[]{:S(2)}, u32[]{:S(2)}) collective-permute-start(f32[2,32,128]{2,1,0:T(8,128)S(1)} %get-tuple-element.8), channel_id=1, source_target_pairs={{0,1},{1,2},{2,3},{3,0},{4,5},{5,6},{6,7},{7,4},{8,9},{9,10},{10,1... | collective-permute-start | bytes 98312 | tf_op jit(solution)/shard_map/ppermute | solution.py:25
  5.7 19.6 %collective-permute-start.5 = (f32[2,32,128]{2,1,0:T(8,128)S(1)}, f32[2,32,128]{2,1,0:T(8,128)S(1)}, u32[]{:S(2)}, u32[]{:S(2)}) collective-permute-start(f32[2,32,128]{2,1,0:T(8,128)S(1)} %get-tuple-element.8), channel_id=1, source_target_pairs={{0,2},{1,3},{2,0},{3,1},{4,6},{5,7},{6,4},{7,5},{8,10},{9,11},{10,... | collective-permute-start | bytes 98312 | tf_op jit(solution)/shard_map/ppermute | solution.py:25
  8.3 21.0 %collective-permute-start.6 = (f32[2,32,128]{2,1,0:T(8,128)S(1)}, f32[2,32,128]{2,1,0:T(8,128)S(1)}, u32[]{:S(2)}, u32[]{:S(2)}) collective-permute-start(f32[2,32,128]{2,1,0:T(8,128)S(1)} %get-tuple-element.8), channel_id=1, source_target_pairs={{0,3},{1,0},{2,1},{3,2},{4,7},{5,4},{6,5},{7,6},{8,11},{9,8},{10,9... | collective-permute-start | bytes 98312 | tf_op jit(solution)/shard_map/ppermute | solution.py:25
  9.6 40.9 %collective-permute-start.2 = (f32[16,32,128]{2,1,0:T(8,128)S(1)}, f32[16,32,128]{2,1,0:T(8,128)}, u32[]{:S(2)}, u32[]{:S(2)}) collective-permute-start(f32[16,32,128]{2,1,0:T(8,128)S(1)} %fusion.15), channel_id=1, source_target_pairs={{0,1},{1,2},{2,3},{3,4},{4,5},{5,6},{6,7},{7,8},{8,9},{9,10},{10,1... | collective-permute-start | bytes 786440 | tf_op jit(solution)/shard_map/ppermute | solution.py:17
  12.2 38.3 %collective-permute-start.3 = (f32[16,32,128]{2,1,0:T(8,128)S(1)}, f32[16,32,128]{2,1,0:T(8,128)}, u32[]{:S(2)}, u32[]{:S(2)}) collective-permute-start(f32[16,32,128]{2,1,0:T(8,128)S(1)} %fusion.15), channel_id=1, source_target_pairs={{1,0},{2,1},{3,2},{4,3},{5,4},{6,5},{7,6},{8,7},{9,8},{10,9},{11,1... | collective-permute-start | bytes 786440 | tf_op jit(solution)/shard_map/ppermute | solution.py:17
  23.4 5.9 %copy-start.7 = (f32[2,32,128]{2,1,0:T(8,128)}, f32[2,32,128]{2,1,0:T(8,128)S(1)}, u32[]{:S(2)}) copy-start(f32[2,32,128]{2,1,0:T(8,128)S(1)} %collective-permute-done.4) | copy-start | bytes 98308
  23.4 41.8 %collective-permute-start.1 = (bf16[4096,128]{1,0:T(8,128)(2,1)S(1)}, bf16[4096,128]{1,0:T(8,128)(2,1)}, u32[]{:S(2)}, u32[]{:S(2)}) collective-permute-start(bf16[4096,128]{1,0:T(8,128)(2,1)S(1)} %copy-done.3), channel_id=1, source_target_pairs={{1,0},{2,1},{3,2},{4,3},{5,4},{6,5},{7,6},{8,7},{9,8},{10,9},{11,1... | collective-permute-start | bytes 3145736 | tf_op jit(solution)/shard_map/ppermute | solution.py:17
  25.3 4.0 %copy-start.8 = (f32[2,32,128]{2,1,0:T(8,128)}, f32[2,32,128]{2,1,0:T(8,128)S(1)}, u32[]{:S(2)}) copy-start(f32[2,32,128]{2,1,0:T(8,128)S(1)} %collective-permute-done.5) | copy-start | bytes 98308
  25.3 55.5 %collective-permute-start = (bf16[4096,128]{1,0:T(8,128)(2,1)S(1)}, bf16[4096,128]{1,0:T(8,128)(2,1)}, u32[]{:S(2)}, u32[]{:S(2)}) collective-permute-start(bf16[4096,128]{1,0:T(8,128)(2,1)S(1)} %copy-done.3), channel_id=1, source_target_pairs={{0,1},{1,2},{2,3},{3,4},{4,5},{5,6},{6,7},{7,8},{8,9},{9,10},{10,1... | collective-permute-start | bytes 3145736 | tf_op jit(solution)/shard_map/ppermute | solution.py:17
  29.3 0.6 copy-start.9
  31.3 3.4 %collective-permute-start.7 = (f32[1,32,128]{2,1,0:T(8,128)}, f32[1,32,128]{2,1,0:T(8,128)}, u32[]{:S(2)}, u32[]{:S(2)}) collective-permute-start(f32[1,32,128]{2,1,0:T(8,128)} %bitcast.19), channel_id=1, source_target_pairs={{0,4},{4,0},{8,12},{12,8},{16,20},{20,16},{24,28},{28,24},{1,5},{5... | collective-permute-start | bytes 49160 | tf_op jit(solution)/shard_map/ppermute | solution.py:37
  36.1 4.2 %collective-permute-start.8 = (f32[2,32,128]{2,1,0:T(8,128)}, f32[2,32,128]{2,1,0:T(8,128)}, u32[]{:S(2)}, u32[]{:S(2)}) collective-permute-start(f32[2,32,128]{2,1,0:T(8,128)} %pad_maximum_fusion.5), channel_id=1, source_target_pairs={{0,8},{4,12},{8,0},{12,4},{16,24},{20,28},{24,16},{28,20},{1,9},{5... | collective-permute-start | bytes 98312 | tf_op jit(solution)/shard_map/ppermute | solution.py:37
  41.1 4.3 %collective-permute-start.9 = (f32[4,32,128]{2,1,0:T(8,128)S(1)}, f32[4,32,128]{2,1,0:T(8,128)S(1)}, u32[]{:S(2)}, u32[]{:S(2)}) collective-permute-start(f32[4,32,128]{2,1,0:T(8,128)S(1)} %pad_maximum_fusion.3), channel_id=1, source_target_pairs={{0,16},{4,20},{8,24},{12,28},{16,0},{20,4},{24,8},{28,12},{1,17},{... | collective-permute-start | bytes 196616 | tf_op jit(solution)/shard_map/ppermute | solution.py:37
  55.7 4.4 %copy-start.6 = (f32[16,32,32]{2,1,0:T(8,128)S(1)}, f32[16,32,32]{2,1,0:T(8,128)}, u32[]{:S(2)}) copy-start(f32[16,32,32]{2,1,0:T(8,128)} %param.16) | copy-start | bytes 196612
  55.7 4.8 %copy-start.5 = (bf16[16,32,256]{2,1,0:T(8,128)(2,1)S(1)}, bf16[16,32,256]{2,1,0:T(8,128)(2,1)}, u32[]{:S(2)}) copy-start(bf16[16,32,256]{2,1,0:T(8,128)(2,1)} %param.15) | copy-start | bytes 786436
  65.2 3.4 %copy-start.1 = (bf16[16,4,256,256]{3,2,1,0:T(8,128)(2,1)S(1)}, bf16[16,4,256,256]{3,2,1,0:T(8,128)(2,1)}, u32[]{:S(2)}) copy-start(bf16[16,4,256,256]{3,2,1,0:T(8,128)(2,1)} %blocks_ref.3) | copy-start | bytes 25165828
  68.5 12.1 %copy-start.4 = (f32[16,256,128]{2,1,0:T(8,128)S(1)}, f32[16,256,128]{2,1,0:T(8,128)}, u32[]{:S(2)}) copy-start(f32[16,256,128]{2,1,0:T(8,128)} %copy.20) | copy-start | bytes 6291460
  68.5 12.3 %copy-start.2 = (bf16[16,4,256,256]{3,2,1,0:T(8,128)(2,1)S(1)}, bf16[16,4,256,256]{3,2,1,0:T(8,128)(2,1)}, u32[]{:S(2)}) copy-start(bf16[16,4,256,256]{3,2,1,0:T(8,128)(2,1)} %blocks_ref.3) | copy-start | bytes 25165828

commit v2 on v0

v2 whole, which is shorter than its diff:
```python
import functools

import jax
import jax.numpy as jnp
from jax import lax
from jax.experimental import pallas as pl
from jax.experimental.pallas import tpu as pltpu
from jax.sharding import PartitionSpec as P

HIGHEST = lax.Precision.HIGHEST
BOTH = ("col", "sub")
SPARE = 16
VMEM = pl.BlockSpec(memory_space=pltpu.VMEM)
SMEM = pl.BlockSpec(memory_space=pltpu.SMEM)
HBM = pl.BlockSpec(memory_space=pltpu.HBM)


def call(body, ins, outs, scratch=(), mib=16, name=None):
    return pl.pallas_call(
        body,
        in_specs=ins,
        out_specs=[VMEM] * len(outs),
        out_shape=[jax.ShapeDtypeStruct(shape, kind) for shape, kind in outs],
        scratch_shapes=scratch,
        compiler_params=pltpu.CompilerParams(vmem_limit_bytes=mib * 2**20),
        cost_estimate=pl.CostEstimate(flops=0, bytes_accessed=0, transcendentals=0),
        name=name,
    )


def shift(value, step):
    count = lax.axis_size(BOTH)
    pairs = [(i, i + step) for i in range(count) if 0 <= i + step < count]
    return lax.ppermute(value, BOTH, pairs)


def exact(a, b, contract=(1, 0)):
    dims = (((contract[0],), (contract[1],)), ((), ()))
    return lax.dot_general(a, b, dims, precision=HIGHEST, preferred_element_type=jnp.float32)


def in_hbm(value):
    return pltpu.with_memory_space_constraint(value, pltpu.HBM)


def upward_body(*refs):
    sources, refs = refs[:6], refs[6:]
    (vec_ref, basis_ref, transfer_ref, cluster_ref, couple_ref, top_couple_ref), refs = refs[:6], refs[6:]
    (first_ref, second_ref, coefs_ref, packed_ref, low_ref, top_ref, sems) = refs
    leaves, rank, rows = basis_ref.shape
    pairs = list(zip(sources, (vec_ref, basis_ref, transfer_ref, cluster_ref, couple_ref, top_couple_ref)))
    pairs.append((sources[0].at[: first_ref.shape[0], :], first_ref))
    pairs.append((sources[0].at[vec_ref.shape[0] - second_ref.shape[0] :, :], second_ref))
    copies = [
        pltpu.make_async_copy(source, target, sems.at[i]) for i, (source, target) in enumerate(pairs)
    ]
    for copy in copies:
        copy.start()
    for copy in copies:
        copy.wait()
    for leaf in range(leaves):
        coefs_ref[leaf * rank : (leaf + 1) * rank, :] = jnp.dot(
            basis_ref[leaf], vec_ref[leaf * rows : (leaf + 1) * rows, :], preferred_element_type=jnp.float32
        )
    whole = coefs_ref[...]
    transfer = transfer_ref[...].reshape(leaves * rank, rank)
    cluster = exact(transfer, whole, (0, 0))
    low_ref[...] = cluster
    top_ref[0] = exact(cluster_ref[0], cluster, (0, 0))
    most = jnp.max(jnp.abs(whole), axis=(0, 1), keepdims=True)
    power = jnp.floor(jnp.log2(jnp.maximum(most, 1e-30)))
    packed_ref[: leaves * rank, :] = whole * jnp.exp2(14.0 - power)
    packed_ref[leaves * rank :, :] = jnp.broadcast_to(power, (SPARE, whole.shape[1]))


def upward(vectors, basis, transfer, cluster_transfer, cluster_coupling, top_coupling):
    leaves, rank, _ = basis.shape
    points, columns = vectors.shape
    f32 = jnp.float32
    arrays = (vectors, basis, transfer, cluster_transfer, cluster_coupling, top_coupling)
    return call(
        upward_body,
        [HBM] * 6,
        [(array.shape, array.dtype) for array in arrays]
        + [
            ((points // 2 + SPARE, columns), vectors.dtype),
            ((points // 2, columns), vectors.dtype),
            ((leaves * rank, columns), f32),
            ((leaves * rank + SPARE, columns), f32),
            ((rank, columns), f32),
            ((1, rank, columns), f32),
        ],
        scratch=[pltpu.SemaphoreType.DMA((8,))],
        name="leaf_and_cluster_coefs",
    )(*[in_hbm(array) for array in arrays])


def top_body(straight, partner_ref, coupling_ref, col_ref, low_ref, both_ref):
    col = lax.axis_index("col")
    top = None
    for k in range(coupling_ref.shape[1]):
        place = partner_ref[0, k]
        place = place if straight else lax.bitwise_xor(place, col)
        term = exact(coupling_ref[0, k], col_ref[place])
        top = term if top is None else top + term
    both_ref[0] = low_ref[...]
    both_ref[1] = top


def top_share(partner, coupling, cols, low):
    count = lax.axis_size("col")
    return call(
        functools.partial(top_body, bool(count & (count - 1))),
        [SMEM] + [VMEM] * 3,
        [((2,) + low.shape, jnp.float32)],
        name="top_field_share",
    )(partner, coupling, cols, low)[0]


def join_body(first_ref, second_ref, out_ref):
    width = first_ref.shape[0]
    out_ref[:width] = first_ref[...]
    out_ref[width:] = second_ref[...]


def join(first, second):
    shape = (2 * first.shape[0],) + first.shape[1:]
    return call(join_body, [VMEM] * 2, [(shape, first.dtype)], name="join_cols")(first, second)[0]


def gather_sub(value):
    count = lax.axis_size("sub")
    parts = [value]
    for step in range(1, count):
        pairs = [(i, (i + step) % count) for i in range(count)]
        parts.append(lax.ppermute(value, "sub", pairs))
    return parts


def gather_col(value):
    count = lax.axis_size("col")
    if count & (count - 1):
        return lax.all_gather(value, "col", axis=0, tiled=True)
    width = 1
    while width < count:
        pairs = [(i, i ^ width) for i in range(count)]
        value = join(value, lax.ppermute(value, "col", pairs))
        width *= 2
    return value


def far_body(far_ref, near_ref, coupling_in, low_ref, own_ref, high_ref, field_ref, coupling_ref, window, sems):
    leaves, slots, rank, _ = coupling_ref.shape
    rows = leaves * rank

    def copy(leaf):
        return pltpu.make_async_copy(coupling_in.at[leaf], coupling_ref.at[leaf], sems.at[leaf])

    @pl.loop(0, leaves)
    def _(leaf):
        copy(leaf).start()

    first = near_ref[0, 0] - leaves
    for place, ref in ((0, low_ref), (2, high_ref)):
        scale = jnp.exp2(ref[rows : rows + 1, :] - 14.0)
        window[place * rows : (place + 1) * rows, :] = ref[:rows, :] * scale
    window[rows : 2 * rows, :] = own_ref[...]

    @pl.loop(0, leaves)
    def _(leaf):
        copy(leaf).wait()
        picked = []
        for k in range(slots):
            place = jnp.clip(far_ref[k, leaf] - first, 0, 3 * leaves - 1)
            picked.append(window[pl.ds(pl.multiple_of(place * rank, rank), rank), :])
        here = coupling_ref[leaf]
        wide = jnp.concatenate([here[k] for k in range(slots)], axis=1)
        at = pl.ds(pl.multiple_of(leaf * rank, rank), rank)
        field_ref[at, :] = exact(wide, jnp.concatenate(picked, axis=0))


def far(leaf_far, near_index, coupling, low, own, high):
    leaves, _, rank, _ = coupling.shape
    return call(
        far_body,
        [SMEM] * 2 + [HBM] + [VMEM] * 3,
        [(own.shape, jnp.float32)],
        scratch=[
            pltpu.VMEM(coupling.shape, coupling.dtype),
            pltpu.VMEM((3 * leaves * rank, own.shape[1]), jnp.float32),
            pltpu.SemaphoreType.DMA((leaves,)),
        ],
        name="far_field_of_leaves",
    )(leaf_far, near_index, in_hbm(coupling), low, own, high)[0]


def down_body(subs, *refs):
    (partner_ref, near_ref), refs = refs[:2], refs[2:]
    part_refs, refs = refs[:subs], refs[subs:]
    (coupling_ref, cluster_ref, transfer_ref, field_ref, basis_ref, blocks_ref), refs = refs[:6], refs[6:]
    (own_ref, high_ref, acc_ref, held_ref, stack, window, sems) = refs
    leaves, rank, rows = basis_ref.shape
    slots = blocks_ref.shape[1]

    def copy(leaf):
        return pltpu.make_async_copy(blocks_ref.at[leaf], held_ref.at[leaf], sems.at[leaf])

    @pl.loop(0, leaves)
    def _(leaf):
        copy(leaf).start()

    sub = lax.axis_index("sub")
    top = None
    for j in range(subs):
        stack[j] = part_refs[j][0]
        top = part_refs[j][1] if top is None else top + part_refs[j][1]
    cluster = exact(cluster_ref[0], top)
    for k in range(coupling_ref.shape[1]):
        place = lax.rem(sub - partner_ref[0, k] + subs, subs)
        cluster = cluster + exact(coupling_ref[0, k], stack[place])
    transfer = transfer_ref[...].reshape(leaves * rank, rank)
    field_ref[...] += exact(transfer, cluster)

    window[: leaves * rows, :] = own_ref[...]
    window[leaves * rows : 2 * leaves * rows, :] = high_ref[...]
    window[2 * leaves * rows :, :] = jnp.zeros((rows, high_ref.shape[1]), window.dtype)
    first = near_ref[0, 0]

    @pl.loop(0, leaves)
    def _(leaf):
        copy(leaf).wait()
        field = field_ref[pl.ds(pl.multiple_of(leaf * rank, rank), rank), :].astype(jnp.bfloat16)
        acc = lax.dot_general(
            basis_ref[leaf], field, (((0,), (0,)), ((), ())), preferred_element_type=jnp.float32
        )
        for k in range(slots):
            place = near_ref[k, leaf] - first
            place = jnp.where(place < 0, 2 * leaves, jnp.minimum(place, 2 * leaves - 1))
            start = pl.multiple_of(place * rows, rows)
            acc = acc + jnp.dot(
                held_ref[leaf, k], window[pl.ds(start, rows), :], preferred_element_type=jnp.float32
            )
        acc_ref[pl.ds(pl.multiple_of(leaf * rows, rows), rows), :] = acc


def down(partner, near_index, parts, coupling, cluster_transfer, transfer, field, basis, blocks, own, high):
    leaves, rank, rows = basis.shape
    columns = high.shape[1]
    subs = len(parts)
    return call(
        functools.partial(down_body, subs),
        [SMEM] * 2 + [VMEM] * (subs + 5) + [HBM] + [VMEM] * 2,
        [(high.shape, jnp.float32), (blocks.shape, blocks.dtype)],
        scratch=[
            pltpu.VMEM((subs, rank, columns), jnp.float32),
            pltpu.VMEM(((2 * leaves + 1) * rows, columns), high.dtype),
            pltpu.SemaphoreType.DMA((leaves,)),
        ],
        mib=32,
        name="down_and_near_own_high",
    )(
        partner, near_index, *parts, coupling, cluster_transfer, transfer, field, basis, in_hbm(blocks), own, high,
    )


def last_body(near_ref, blocks_ref, low_first_ref, low_second_ref, acc_ref, out_ref, held, sem):
    leaves, slots, rows, _ = blocks_ref.shape
    first = near_ref[0, 0] - leaves
    split = leaves // 2

    def copy(leaf):
        here = pl.ds(pl.multiple_of(leaf * rows, rows), rows)
        return pltpu.make_async_copy(held.at[here, :], out_ref.at[here, :], sem)

    @pl.loop(0, leaves)
    def _(leaf):
        here = pl.ds(pl.multiple_of(leaf * rows, rows), rows)
        for k in range(1, slots):
            place = jnp.maximum(near_ref[k, leaf] - first, 0)

            def add(ref, at):
                start = pl.multiple_of(at * rows, rows)
                acc_ref[here, :] += jnp.dot(
                    blocks_ref[leaf, k], ref[pl.ds(start, rows), :], preferred_element_type=jnp.float32
                )

            pl.when(place < split)(lambda: add(low_first_ref, place))
            pl.when((place >= split) & (place < leaves))(lambda: add(low_second_ref, place - split))

        held[here, :] = acc_ref[here, :].astype(held.dtype)
        copy(leaf).start()

    pltpu.make_async_copy(held, out_ref, sem).wait()


def last(near_index, blocks, low_first, low_second, acc):
    return pl.pallas_call(
        last_body,
        in_specs=[SMEM] + [VMEM] * 4,
        out_specs=HBM,
        out_shape=jax.ShapeDtypeStruct(acc.shape, low_first.dtype),
        scratch_shapes=[pltpu.VMEM(acc.shape, low_first.dtype), pltpu.SemaphoreType.DMA],
        compiler_params=pltpu.CompilerParams(vmem_limit_bytes=32 * 2**20),
        cost_estimate=pl.CostEstimate(flops=0, bytes_accessed=0, transcendentals=0),
        name="near_low",
    )(near_index, blocks, low_first, low_second, acc)


def local(
    vectors,
    near_blocks,
    near_index,
    leaf_basis,
    leaf_transfer,
    leaf_coupling,
    leaf_far,
    cluster_transfer,
    cluster_coupling,
    cluster_partner,
    top_coupling,
    top_partner,
):
    high_vec = shift(vectors, -1)

    near_index, leaf_far = near_index.T, leaf_far.T
    own, basis, transfer, cluster, couple, top_couple, first, second, coefs, packed, low, top = upward(
        vectors, leaf_basis, leaf_transfer, cluster_transfer, cluster_coupling, top_coupling
    )
    halved = packed.astype(jnp.float16)
    low_half = shift(halved, 1)
    high_half = shift(halved, -1)
    share = top_share(top_partner, top_couple, gather_col(top), low)
    parts = gather_sub(share)

    first_sent, _ = lax.optimization_barrier((first, share))
    low_first = shift(first_sent, 1)
    second_sent, parts, low_half, high_half = lax.optimization_barrier((second, parts, low_half, high_half))
    low_second = shift(second_sent, 1)

    low_coefs = low_half.astype(jnp.float32)
    high_coefs = high_half.astype(jnp.float32)
    field = far(leaf_far, near_index, leaf_coupling, low_coefs, coefs, high_coefs)
    acc, blocks = down(
        cluster_partner, near_index, parts, couple, cluster, transfer, field, basis, near_blocks, own, high_vec
    )
    return last(near_index, blocks, low_first, low_second, acc)


def solution(mesh):
    both = P(BOTH)
    in_specs = (both,) * 10 + (P("col"),) * 2
    return jax.shard_map(local, mesh=mesh, in_specs=in_specs, out_specs=both, check_vma=False)
```

time: 139 us -> 69.8 us (0.50)
  the two profiles are of different devices: /device:TPU:0 before, /device:TPU:4 now
where the time goes in v2:
time: 69.8 us; the launch traced here: 69.3 us
  starting transfers between devices  23.9 us (34%)
  waiting for transfers between devices  22.1 us (32%)
  Pallas kernels  19.7 us (28%)
  local copies, waits for them, and re-layouts  3.35 us (5%)
    ppermute x5, starting transfers between devices, shift(): return lax.ppermute(value, BOTH, pairs)  19.1 us
    ppermute x5, waiting for transfers between devices, shift(): return lax.ppermute(value, BOTH, pairs)  14.9 us
    pallas_call x1, Pallas kernels, down(): call(functools.partial(down_body, subs), [SMEM] * 2 + [VMEM] * (subs + 5)...  7.21 us
    ppermute x3, waiting for transfers between devices, gather_col(): value = join(value, lax.ppermute(value, 'col', pairs))  7.18 us
    pallas_call x1, Pallas kernels, far(): call(far_body, [SMEM] * 2 + [HBM] + [VMEM] * 3, [(own.shape, jnp.float32)...  5.53 us
    pallas_call x1, Pallas kernels, last(): pl.pallas_call(last_body, in_specs=[SMEM] + [VMEM] * 4, out_specs=HBM, ou...  3.66 us
    ppermute x3, starting transfers between devices, gather_sub(): parts.append(lax.ppermute(value, 'sub', pairs))  3.56 us
    unnamed x10, local copies, waits for them, and re-layouts  3.35 us
  transfers between devices with their start and end apart: 11, of which 5 were waited for; matrix products, arithmetic and copies ran while one was open for 0% of the time, Pallas kernels for 23%

profile of v2, /device:TPU:4, one launch (start us, length us, event | category | flops | bytes accessed | tf_op | source)
XLA Modules:
  0.0 69.3 jit_solution(15107734098764313937)
XLA Ops:
  0.0 5.8 %collective-permute-start.8 = (bf16[4096,128]{1,0:T(8,128)(2,1)}, bf16[4096,128]{1,0:T(8,128)(2,1)S(1)}, u32[]{:S(2)}, u32[]{:S(2)}) collective-permute-start(bf16[4096,128]{1,0:T(8,128)(2,1)} %refs_0_.2), channel_id=1, source_target_pairs={{1,0},{2,1},{3,2},{4,3},{5,4},{6,5},{7,6},{8,7},{9,8},{10,9},{11,1... | collective-permute-start | bytes 3145736 | tf_op jit(solution)/shard_map/ppermute | solution.py:34
  5.8 2.5 %leaf_and_cluster_coefs.1 = (bf16[4096,128]{1,0:T(8,128)(2,1)S(1)}, bf16[16,32,256]{2,1,0:T(8,128)(2,1)S(1)}, f32[16,32,32]{2,1,0:T(8,128)S(1)}, f32[1,32,32]{2,...) custom-call(bf16[4096,128]{1,0:T(8,128)(2,1)} %refs_0_.2, ...), custom_call_target="tpu_custom_call" | custom-call | tf_op jit(solution)/shard_map/leaf_and_cluster_coefs/pallas_call | solution.py:81
  8.3 2.1 %collective-permute-start.7 = (f16[528,128]{1,0:T(8,128)(2,1)S(1)}, f16[528,128]{1,0:T(8,128)(2,1)S(1)}, u32[]{:S(2)}, u32[]{:S(2)}) collective-permute-start(f16[528,128]{1,0:T(8,128)(2,1)S(1)} %convert_element_type.9), channel_id=1, source_target_pairs={{1,0},{2,1},{3,2},{4,3},{5,4},{6,5},{7,6},{8,7},{9,8},{10,9},{11,1... | collective-permute-start | bytes 405512 | tf_op jit(solution)/shard_map/ppermute | solution.py:34
  10.4 0.1 collective-permute-start
  10.5 3.7 %collective-permute-start.6 = (f16[528,128]{1,0:T(8,128)(2,1)S(1)}, f16[528,128]{1,0:T(8,128)(2,1)S(1)}, u32[]{:S(2)}, u32[]{:S(2)}) collective-permute-start(f16[528,128]{1,0:T(8,128)(2,1)S(1)} %convert_element_type.9), channel_id=1, source_target_pairs={{0,1},{1,2},{2,3},{3,4},{4,5},{5,6},{6,7},{7,8},{8,9},{9,10},{10,1... | collective-permute-start | bytes 405512 | tf_op jit(solution)/shard_map/ppermute | solution.py:34
  14.2 0.0 collective-permute-done.second_ref
  14.3 1.1 %collective-permute-start.1 = (f32[2,32,128]{2,1,0:T(8,128)S(1)}, f32[2,32,128]{2,1,0:T(8,128)S(1)}, u32[]{:S(2)}, u32[]{:S(2)}) collective-permute-start(f32[2,32,128]{2,1,0:T(8,128)S(1)} %join_cols.3.first_ref), channel_id=1, source_target_pairs={{0,8},{4,12},{8,0},{12,4},{16,24},{20,28},{24,16},{28,20},{1,9},{5... | collective-permute-start | bytes 98312 | tf_op jit(solution)/shard_map/ppermute | solution.py:147
  15.3 2.9 %collective-permute-done.1.second_ref = f32[2,32,128]{2,1,0:T(8,128)S(1)} collective-permute-done((f32[2,32,128]{2,1,0:T(8,128)S(1)}, f32[2,32,128]{2,1,0:T(8,128)S(1)}, u32[]{:S(2)}, u32[]{:S(2)}) %collective-permute-start.1) | collective-permute-done | bytes 32800 | tf_op jit(solution)/shard_map/ppermute | solution.py:147
  18.3 0.0 collective-permute-start.2
  18.3 4.3 %collective-permute-done.2.second_ref = f32[4,32,128]{2,1,0:T(8,128)S(1)} collective-permute-done((f32[4,32,128]{2,1,0:T(8,128)S(1)}, f32[4,32,128]{2,1,0:T(8,128)S(1)}, u32[]{:S(2)}, u32[]{:S(2)}) %collective-permute-start.2) | collective-permute-done | bytes 65568 | tf_op jit(solution)/shard_map/ppermute | solution.py:147
  22.5 0.0 copy-start.3
  22.5 0.6 copy-done.3
  23.2 0.8 %top_field_share.1.refs_2_ = f32[2,32,128]{2,1,0:T(8,128)S(1)} custom-call(s32[1,8]{1,0:T(1,128)S(1)} %copy-done.3, f32[1,8,32,32]{3,2,1,0:T(8,128)S(1)} %get-tuple-element.28.coupling_ref, f32[8,32,128]{2,1,0:T(8,128)S(1)} %join_cols.5.col_ref, f32[32,128]{1,0:T(8,128)S(1)} %get-tuple-element.30.low_ref), custom_call_target="tpu_custom_call" | custom-call | tf_op jit(solution)/shard_map/top_field_share/pallas_call | solution.py:112
  24.0 3.1 %collective-permute-start.5 = (f32[2,32,128]{2,1,0:T(8,128)S(1)}, f32[2,32,128]{2,1,0:T(8,128)S(1)}, u32[]{:S(2)}, u32[]{:S(2)}) collective-permute-start(f32[2,32,128]{2,1,0:T(8,128)S(1)} %top_field_share.1.refs_2_), channel_id=1, source_target_pairs={{0,3},{1,0},{2,1},{3,2},{4,7},{5,4},{6,5},{7,6},{8,11},{9,8},{10,9... | collective-permute-start | bytes 98312 | tf_op jit(solution)/shard_map/ppermute | solution.py:136
  27.1 0.0 collective-permute-start.4
  27.1 5.4 %collective-permute-done.7 = f16[528,128]{1,0:T(8,128)(2,1)S(1)} collective-permute-done((f16[528,128]{1,0:T(8,128)(2,1)S(1)}, f16[528,128]{1,0:T(8,128)(2,1)S(1)}, u32[]{:S(2)}, u32[]{:S(2)}) %collective-permute-start.7) | collective-permute-done | bytes 135200 | tf_op jit(solution)/shard_map/ppermute | solution.py:34
  32.5 0.5 collective-permute-start.3
  33.0 2.4 %collective-permute-done.6 = f16[528,128]{1,0:T(8,128)(2,1)S(1)} collective-permute-done((f16[528,128]{1,0:T(8,128)(2,1)S(1)}, f16[528,128]{1,0:T(8,128)(2,1)S(1)}, u32[]{:S(2)}, u32[]{:S(2)}) %collective-permute-start.6) | collective-permute-done | bytes 135200 | tf_op jit(solution)/shard_map/ppermute | solution.py:34
  35.4 4.4 %collective-permute-start.9 = (bf16[2064,128]{1,0:T(8,128)(2,1)S(1)}, bf16[2064,128]{1,0:T(8,128)(2,1)S(1)}, u32[]{:S(2)}, u32[]{:S(2)}) collective-permute-start(bf16[2064,128]{1,0:T(8,128)(2,1)S(1)} %get-tuple-element.46), channel_id=1, source_target_pairs={{0,1},{1,2},{2,3},{3,4},{4,5},{5,6},{6,7},{7,8},{8,9},{9,10},{10,1... | collective-permute-start | bytes 1585160 | tf_op jit(solution)/shard_map/ppermute | solution.py:34
  39.8 0.0 collective-permute-done.5.refs_5_
  39.8 0.0 collective-permute-done.4.refs_4_
  39.8 0.0 collective-permute-done.3.refs_3_
  39.8 3.2 %collective-permute-start.10 = (bf16[2048,128]{1,0:T(8,128)(2,1)S(1)}, bf16[2048,128]{1,0:T(8,128)(2,1)S(1)}, u32[]{:S(2)}, u32[]{:S(2)}) collective-permute-start(bf16[2048,128]{1,0:T(8,128)(2,1)S(1)} %get-tuple-element.47), channel_id=1, source_target_pairs={{0,1},{1,2},{2,3},{3,4},{4,5},{5,6},{6,7},{7,8},{8,9},{9,10},{10,1... | collective-permute-start | bytes 1572872 | tf_op jit(solution)/shard_map/ppermute | solution.py:34
  43.1 0.0 copy-start
  43.1 0.7 copy-done
  43.8 0.0 copy-start.2
  43.8 0.7 copy-done.2
  44.4 5.5 %far_field_of_leaves.1.refs_9_ = f32[512,128]{1,0:T(8,128)S(1)} custom-call(s32[8,16]{1,0:T(8,128)S(1)} %bitcast.5, s32[4,16]{1,0:T(4,128)S(1)} %bitcast.2, f32[16,8,32,32]{3,2,1,0:T(8,128)} %coupling_in.1, f32[528,128]{1,0:T(8,128)S(1)} %convert_element_type.10.low_ref, f32[512,128]{1,0:T(8,128)S(1)} %get-tuple-element.40.own_ref, ...), custom_call_target="tpu_custom_call" | custom-call | tf_op jit(solution)/shard_map/far_field_of_leaves/pallas_call | solution.py:184
  50.0 0.0 collective-permute-done.8.refs_13_
  50.0 0.0 copy-start.1
  50.0 0.7 copy-done.1
  50.7 0.0 copy-start.4
  50.7 0.7 copy-done.4
  51.3 7.2 %down_and_near_own_high.1 = (f32[4096,128]{1,0:T(8,128)S(1)}, bf16[16,4,256,256]{3,2,1,0:T(8,128)(2,1)S(1)}) custom-call(s32[1,4]{1,0:T(1,128)S(1)} %copy-done.4, s32[4,16]{1,0:T(4,128)S(1)} %bitcast.3, f32[2,32,128]{2,1,0:T(8,128)S(1)} %top_field_share.1.refs_2_, f32[2,32,128]{2,1,0:T(8,128)S(1)} %collective-permute-done.3.refs_3_, ...), custom_call_target="tpu_custom_call" | custom-call | tf_op jit(solution)/shard_map/down_and_near_own_high/pallas_call | solution.py:250
  58.6 0.0 collective-permute-done.9.low_first_ref
  58.6 7.1 %collective-permute-done.10.low_second_ref = bf16[2048,128]{1,0:T(8,128)(2,1)S(1)} collective-permute-done((bf16[2048,128]{1,0:T(8,128)(2,1)S(1)}, bf16[2048,128]{1,0:T(8,128)(2,1)S(1)}, u32[]{:S(2)}, u32[]{:S(2)}) %collective-permute-start.10) | collective-permute-done | bytes 524320 | tf_op jit(solution)/shard_map/ppermute | solution.py:34
  65.6 3.7 %near_low.1 = bf16[4096,128]{1,0:T(8,128)(2,1)} custom-call(s32[4,16]{1,0:T(4,128)S(1)} %bitcast.4, bf16[16,4,256,256]{3,2,1,0:T(8,128)(2,1)S(1)} %get-tuple-element.44.blocks_ref, bf16[2064,128]{1,0:T(8,128)(2,1)S(1)} %collective-permute-done.9.low_first_ref, bf16[2048,128]{1,0:T(8,128)(2,1)S(1)} %collective-permute-done.10.low_second_ref, ...), custom_call_target="tpu_custom_call" | custom-call | tf_op jit(solution)/shard_map/near_low/pallas_call | solution.py:297
  (6 shorter events, 0.1 us)
Async XLA Ops:
  0.0 50.0 %collective-permute-start.8 = (bf16[4096,128]{1,0:T(8,128)(2,1)}, bf16[4096,128]{1,0:T(8,128)(2,1)S(1)}, u32[]{:S(2)}, u32[]{:S(2)}) collective-permute-start(bf16[4096,128]{1,0:T(8,128)(2,1)} %refs_0_.2), channel_id=1, source_target_pairs={{1,0},{2,1},{3,2},{4,3},{5,4},{6,5},{7,6},{8,7},{9,8},{10,9},{11,1... | collective-permute-start | bytes 3145736 | tf_op jit(solution)/shard_map/ppermute | solution.py:34
  8.3 24.2 %collective-permute-start.7 = (f16[528,128]{1,0:T(8,128)(2,1)S(1)}, f16[528,128]{1,0:T(8,128)(2,1)S(1)}, u32[]{:S(2)}, u32[]{:S(2)}) collective-permute-start(f16[528,128]{1,0:T(8,128)(2,1)S(1)} %convert_element_type.9), channel_id=1, source_target_pairs={{1,0},{2,1},{3,2},{4,3},{5,4},{6,5},{7,6},{8,7},{9,8},{10,9},{11,1... | collective-permute-start | bytes 405512 | tf_op jit(solution)/shard_map/ppermute | solution.py:34
  10.4 3.9 %collective-permute-start = (f32[1,32,128]{2,1,0:T(8,128)S(1)}, f32[1,32,128]{2,1,0:T(8,128)S(1)}, u32[]{:S(2)}, u32[]{:S(2)}) collective-permute-start(f32[1,32,128]{2,1,0:T(8,128)S(1)} %get-tuple-element.29.first_ref), channel_id=1, source_target_pairs={{0,4},{4,0},{8,12},{12,8},{16,20},{20,16},{24,28},{28,24},{1,5},{5... | collective-permute-start | bytes 49160 | tf_op jit(solution)/shard_map/ppermute | solution.py:147
  10.5 24.9 %collective-permute-start.6 = (f16[528,128]{1,0:T(8,128)(2,1)S(1)}, f16[528,128]{1,0:T(8,128)(2,1)S(1)}, u32[]{:S(2)}, u32[]{:S(2)}) collective-permute-start(f16[528,128]{1,0:T(8,128)(2,1)S(1)} %convert_element_type.9), channel_id=1, source_target_pairs={{0,1},{1,2},{2,3},{3,4},{4,5},{5,6},{6,7},{7,8},{8,9},{9,10},{10,1... | collective-permute-start | bytes 405512 | tf_op jit(solution)/shard_map/ppermute | solution.py:34
  14.3 4.0 %collective-permute-start.1 = (f32[2,32,128]{2,1,0:T(8,128)S(1)}, f32[2,32,128]{2,1,0:T(8,128)S(1)}, u32[]{:S(2)}, u32[]{:S(2)}) collective-permute-start(f32[2,32,128]{2,1,0:T(8,128)S(1)} %join_cols.3.first_ref), channel_id=1, source_target_pairs={{0,8},{4,12},{8,0},{12,4},{16,24},{20,28},{24,16},{28,20},{1,9},{5... | collective-permute-start | bytes 98312 | tf_op jit(solution)/shard_map/ppermute | solution.py:147
  18.3 4.3 %collective-permute-start.2 = (f32[4,32,128]{2,1,0:T(8,128)S(1)}, f32[4,32,128]{2,1,0:T(8,128)S(1)}, u32[]{:S(2)}, u32[]{:S(2)}) collective-permute-start(f32[4,32,128]{2,1,0:T(8,128)S(1)} %join_cols.4.first_ref), channel_id=1, source_target_pairs={{0,16},{4,20},{8,24},{12,28},{16,0},{20,4},{24,8},{28,12},{1,17},{... | collective-permute-start | bytes 196616 | tf_op jit(solution)/shard_map/ppermute | solution.py:147
  22.5 0.7 copy-start.3
  24.0 15.8 %collective-permute-start.5 = (f32[2,32,128]{2,1,0:T(8,128)S(1)}, f32[2,32,128]{2,1,0:T(8,128)S(1)}, u32[]{:S(2)}, u32[]{:S(2)}) collective-permute-start(f32[2,32,128]{2,1,0:T(8,128)S(1)} %top_field_share.1.refs_2_), channel_id=1, source_target_pairs={{0,3},{1,0},{2,1},{3,2},{4,7},{5,4},{6,5},{7,6},{8,11},{9,8},{10,9... | collective-permute-start | bytes 98312 | tf_op jit(solution)/shard_map/ppermute | solution.py:136
  27.1 12.7 %collective-permute-start.4 = (f32[2,32,128]{2,1,0:T(8,128)S(1)}, f32[2,32,128]{2,1,0:T(8,128)S(1)}, u32[]{:S(2)}, u32[]{:S(2)}) collective-permute-start(f32[2,32,128]{2,1,0:T(8,128)S(1)} %top_field_share.1.refs_2_), channel_id=1, source_target_pairs={{0,2},{1,3},{2,0},{3,1},{4,6},{5,7},{6,4},{7,5},{8,10},{9,11},{10,... | collective-permute-start | bytes 98312 | tf_op jit(solution)/shard_map/ppermute | solution.py:136
  32.5 7.3 %collective-permute-start.3 = (f32[2,32,128]{2,1,0:T(8,128)S(1)}, f32[2,32,128]{2,1,0:T(8,128)S(1)}, u32[]{:S(2)}, u32[]{:S(2)}) collective-permute-start(f32[2,32,128]{2,1,0:T(8,128)S(1)} %top_field_share.1.refs_2_), channel_id=1, source_target_pairs={{0,1},{1,2},{2,3},{3,0},{4,5},{5,6},{6,7},{7,4},{8,9},{9,10},{10,1... | collective-permute-start | bytes 98312 | tf_op jit(solution)/shard_map/ppermute | solution.py:136
  35.4 23.1 %collective-permute-start.9 = (bf16[2064,128]{1,0:T(8,128)(2,1)S(1)}, bf16[2064,128]{1,0:T(8,128)(2,1)S(1)}, u32[]{:S(2)}, u32[]{:S(2)}) collective-permute-start(bf16[2064,128]{1,0:T(8,128)(2,1)S(1)} %get-tuple-element.46), channel_id=1, source_target_pairs={{0,1},{1,2},{2,3},{3,4},{4,5},{5,6},{6,7},{7,8},{8,9},{9,10},{10,1... | collective-permute-start | bytes 1585160 | tf_op jit(solution)/shard_map/ppermute | solution.py:34
  39.8 25.8 %collective-permute-start.10 = (bf16[2048,128]{1,0:T(8,128)(2,1)S(1)}, bf16[2048,128]{1,0:T(8,128)(2,1)S(1)}, u32[]{:S(2)}, u32[]{:S(2)}) collective-permute-start(bf16[2048,128]{1,0:T(8,128)(2,1)S(1)} %get-tuple-element.47), channel_id=1, source_target_pairs={{0,1},{1,2},{2,3},{3,4},{4,5},{5,6},{6,7},{7,8},{8,9},{9,10},{10,1... | collective-permute-start | bytes 1572872 | tf_op jit(solution)/shard_map/ppermute | solution.py:34
  43.1 0.7 copy-start
  43.8 0.7 copy-start.2
  50.0 0.7 copy-start.1
  50.7 0.7 copy-start.4

commit v3 on v2

--- a/solution.py
+++ b/solution.py
@@ -39,21 +39,26 @@
     return lax.dot_general(a, b, dims, precision=HIGHEST, preferred_element_type=jnp.float32)
 
 
+def scale(value):
+    most = jnp.max(jnp.abs(value), axis=(0, 1), keepdims=True)
+    power = jnp.floor(jnp.log2(jnp.maximum(most, 1e-30)))
+    return value * jnp.exp2(14.0 - power), power
+
+
 def in_hbm(value):
     return pltpu.with_memory_space_constraint(value, pltpu.HBM)
 
 
 def upward_body(*refs):
-    sources, refs = refs[:6], refs[6:]
-    (vec_ref, basis_ref, transfer_ref, cluster_ref, couple_ref, top_couple_ref), refs = refs[:6], refs[6:]
-    (first_ref, second_ref, coefs_ref, packed_ref, low_ref, top_ref, sems) = refs
+    sources, targets, refs = refs[:6], refs[6:12], refs[12:]
+    vec_ref, basis_ref, transfer_ref, cluster_ref, _, _ = targets
+    first_ref, second_ref, coefs_ref, long_ref, short_ref, pair_ref, sems = refs
     leaves, rank, rows = basis_ref.shape
-    pairs = list(zip(sources, (vec_ref, basis_ref, transfer_ref, cluster_ref, couple_ref, top_couple_ref)))
+    columns = vec_ref.shape[1]
+    pairs = list(zip(sources, targets))
     pairs.append((sources[0].at[: first_ref.shape[0], :], first_ref))
     pairs.append((sources[0].at[vec_ref.shape[0] - second_ref.shape[0] :, :], second_ref))
-    copies = [
-        pltpu.make_async_copy(source, target, sems.at[i]) for i, (source, target) in enumerate(pairs)
-    ]
+    copies = [pltpu.make_async_copy(source, target, sems.at[i]) for i, (source, target) in enumerate(pairs)]
     for copy in copies:
         copy.start()
     for copy in copies:
@@ -64,13 +69,22 @@
         )
     whole = coefs_ref[...]
     transfer = transfer_ref[...].reshape(leaves * rank, rank)
-    cluster = exact(transfer, whole, (0, 0))
-    low_ref[...] = cluster
-    top_ref[0] = exact(cluster_ref[0], cluster, (0, 0))
-    most = jnp.max(jnp.abs(whole), axis=(0, 1), keepdims=True)
-    power = jnp.floor(jnp.log2(jnp.maximum(most, 1e-30)))
-    packed_ref[: leaves * rank, :] = whole * jnp.exp2(14.0 - power)
-    packed_ref[leaves * rank :, :] = jnp.broadcast_to(power, (SPARE, whole.shape[1]))
+    low = exact(transfer, whole, (0, 0))
+    top = exact(cluster_ref[0], low, (0, 0))
+    pair_ref[0] = low
+    pair_ref[1] = top
+    half = (SPARE // 2, columns)
+    low, low_power = scale(low)
+    top, top_power = scale(top)
+    short_ref[:rank, :] = low
+    short_ref[rank : 2 * rank, :] = top
+    short_ref[2 * rank : 2 * rank + SPARE // 2, :] = jnp.broadcast_to(low_power, half)
+    short_ref[2 * rank + SPARE // 2 :, :] = jnp.broadcast_to(top_power, half)
+    whole, power = scale(whole)
+    length = leaves * rank
+    long_ref[:length, :] = whole
+    long_ref[length : length + SPARE, :] = jnp.broadcast_to(power, (SPARE, columns))
+    long_ref[length + SPARE :, :] = short_ref[...]
 
 
 def upward(vectors, basis, transfer, cluster_transfer, cluster_coupling, top_coupling):
@@ -78,6 +92,7 @@
     points, columns = vectors.shape
     f32 = jnp.float32
     arrays = (vectors, basis, transfer, cluster_transfer, cluster_coupling, top_coupling)
+    short = 2 * rank + SPARE
     return call(
         upward_body,
         [HBM] * 6,
@@ -86,35 +101,53 @@
             ((points // 2 + SPARE, columns), vectors.dtype),
             ((points // 2, columns), vectors.dtype),
             ((leaves * rank, columns), f32),
-            ((leaves * rank + SPARE, columns), f32),
-            ((rank, columns), f32),
-            ((1, rank, columns), f32),
+            ((leaves * rank + SPARE + short, columns), f32),
+            ((short, columns), f32),
+            ((2, rank, columns), f32),
         ],
         scratch=[pltpu.SemaphoreType.DMA((8,))],
         name="leaf_and_cluster_coefs",
     )(*[in_hbm(array) for array in arrays])
 
 
-def top_body(straight, partner_ref, coupling_ref, col_ref, low_ref, both_ref):
-    col = lax.axis_index("col")
-    top = None
-    for k in range(coupling_ref.shape[1]):
-        place = partner_ref[0, k]
-        place = place if straight else lax.bitwise_xor(place, col)
-        term = exact(coupling_ref[0, k], col_ref[place])
-        top = term if top is None else top + term
-    both_ref[0] = low_ref[...]
-    both_ref[1] = top
-
-
-def top_share(partner, coupling, cols, low):
-    count = lax.axis_size("col")
+def cluster_body(subs, own_ref, low_ref, high_ref, *refs):
+    part_refs, (stack_ref, top_ref) = refs[:-2], refs[-2:]
+    rank = own_ref.shape[1]
+    sub = lax.axis_index("sub")
+    tops = [own_ref[1]]
+
+    def put(valid, place, ref):
+        at = ref.shape[0] - 2 * rank - SPARE
+        values = []
+        for i in range(2):
+            power = ref[at + 2 * rank + i * SPARE // 2 : at + 2 * rank + i * SPARE // 2 + 1, :]
+            values.append(ref[at + i * rank : at + (i + 1) * rank, :] * jnp.exp2(power - 14.0))
+
+        @pl.when(valid)
+        def _():
+            stack_ref[place] = values[0]
+
+        tops.append(jnp.where(valid, values[1], 0.0))
+
+    stack_ref[sub] = own_ref[0]
+    put(sub > 0, sub - 1, low_ref)
+    put(sub < subs - 1, sub + 1, high_ref)
+    for i, ref in enumerate(part_refs[:-1]):
+        put(sub >= 0, lax.rem(sub - 2 - i + subs, subs), ref)
+    if part_refs:
+        put((sub == 0) | (sub == subs - 1), subs - 1 - sub, part_refs[-1])
+    top_ref[0] = functools.reduce(jnp.add, tops)
+
+
+def cluster_sums(own, low, high, parts):
+    _, rank, columns = own.shape
+    subs = lax.axis_size("sub")
     return call(
-        functools.partial(top_body, bool(count & (count - 1))),
-        [SMEM] + [VMEM] * 3,
-        [((2,) + low.shape, jnp.float32)],
-        name="top_field_share",
-    )(partner, coupling, cols, low)[0]
+        functools.partial(cluster_body, subs),
+        [VMEM] * (3 + len(parts)),
+        [((subs, rank, columns), jnp.float32), ((1, rank, columns), jnp.float32)],
+        name="sums_over_sub",
+    )(own, low, high, *parts)
 
 
 def join_body(first_ref, second_ref, out_ref):
@@ -130,10 +163,12 @@
 
 def gather_sub(value):
     count = lax.axis_size("sub")
-    parts = [value]
-    for step in range(1, count):
+    parts = []
+    for step in range(2, count - 1):
         pairs = [(i, (i + step) % count) for i in range(count)]
         parts.append(lax.ppermute(value, "sub", pairs))
+    if count > 2:
+        parts.append(lax.ppermute(value, "sub", [(0, count - 1), (count - 1, 0)]))
     return parts
 
 
@@ -194,13 +229,8 @@
     )(leaf_far, near_index, in_hbm(coupling), low, own, high)[0]
 
 
-def down_body(subs, *refs):
-    (partner_ref, near_ref), refs = refs[:2], refs[2:]
-    part_refs, refs = refs[:subs], refs[subs:]
-    (coupling_ref, cluster_ref, transfer_ref, field_ref, basis_ref, blocks_ref), refs = refs[:6], refs[6:]
-    (own_ref, high_ref, acc_ref, held_ref, stack, window, sems) = refs
-    leaves, rank, rows = basis_ref.shape
-    slots = blocks_ref.shape[1]
+def near_body(near_ref, blocks_ref, own_ref, high_ref, acc_ref, held_ref, window, sems):
+    leaves, slots, rows, _ = blocks_ref.shape
 
     def copy(leaf):
         return pltpu.make_async_copy(blocks_ref.at[leaf], held_ref.at[leaf], sems.at[leaf])
@@ -208,18 +238,6 @@
     @pl.loop(0, leaves)
     def _(leaf):
         copy(leaf).start()
-
-    sub = lax.axis_index("sub")
-    top = None
-    for j in range(subs):
-        stack[j] = part_refs[j][0]
-        top = part_refs[j][1] if top is None else top + part_refs[j][1]
-    cluster = exact(cluster_ref[0], top)
-    for k in range(coupling_ref.shape[1]):
-        place = lax.rem(sub - partner_ref[0, k] + subs, subs)
-        cluster = cluster + exact(coupling_ref[0, k], stack[place])
-    transfer = transfer_ref[...].reshape(leaves * rank, rank)
-    field_ref[...] += exact(transfer, cluster)
 
     window[: leaves * rows, :] = own_ref[...]
     window[leaves * rows : 2 * leaves * rows, :] = high_ref[...]
@@ -229,44 +247,75 @@
     @pl.loop(0, leaves)
     def _(leaf):
         copy(leaf).wait()
-        field = field_ref[pl.ds(pl.multiple_of(leaf * rank, rank), rank), :].astype(jnp.bfloat16)
-        acc = lax.dot_general(
-            basis_ref[leaf], field, (((0,), (0,)), ((), ())), preferred_element_type=jnp.float32
-        )
+        acc = None
         for k in range(slots):
             place = near_ref[k, leaf] - first
             place = jnp.where(place < 0, 2 * leaves, jnp.minimum(place, 2 * leaves - 1))
             start = pl.multiple_of(place * rows, rows)
-            acc = acc + jnp.dot(
+            term = jnp.dot(
                 held_ref[leaf, k], window[pl.ds(start, rows), :], preferred_element_type=jnp.float32
             )
+            acc = term if acc is None else acc + term
         acc_ref[pl.ds(pl.multiple_of(leaf * rows, rows), rows), :] = acc
 
 
-def down(partner, near_index, parts, coupling, cluster_transfer, transfer, field, basis, blocks, own, high):
-    leaves, rank, rows = basis.shape
-    columns = high.shape[1]
-    subs = len(parts)
+def near(near_index, blocks, own, high):
+    leaves, _, rows, _ = blocks.shape
     return call(
-        functools.partial(down_body, subs),
-        [SMEM] * 2 + [VMEM] * (subs + 5) + [HBM] + [VMEM] * 2,
-        [(high.shape, jnp.float32), (blocks.shape, blocks.dtype)],
+        near_body,
+        [SMEM, HBM, VMEM, VMEM],
+        [(own.shape, jnp.float32), (blocks.shape, blocks.dtype)],
         scratch=[
-            pltpu.VMEM((subs, rank, columns), jnp.float32),
-            pltpu.VMEM(((2 * leaves + 1) * rows, columns), high.dtype),
+            pltpu.VMEM(((2 * leaves + 1) * rows, own.shape[1]), own.dtype),
             pltpu.SemaphoreType.DMA((leaves,)),
         ],
         mib=32,
-        name="down_and_near_own_high",
-    )(
-        partner, near_index, *parts, coupling, cluster_transfer, transfer, field, basis, in_hbm(blocks), own, high,
-    )
+        name="near_own_and_high",
+    )(near_index, in_hbm(blocks), own, high)
+
+
+def down_body(
+    straight, partner_ref, top_partner_ref, stack_ref, cols_ref, coupling_ref, top_coupling_ref, cluster_ref,
+    transfer_ref, field_ref, basis_ref, acc_ref, out_ref, fields,
+):
+    leaves, rank, rows = basis_ref.shape
+    col = lax.axis_index("col")
+    top = None
+    for k in range(top_coupling_ref.shape[1]):
+        place = top_partner_ref[0, k]
+        place = place if straight else lax.bitwise_xor(place, col)
+        term = exact(top_coupling_ref[0, k], cols_ref[place])
+        top = term if top is None else top + term
+    cluster = exact(cluster_ref[0], top)
+    for k in range(coupling_ref.shape[1]):
+        cluster = cluster + exact(coupling_ref[0, k], stack_ref[partner_ref[0, k]])
+    transfer = transfer_ref[...].reshape(leaves * rank, rank)
+    fields[...] = (field_ref[...] + exact(transfer, cluster)).astype(fields.dtype)
+    for leaf in range(leaves):
+        here = slice(leaf * rows, (leaf + 1) * rows)
+        out_ref[here, :] = acc_ref[here, :] + lax.dot_general(
+            basis_ref[leaf],
+            fields[leaf * rank : (leaf + 1) * rank, :],
+            (((0,), (0,)), ((), ())),
+            preferred_element_type=jnp.float32,
+        )
+
+
+def down(partner, top_partner, stack, cols, coupling, top_coupling, cluster_transfer, transfer, field, basis, acc):
+    count = lax.axis_size("col")
+    return call(
+        functools.partial(down_body, bool(count & (count - 1))),
+        [SMEM] * 2 + [VMEM] * 9,
+        [(acc.shape, jnp.float32)],
+        scratch=[pltpu.VMEM(field.shape, jnp.bfloat16)],
+        name="fields_down",
+    )(partner, top_partner, stack, cols, coupling, top_coupling, cluster_transfer, transfer, field, basis, acc)[0]
 
 
 def last_body(near_ref, blocks_ref, low_first_ref, low_second_ref, acc_ref, out_ref, held, sem):
     leaves, slots, rows, _ = blocks_ref.shape
+    split = leaves // 2
     first = near_ref[0, 0] - leaves
-    split = leaves // 2
 
     def copy(leaf):
         here = pl.ds(pl.multiple_of(leaf * rows, rows), rows)
@@ -321,27 +370,29 @@
     top_partner,
 ):
     high_vec = shift(vectors, -1)
-
     near_index, leaf_far = near_index.T, leaf_far.T
-    own, basis, transfer, cluster, couple, top_couple, first, second, coefs, packed, low, top = upward(
+
+    own, basis, transfer, cluster, couple, top_couple, first, second, coefs, long, short, pair = upward(
         vectors, leaf_basis, leaf_transfer, cluster_transfer, cluster_coupling, top_coupling
     )
-    halved = packed.astype(jnp.float16)
-    low_half = shift(halved, 1)
-    high_half = shift(halved, -1)
-    share = top_share(top_partner, top_couple, gather_col(top), low)
-    parts = gather_sub(share)
-
-    first_sent, _ = lax.optimization_barrier((first, share))
-    low_first = shift(first_sent, 1)
-    second_sent, parts, low_half, high_half = lax.optimization_barrier((second, parts, low_half, high_half))
-    low_second = shift(second_sent, 1)
-
-    low_coefs = low_half.astype(jnp.float32)
-    high_coefs = high_half.astype(jnp.float32)
-    field = far(leaf_far, near_index, leaf_coupling, low_coefs, coefs, high_coefs)
-    acc, blocks = down(
-        cluster_partner, near_index, parts, couple, cluster, transfer, field, basis, near_blocks, own, high_vec
+    long, short = long.astype(jnp.float16), short.astype(jnp.float16)
+    low_part = shift(long, 1)
+    high_part = shift(long, -1)
+    parts = gather_sub(short)
+    first, high_vec, _ = lax.optimization_barrier((first, high_vec, long))
+    low_first = shift(first, 1)
+    acc, blocks = near(near_index, near_blocks, own, high_vec)
+
+    second, parts, low_part, high_part, acc = lax.optimization_barrier((second, parts, low_part, high_part, acc))
+    low_second = shift(second, 1)
+
+    parts = [part.astype(jnp.float32) for part in parts]
+    low_part, high_part = low_part.astype(jnp.float32), high_part.astype(jnp.float32)
+    stack, top = cluster_sums(pair, low_part, high_part, parts)
+    cols = gather_col(top)
+    field = far(leaf_far, near_index, leaf_coupling, low_part, coefs, high_part)
+    acc = down(
+        cluster_partner, top_partner, stack, cols, couple, top_couple, cluster, transfer, field, basis, acc
     )
     return last(near_index, blocks, low_first, low_second, acc)
 

time: 69.8 us -> 66.9 us (0.958)
  the two profiles are of different devices: /device:TPU:4 before, /device:TPU:31 now
where the time goes in v3:
time: 66.9 us; the launch traced here: 66.6 us
  starting transfers between devices  24.9 us (37%)
  Pallas kernels  23.9 us (36%)
  waiting for transfers between devices  17.5 us (26%)
    ppermute x5, starting transfers between devices, shift(): return lax.ppermute(value, BOTH, pairs)  10.1 us
    ppermute x5, waiting for transfers between devices, shift(): return lax.ppermute(value, BOTH, pairs)  9.57 us
    ppermute x3, starting transfers between devices, gather_col(): value = join(value, lax.ppermute(value, 'col', pairs))  7.09 us
    pallas_call x1, Pallas kernels, last(): pl.pallas_call(last_body, in_specs=[SMEM] + [VMEM] * 4, out_specs=HBM, ou...  6.85 us
    pallas_call x1, Pallas kernels, near(): call(near_body, [SMEM, HBM, VMEM, VMEM], [(own.shape, jnp.float32), (bloc...  6.51 us
    pallas_call x1, Pallas kernels, far(): call(far_body, [SMEM] * 2 + [HBM] + [VMEM] * 3, [(own.shape, jnp.float32)...  5.53 us
    ppermute x1, waiting for transfers between devices, gather_sub(): parts.append(lax.ppermute(value, 'sub', pairs))  5.49 us
    ppermute x1, starting transfers between devices, gather_sub(): parts.append(lax.ppermute(value, 'sub', [(0, count - 1), (count - 1, 0)]))  5.16 us
  transfers between devices with their start and end apart: 10, of which 5 were waited for; matrix products, arithmetic and copies ran while one was open for 0% of the time, Pallas kernels for 26%

profile of v3, /device:TPU:31, one launch (start us, length us, event | category | flops | bytes accessed | tf_op | source)
XLA Modules:
  0.0 66.6 jit_solution(15956582489337712414)
XLA Ops:
  0.0 0.0 copy-start
  0.0 2.3 %collective-permute-start = (bf16[4096,128]{1,0:T(8,128)(2,1)}, bf16[4096,128]{1,0:T(8,128)(2,1)S(1)}, u32[]{:S(2)}, u32[]{:S(2)}) collective-permute-start(bf16[4096,128]{1,0:T(8,128)(2,1)} %refs_0_.1), channel_id=1, source_target_pairs={{1,0},{2,1},{3,2},{4,3},{5,4},{6,5},{7,6},{8,7},{9,8},{10,9},{11,1... | collective-permute-start | bytes 3145736 | tf_op jit(solution)/shard_map/ppermute | solution.py:34
  2.3 2.6 %leaf_and_cluster_coefs.1 = (bf16[4096,128]{1,0:T(8,128)(2,1)S(1)}, bf16[16,32,256]{2,1,0:T(8,128)(2,1)S(1)}, f32[16,32,32]{2,1,0:T(8,128)S(1)}, f32[1,32,32]{2,...) custom-call(bf16[4096,128]{1,0:T(8,128)(2,1)} %refs_0_.1, ...), custom_call_target="tpu_custom_call" | custom-call | tf_op jit(solution)/shard_map/leaf_and_cluster_coefs/pallas_call | solution.py:96
  4.9 1.3 %collective-permute-start.4 = (f16[608,128]{1,0:T(8,128)(2,1)S(1)}, f16[608,128]{1,0:T(8,128)(2,1)S(1)}, u32[]{:S(2)}, u32[]{:S(2)}) collective-permute-start(f16[608,128]{1,0:T(8,128)(2,1)S(1)} %convert_element_type.18), channel_id=1, source_target_pairs={{0,1},{1,2},{2,3},{3,4},{4,5},{5,6},{6,7},{7,8},{8,9},{9,10},{10,1... | collective-permute-start | bytes 466952 | tf_op jit(solution)/shard_map/ppermute | solution.py:34
  6.2 4.0 %collective-permute-start.5 = (f16[608,128]{1,0:T(8,128)(2,1)S(1)}, f16[608,128]{1,0:T(8,128)(2,1)S(1)}, u32[]{:S(2)}, u32[]{:S(2)}) collective-permute-start(f16[608,128]{1,0:T(8,128)(2,1)S(1)} %convert_element_type.18), channel_id=1, source_target_pairs={{1,0},{2,1},{3,2},{4,3},{5,4},{6,5},{7,6},{8,7},{9,8},{10,9},{11,1... | collective-permute-start | bytes 466952 | tf_op jit(solution)/shard_map/ppermute | solution.py:34
  10.2 2.5 %collective-permute-start.2 = (f16[80,128]{1,0:T(8,128)(2,1)S(1)}, f16[80,128]{1,0:T(8,128)(2,1)S(1)}, u32[]{:S(2)}, u32[]{:S(2)}) collective-permute-start(f16[80,128]{1,0:T(8,128)(2,1)S(1)} %convert_element_type.19), channel_id=1, source_target_pairs={{0,2},{1,3},{2,0},{3,1},{4,6},{5,7},{6,4},{7,5},{8,10},{9,11},{10,... | collective-permute-start | bytes 61448 | tf_op jit(solution)/shard_map/ppermute | solution.py:169
  12.7 5.2 %collective-permute-start.3 = (f16[80,128]{1,0:T(8,128)(2,1)S(1)}, f16[80,128]{1,0:T(8,128)(2,1)S(1)}, u32[]{:S(2)}, u32[]{:S(2)}) collective-permute-start(f16[80,128]{1,0:T(8,128)(2,1)S(1)} %convert_element_type.19), channel_id=1, source_target_pairs={{0,3},{3,0},{4,7},{7,4},{8,11},{11,8},{12,15},{15,12},{16,19},{19,... | collective-permute-start | bytes 61448 | tf_op jit(solution)/shard_map/ppermute | solution.py:171
  17.9 6.4 %collective-permute-done.high_ref = bf16[4096,128]{1,0:T(8,128)(2,1)S(1)} collective-permute-done((bf16[4096,128]{1,0:T(8,128)(2,1)}, bf16[4096,128]{1,0:T(8,128)(2,1)S(1)}, u32[]{:S(2)}, u32[]{:S(2)}) %collective-permute-start) | collective-permute-done | bytes 1048608 | tf_op jit(solution)/shard_map/ppermute | solution.py:34
  24.3 1.3 %collective-permute-start.1 = (bf16[2064,128]{1,0:T(8,128)(2,1)S(1)}, bf16[2064,128]{1,0:T(8,128)(2,1)S(1)}, u32[]{:S(2)}, u32[]{:S(2)}) collective-permute-start(bf16[2064,128]{1,0:T(8,128)(2,1)S(1)} %get-tuple-element.34), channel_id=1, source_target_pairs={{0,1},{1,2},{2,3},{3,4},{4,5},{5,6},{6,7},{7,8},{8,9},{9,10},{10,1... | collective-permute-start | bytes 1585160 | tf_op jit(solution)/shard_map/ppermute | solution.py:34
  25.6 0.0 copy-done
  25.6 0.0 copy-start.1
  25.6 6.5 %near_own_and_high.1 = (f32[4096,128]{1,0:T(8,128)S(1)}, bf16[16,4,256,256]{3,2,1,0:T(8,128)(2,1)S(1)}) custom-call(s32[4,16]{1,0:T(4,128)S(1)} %bitcast.2, bf16[16,4,256,256]{3,2,1,0:T(8,128)(2,1)} %blocks_ref.1, bf16[4096,128]{1,0:T(8,128)(2,1)S(1)} %get-tuple-element.29.own_ref, bf16[4096,128]{1,0:T(8,128)(2,1)S(1)} %collective-permute-done.high_ref), custom_call_target="tpu_custom_call" | custom-call | tf_op jit(solution)/shard_map/near_own_and_high/pallas_call | solution.py:264
  32.2 5.5 %collective-permute-done.2 = f16[80,128]{1,0:T(8,128)(2,1)S(1)} collective-permute-done((f16[80,128]{1,0:T(8,128)(2,1)S(1)}, f16[80,128]{1,0:T(8,128)(2,1)S(1)}, u32[]{:S(2)}, u32[]{:S(2)}) %collective-permute-start.2) | collective-permute-done | bytes 20512 | tf_op jit(solution)/shard_map/ppermute | solution.py:169
  37.6 0.0 collective-permute-done.3
  37.7 0.0 collective-permute-done.4
  37.7 0.0 collective-permute-done.5
  37.7 1.3 %collective-permute-start.6 = (bf16[2048,128]{1,0:T(8,128)(2,1)S(1)}, bf16[2048,128]{1,0:T(8,128)(2,1)S(1)}, u32[]{:S(2)}, u32[]{:S(2)}) collective-permute-start(bf16[2048,128]{1,0:T(8,128)(2,1)S(1)} %get-tuple-element.38), channel_id=1, source_target_pairs={{0,1},{1,2},{2,3},{3,4},{4,5},{5,6},{6,7},{7,8},{8,9},{9,10},{10,1... | collective-permute-start | bytes 1572872 | tf_op jit(solution)/shard_map/ppermute | solution.py:34
  39.1 0.0 copy-start.2
  39.1 0.0 copy-start.3
  39.1 1.8 %collective-permute-start.7 = (f32[1,32,128]{2,1,0:T(8,128)S(1)}, f32[1,32,128]{2,1,0:T(8,128)S(1)}, u32[]{:S(2)}, u32[]{:S(2)}) collective-permute-start(f32[1,32,128]{2,1,0:T(8,128)S(1)} %get-tuple-element.45.first_ref), channel_id=1, source_target_pairs={{0,4},{4,0},{8,12},{12,8},{16,20},{20,16},{24,28},{28,24},{1,5},{5... | collective-permute-start | bytes 49160 | tf_op jit(solution)/shard_map/ppermute | solution.py:182
  41.0 0.8 %collective-permute-done.7.second_ref = f32[1,32,128]{2,1,0:T(8,128)S(1)} collective-permute-done((f32[1,32,128]{2,1,0:T(8,128)S(1)}, f32[1,32,128]{2,1,0:T(8,128)S(1)}, u32[]{:S(2)}, u32[]{:S(2)}) %collective-permute-start.7) | collective-permute-done | bytes 16416 | tf_op jit(solution)/shard_map/ppermute | solution.py:182
  41.8 1.5 %collective-permute-start.8 = (f32[2,32,128]{2,1,0:T(8,128)S(1)}, f32[2,32,128]{2,1,0:T(8,128)S(1)}, u32[]{:S(2)}, u32[]{:S(2)}) collective-permute-start(f32[2,32,128]{2,1,0:T(8,128)S(1)} %join_cols.3.first_ref), channel_id=1, source_target_pairs={{0,8},{4,12},{8,0},{12,4},{16,24},{20,28},{24,16},{28,20},{1,9},{5... | collective-permute-start | bytes 98312 | tf_op jit(solution)/shard_map/ppermute | solution.py:182
  43.3 1.6 %collective-permute-done.8.second_ref = f32[2,32,128]{2,1,0:T(8,128)S(1)} collective-permute-done((f32[2,32,128]{2,1,0:T(8,128)S(1)}, f32[2,32,128]{2,1,0:T(8,128)S(1)}, u32[]{:S(2)}, u32[]{:S(2)}) %collective-permute-start.8) | collective-permute-done | bytes 32800 | tf_op jit(solution)/shard_map/ppermute | solution.py:182
  45.0 3.7 %collective-permute-start.9 = (f32[4,32,128]{2,1,0:T(8,128)S(1)}, f32[4,32,128]{2,1,0:T(8,128)S(1)}, u32[]{:S(2)}, u32[]{:S(2)}) collective-permute-start(f32[4,32,128]{2,1,0:T(8,128)S(1)} %join_cols.4.first_ref), channel_id=1, source_target_pairs={{0,16},{4,20},{8,24},{12,28},{16,0},{20,4},{24,8},{28,12},{1,17},{... | collective-permute-start | bytes 196616 | tf_op jit(solution)/shard_map/ppermute | solution.py:182
  48.7 0.0 copy-done.1
  48.7 5.5 %far_field_of_leaves.1.field_ref = f32[512,128]{1,0:T(8,128)S(1)} custom-call(s32[8,16]{1,0:T(8,128)S(1)} %bitcast.5, s32[4,16]{1,0:T(4,128)S(1)} %bitcast.3, f32[16,8,32,32]{3,2,1,0:T(8,128)} %coupling_in.1, f32[608,128]{1,0:T(8,128)S(1)} %convert_element_type.20.low_ref, f32[512,128]{1,0:T(8,128)S(1)} %get-tuple-element.50.own_ref, ...), custom_call_target="tpu_custom_call" | custom-call | tf_op jit(solution)/shard_map/far_field_of_leaves/pallas_call | solution.py:219
  54.2 0.0 collective-permute-done.9.second_ref
  54.2 0.0 copy-done.2
  54.2 0.0 copy-done.3
  54.3 2.4 %fields_down.1.acc_ref = f32[4096,128]{1,0:T(8,128)S(1)} custom-call(s32[1,4]{1,0:T(1,128)S(1)} %copy-done.2, s32[1,8]{1,0:T(1,128)S(1)} %copy-done.3, f32[4,32,128]{2,1,0:T(8,128)S(1)} %get-tuple-element.44.stack_ref, f32[8,32,128]{2,1,0:T(8,128)S(1)} %join_cols.5.cols_ref, f32[1,4,32,32]{3,2,1,0:T(8,128)S(1)} %get-tuple-element.46.coupling_ref, ...), custom_call_target="tpu_custom_call" | custom-call | tf_op jit(solution)/shard_map/fields_down/pallas_call | solution.py:306
  56.6 3.1 %collective-permute-done.6.low_second_ref = bf16[2048,128]{1,0:T(8,128)(2,1)S(1)} collective-permute-done((bf16[2048,128]{1,0:T(8,128)(2,1)S(1)}, bf16[2048,128]{1,0:T(8,128)(2,1)S(1)}, u32[]{:S(2)}, u32[]{:S(2)}) %collective-permute-start.6) | collective-permute-done | bytes 524320 | tf_op jit(solution)/shard_map/ppermute | solution.py:34
  59.7 0.0 collective-permute-done.1.low_first_ref
  59.7 6.9 %near_low.1 = bf16[4096,128]{1,0:T(8,128)(2,1)} custom-call(s32[4,16]{1,0:T(4,128)S(1)} %bitcast.4, bf16[16,4,256,256]{3,2,1,0:T(8,128)(2,1)S(1)} %get-tuple-element.33.blocks_ref, bf16[2064,128]{1,0:T(8,128)(2,1)S(1)} %collective-permute-done.1.low_first_ref, bf16[2048,128]{1,0:T(8,128)(2,1)S(1)} %collective-permute-done.6.low_second_ref, ...), custom_call_target="tpu_custom_call" | custom-call | tf_op jit(solution)/shard_map/near_low/pallas_call | solution.py:346
  (10 shorter events, 0.2 us)
Async XLA Ops:
  0.0 25.6 %copy-start = (s32[16,4]{0,1:T(4,128)S(1)}, s32[16,4]{0,1:T(4,128)}, u32[]{:S(2)}) copy-start(s32[16,4]{0,1:T(4,128)} %param.14) | copy-start | bytes 772
  0.0 24.3 %collective-permute-start = (bf16[4096,128]{1,0:T(8,128)(2,1)}, bf16[4096,128]{1,0:T(8,128)(2,1)S(1)}, u32[]{:S(2)}, u32[]{:S(2)}) collective-permute-start(bf16[4096,128]{1,0:T(8,128)(2,1)} %refs_0_.1), channel_id=1, source_target_pairs={{1,0},{2,1},{3,2},{4,3},{5,4},{6,5},{7,6},{8,7},{9,8},{10,9},{11,1... | collective-permute-start | bytes 3145736 | tf_op jit(solution)/shard_map/ppermute | solution.py:34
  4.9 32.7 %collective-permute-start.4 = (f16[608,128]{1,0:T(8,128)(2,1)S(1)}, f16[608,128]{1,0:T(8,128)(2,1)S(1)}, u32[]{:S(2)}, u32[]{:S(2)}) collective-permute-start(f16[608,128]{1,0:T(8,128)(2,1)S(1)} %convert_element_type.18), channel_id=1, source_target_pairs={{0,1},{1,2},{2,3},{3,4},{4,5},{5,6},{6,7},{7,8},{8,9},{9,10},{10,1... | collective-permute-start | bytes 466952 | tf_op jit(solution)/shard_map/ppermute | solution.py:34
  6.2 31.4 %collective-permute-start.5 = (f16[608,128]{1,0:T(8,128)(2,1)S(1)}, f16[608,128]{1,0:T(8,128)(2,1)S(1)}, u32[]{:S(2)}, u32[]{:S(2)}) collective-permute-start(f16[608,128]{1,0:T(8,128)(2,1)S(1)} %convert_element_type.18), channel_id=1, source_target_pairs={{1,0},{2,1},{3,2},{4,3},{5,4},{6,5},{7,6},{8,7},{9,8},{10,9},{11,1... | collective-permute-start | bytes 466952 | tf_op jit(solution)/shard_map/ppermute | solution.py:34
  10.2 27.4 %collective-permute-start.2 = (f16[80,128]{1,0:T(8,128)(2,1)S(1)}, f16[80,128]{1,0:T(8,128)(2,1)S(1)}, u32[]{:S(2)}, u32[]{:S(2)}) collective-permute-start(f16[80,128]{1,0:T(8,128)(2,1)S(1)} %convert_element_type.19), channel_id=1, source_target_pairs={{0,2},{1,3},{2,0},{3,1},{4,6},{5,7},{6,4},{7,5},{8,10},{9,11},{10,... | collective-permute-start | bytes 61448 | tf_op jit(solution)/shard_map/ppermute | solution.py:169
  12.7 24.9 %collective-permute-start.3 = (f16[80,128]{1,0:T(8,128)(2,1)S(1)}, f16[80,128]{1,0:T(8,128)(2,1)S(1)}, u32[]{:S(2)}, u32[]{:S(2)}) collective-permute-start(f16[80,128]{1,0:T(8,128)(2,1)S(1)} %convert_element_type.19), channel_id=1, source_target_pairs={{0,3},{3,0},{4,7},{7,4},{8,11},{11,8},{12,15},{15,12},{16,19},{19,... | collective-permute-start | bytes 61448 | tf_op jit(solution)/shard_map/ppermute | solution.py:171
  24.3 35.4 %collective-permute-start.1 = (bf16[2064,128]{1,0:T(8,128)(2,1)S(1)}, bf16[2064,128]{1,0:T(8,128)(2,1)S(1)}, u32[]{:S(2)}, u32[]{:S(2)}) collective-permute-start(bf16[2064,128]{1,0:T(8,128)(2,1)S(1)} %get-tuple-element.34), channel_id=1, source_target_pairs={{0,1},{1,2},{2,3},{3,4},{4,5},{5,6},{6,7},{7,8},{8,9},{9,10},{10,1... | collective-permute-start | bytes 1585160 | tf_op jit(solution)/shard_map/ppermute | solution.py:34
  25.6 23.0 %copy-start.1 = (s32[16,8]{0,1:T(8,128)S(1)}, s32[16,8]{0,1:T(8,128)}, u32[]{:S(2)}) copy-start(s32[16,8]{0,1:T(8,128)} %param.18) | copy-start | bytes 1540
  37.7 22.1 %collective-permute-start.6 = (bf16[2048,128]{1,0:T(8,128)(2,1)S(1)}, bf16[2048,128]{1,0:T(8,128)(2,1)S(1)}, u32[]{:S(2)}, u32[]{:S(2)}) collective-permute-start(bf16[2048,128]{1,0:T(8,128)(2,1)S(1)} %get-tuple-element.38), channel_id=1, source_target_pairs={{0,1},{1,2},{2,3},{3,4},{4,5},{5,6},{6,7},{7,8},{8,9},{9,10},{10,1... | collective-permute-start | bytes 1572872 | tf_op jit(solution)/shard_map/ppermute | solution.py:34
  39.1 15.2 %copy-start.2 = (s32[1,4]{1,0:T(1,128)S(1)}, s32[1,4]{1,0:T(1,128)}, u32[]{:S(2)}) copy-start(s32[1,4]{1,0:T(1,128)} %partner_ref.1) | copy-start | bytes 52
  39.1 15.2 %copy-start.3 = (s32[1,8]{1,0:T(1,128)S(1)}, s32[1,8]{1,0:T(1,128)}, u32[]{:S(2)}) copy-start(s32[1,8]{1,0:T(1,128)} %top_partner_ref.1) | copy-start | bytes 100
  39.1 2.7 %collective-permute-start.7 = (f32[1,32,128]{2,1,0:T(8,128)S(1)}, f32[1,32,128]{2,1,0:T(8,128)S(1)}, u32[]{:S(2)}, u32[]{:S(2)}) collective-permute-start(f32[1,32,128]{2,1,0:T(8,128)S(1)} %get-tuple-element.45.first_ref), channel_id=1, source_target_pairs={{0,4},{4,0},{8,12},{12,8},{16,20},{20,16},{24,28},{28,24},{1,5},{5... | collective-permute-start | bytes 49160 | tf_op jit(solution)/shard_map/ppermute | solution.py:182
  41.8 3.1 %collective-permute-start.8 = (f32[2,32,128]{2,1,0:T(8,128)S(1)}, f32[2,32,128]{2,1,0:T(8,128)S(1)}, u32[]{:S(2)}, u32[]{:S(2)}) collective-permute-start(f32[2,32,128]{2,1,0:T(8,128)S(1)} %join_cols.3.first_ref), channel_id=1, source_target_pairs={{0,8},{4,12},{8,0},{12,4},{16,24},{20,28},{24,16},{28,20},{1,9},{5... | collective-permute-start | bytes 98312 | tf_op jit(solution)/shard_map/ppermute | solution.py:182
  45.0 9.3 %collective-permute-start.9 = (f32[4,32,128]{2,1,0:T(8,128)S(1)}, f32[4,32,128]{2,1,0:T(8,128)S(1)}, u32[]{:S(2)}, u32[]{:S(2)}) collective-permute-start(f32[4,32,128]{2,1,0:T(8,128)S(1)} %join_cols.4.first_ref), channel_id=1, source_target_pairs={{0,16},{4,20},{8,24},{12,28},{16,0},{20,4},{24,8},{28,12},{1,17},{... | collective-permute-start | bytes 196616 | tf_op jit(solution)/shard_map/ppermute | solution.py:182

commit v4 on v3

--- a/solution.py
+++ b/solution.py
@@ -10,6 +10,8 @@
 HIGHEST = lax.Precision.HIGHEST
 BOTH = ("col", "sub")
 SPARE = 16
+GROUP = 4
+BATCH = 8
 VMEM = pl.BlockSpec(memory_space=pltpu.VMEM)
 SMEM = pl.BlockSpec(memory_space=pltpu.SMEM)
 HBM = pl.BlockSpec(memory_space=pltpu.HBM)
@@ -201,17 +203,16 @@
         window[place * rows : (place + 1) * rows, :] = ref[:rows, :] * scale
     window[rows : 2 * rows, :] = own_ref[...]
 
-    @pl.loop(0, leaves)
-    def _(leaf):
+    for leaf in range(leaves):
         copy(leaf).wait()
+    for leaf in range(leaves):
         picked = []
         for k in range(slots):
             place = jnp.clip(far_ref[k, leaf] - first, 0, 3 * leaves - 1)
             picked.append(window[pl.ds(pl.multiple_of(place * rank, rank), rank), :])
         here = coupling_ref[leaf]
         wide = jnp.concatenate([here[k] for k in range(slots)], axis=1)
-        at = pl.ds(pl.multiple_of(leaf * rank, rank), rank)
-        field_ref[at, :] = exact(wide, jnp.concatenate(picked, axis=0))
+        field_ref[leaf * rank : (leaf + 1) * rank, :] = exact(wide, jnp.concatenate(picked, axis=0))
 
 
 def far(leaf_far, near_index, coupling, low, own, high):
@@ -229,54 +230,91 @@
     )(leaf_far, near_index, in_hbm(coupling), low, own, high)[0]
 
 
-def near_body(near_ref, blocks_ref, own_ref, high_ref, acc_ref, held_ref, window, sems):
+def near_body(near_ref, blocks_ref, own_ref, high_ref, acc_ref, held_ref, list_ref, window, sems):
     leaves, slots, rows, _ = blocks_ref.shape
 
     def copy(leaf):
         return pltpu.make_async_copy(blocks_ref.at[leaf], held_ref.at[leaf], sems.at[leaf])
 
-    @pl.loop(0, leaves)
-    def _(leaf):
+    for leaf in range(leaves):
         copy(leaf).start()
 
     window[: leaves * rows, :] = own_ref[...]
     window[leaves * rows : 2 * leaves * rows, :] = high_ref[...]
     window[2 * leaves * rows :, :] = jnp.zeros((rows, high_ref.shape[1]), window.dtype)
     first = near_ref[0, 0]
-
-    @pl.loop(0, leaves)
-    def _(leaf):
-        copy(leaf).wait()
-        acc = None
-        for k in range(slots):
-            place = near_ref[k, leaf] - first
-            place = jnp.where(place < 0, 2 * leaves, jnp.minimum(place, 2 * leaves - 1))
-            start = pl.multiple_of(place * rows, rows)
-            term = jnp.dot(
-                held_ref[leaf, k], window[pl.ds(start, rows), :], preferred_element_type=jnp.float32
-            )
-            acc = term if acc is None else acc + term
-        acc_ref[pl.ds(pl.multiple_of(leaf * rows, rows), rows), :] = acc
+    room = list_ref.shape[1]
+
+    @pl.loop(0, room)
+    def _(i):
+        for row in range(4):
+            list_ref[row, i] = 0
+
+    half = leaves // 2
+
+    def note(leaf, counts):
+        found = jnp.int32(0)
+        for k in range(1, slots):
+            place = near_ref[k, leaf] - first + leaves
+            after = []
+            for i, valid in enumerate((place < half, (place >= half) & (place < leaves))):
+
+                @pl.when(valid)
+                def _(i=i, place=place, k=k, count=counts[i]):
+                    list_ref[2 * i, count] = leaf * slots + k
+                    list_ref[2 * i + 1, count] = jnp.maximum(place - i * half, 0)
+
+                after.append(counts[i] + valid.astype(jnp.int32))
+                found = found + valid.astype(jnp.int32)
+            counts = tuple(after)
+        list_ref[4, leaf] = found
+        return counts
+
+    counts = lax.fori_loop(0, leaves, note, (jnp.int32(0), jnp.int32(0)))
+    list_ref[5, 0] = counts[0]
+    list_ref[5, 1] = counts[1]
+
+    for group in range(0, leaves, GROUP):
+        for leaf in range(group, group + GROUP):
+            copy(leaf).wait()
+        for leaf in range(group, group + GROUP):
+            acc = None
+            for k in range(slots):
+                place = near_ref[k, leaf] - first
+                place = jnp.where(place < 0, 2 * leaves, jnp.minimum(place, 2 * leaves - 1))
+                start = pl.multiple_of(place * rows, rows)
+                term = jnp.dot(
+                    held_ref[leaf, k], window[pl.ds(start, rows), :], preferred_element_type=jnp.float32
+                )
+                acc = term if acc is None else acc + term
+            acc_ref[leaf * rows : (leaf + 1) * rows, :] = acc
 
 
 def near(near_index, blocks, own, high):
-    leaves, _, rows, _ = blocks.shape
-    return call(
+    leaves, slots, rows, _ = blocks.shape
+    room = leaves * slots + BATCH
+    return pl.pallas_call(
         near_body,
-        [SMEM, HBM, VMEM, VMEM],
-        [(own.shape, jnp.float32), (blocks.shape, blocks.dtype)],
-        scratch=[
+        in_specs=[SMEM, HBM, VMEM, VMEM],
+        out_specs=[VMEM, VMEM, SMEM],
+        out_shape=[
+            jax.ShapeDtypeStruct(own.shape, jnp.float32),
+            jax.ShapeDtypeStruct(blocks.shape, blocks.dtype),
+            jax.ShapeDtypeStruct((6, room), jnp.int32),
+        ],
+        scratch_shapes=[
             pltpu.VMEM(((2 * leaves + 1) * rows, own.shape[1]), own.dtype),
             pltpu.SemaphoreType.DMA((leaves,)),
         ],
-        mib=32,
+        compiler_params=pltpu.CompilerParams(vmem_limit_bytes=32 * 2**20),
+        cost_estimate=pl.CostEstimate(flops=0, bytes_accessed=0, transcendentals=0),
         name="near_own_and_high",
     )(near_index, in_hbm(blocks), own, high)
 
 
 def down_body(
     straight, partner_ref, top_partner_ref, stack_ref, cols_ref, coupling_ref, top_coupling_ref, cluster_ref,
-    transfer_ref, field_ref, basis_ref, acc_ref, out_ref, fields,
+    transfer_ref, field_ref, basis_ref, acc_ref, sum_ref, out_ref, fields, held, sem,
 ):
     leaves, rank, rows = basis_ref.shape
     col = lax.axis_index("col")
@@ -293,66 +331,114 @@
     fields[...] = (field_ref[...] + exact(transfer, cluster)).astype(fields.dtype)
     for leaf in range(leaves):
         here = slice(leaf * rows, (leaf + 1) * rows)
-        out_ref[here, :] = acc_ref[here, :] + lax.dot_general(
+        total = acc_ref[here, :] + lax.dot_general(
             basis_ref[leaf],
             fields[leaf * rank : (leaf + 1) * rank, :],
             (((0,), (0,)), ((), ())),
             preferred_element_type=jnp.float32,
         )
+        sum_ref[here, :] = total
+        held[here, :] = total.astype(held.dtype)
+    copy = pltpu.make_async_copy(held, out_ref, sem)
+    copy.start()
+    copy.wait()
 
 
 def down(partner, top_partner, stack, cols, coupling, top_coupling, cluster_transfer, transfer, field, basis, acc):
     count = lax.axis_size("col")
-    return call(
+    return pl.pallas_call(
         functools.partial(down_body, bool(count & (count - 1))),
-        [SMEM] * 2 + [VMEM] * 9,
-        [(acc.shape, jnp.float32)],
-        scratch=[pltpu.VMEM(field.shape, jnp.bfloat16)],
+        in_specs=[SMEM] * 2 + [VMEM] * 9,
+        out_specs=[VMEM, HBM],
+        out_shape=[jax.ShapeDtypeStruct(acc.shape, jnp.float32), pltpu.HBM(acc.shape, jnp.bfloat16)],
+        scratch_shapes=[
+            pltpu.VMEM(field.shape, jnp.bfloat16),
+            pltpu.VMEM(acc.shape, jnp.bfloat16),
+            pltpu.SemaphoreType.DMA,
+        ],
+        compiler_params=pltpu.CompilerParams(vmem_limit_bytes=16 * 2**20),
+        cost_estimate=pl.CostEstimate(flops=0, bytes_accessed=0, transcendentals=0),
         name="fields_down",
-    )(partner, top_partner, stack, cols, coupling, top_coupling, cluster_transfer, transfer, field, basis, acc)[0]
-
-
-def last_body(near_ref, blocks_ref, low_first_ref, low_second_ref, acc_ref, out_ref, held, sem):
-    leaves, slots, rows, _ = blocks_ref.shape
-    split = leaves // 2
-    first = near_ref[0, 0] - leaves
+    )(partner, top_partner, stack, cols, coupling, top_coupling, cluster_transfer, transfer, field, basis, acc)
+
+
+def add_listed(list_ref, part, blocks_ref, low_ref, acc_ref):
+    _, slots, rows, _ = blocks_ref.shape
+    count = list_ref[5, part]
+
+    @pl.loop(0, pl.cdiv(count, BATCH))
+    def _(batch):
+        terms = []
+        for i in range(BATCH):
+            at = list_ref[2 * part, batch * BATCH + i]
+            start = pl.multiple_of(list_ref[2 * part + 1, batch * BATCH + i] * rows, rows)
+            block = blocks_ref[at // slots, lax.rem(at, slots)]
+            terms.append(jnp.dot(block, low_ref[pl.ds(start, rows), :], preferred_element_type=jnp.float32))
+        for i in range(BATCH):
+            at = batch * BATCH + i
+
+            @pl.when(at < count)
+            def _(i=i, at=at):
+                start = pl.multiple_of(list_ref[2 * part, at] // slots * rows, rows)
+                acc_ref[pl.ds(start, rows), :] += terms[i]
+
+
+def low_body(list_ref, blocks_ref, low_ref, acc_in, acc_ref):
+    add_listed(list_ref, 0, blocks_ref, low_ref, acc_ref)
+
+
+def near_low(places, blocks, low, acc):
+    return pl.pallas_call(
+        low_body,
+        in_specs=[SMEM] + [VMEM] * 3,
+        out_specs=VMEM,
+        out_shape=jax.ShapeDtypeStruct(acc.shape, acc.dtype),
+        input_output_aliases={3: 0},
+        compiler_params=pltpu.CompilerParams(vmem_limit_bytes=16 * 2**20),
+        cost_estimate=pl.CostEstimate(flops=0, bytes_accessed=0, transcendentals=0),
+        name="near_low_first",
+    )(places, blocks, low, acc)
+
+
+def last_body(list_ref, blocks_ref, low_ref, acc_ref, out_in, out_ref, held, sems):
+    leaves, _, rows, _ = blocks_ref.shape
+    add_listed(list_ref, 1, blocks_ref, low_ref, acc_ref)
 
     def copy(leaf):
-        here = pl.ds(pl.multiple_of(leaf * rows, rows), rows)
-        return pltpu.make_async_copy(held.at[here, :], out_ref.at[here, :], sem)
-
-    @pl.loop(0, leaves)
-    def _(leaf):
-        here = pl.ds(pl.multiple_of(leaf * rows, rows), rows)
-        for k in range(1, slots):
-            place = jnp.maximum(near_ref[k, leaf] - first, 0)
-
-            def add(ref, at):
-                start = pl.multiple_of(at * rows, rows)
-                acc_ref[here, :] += jnp.dot(
-                    blocks_ref[leaf, k], ref[pl.ds(start, rows), :], preferred_element_type=jnp.float32
-                )
-
-            pl.when(place < split)(lambda: add(low_first_ref, place))
-            pl.when((place >= split) & (place < leaves))(lambda: add(low_second_ref, place - split))
-
-        held[here, :] = acc_ref[here, :].astype(held.dtype)
-        copy(leaf).start()
-
-    pltpu.make_async_copy(held, out_ref, sem).wait()
-
-
-def last(near_index, blocks, low_first, low_second, acc):
+        here = slice(leaf * rows, (leaf + 1) * rows)
+        return pltpu.make_async_copy(held.at[here, :], out_ref.at[here, :], sems.at[leaf])
+
+    for leaf in range(leaves):
+
+        @pl.when(list_ref[4, leaf] > 0)
+        def _(leaf=leaf):
+            here = slice(leaf * rows, (leaf + 1) * rows)
+            held[here, :] = acc_ref[here, :].astype(held.dtype)
+            copy(leaf).start()
+
+    for leaf in range(leaves):
+
+        @pl.when(list_ref[4, leaf] > 0)
+        def _(leaf=leaf):
+            copy(leaf).wait()
+
+
+def last(places, blocks, low, acc, out):
+    leaves = blocks.shape[0]
     return pl.pallas_call(
         last_body,
-        in_specs=[SMEM] + [VMEM] * 4,
+        in_specs=[SMEM] + [VMEM] * 3 + [HBM],
         out_specs=HBM,
-        out_shape=jax.ShapeDtypeStruct(acc.shape, low_first.dtype),
-        scratch_shapes=[pltpu.VMEM(acc.shape, low_first.dtype), pltpu.SemaphoreType.DMA],
+        out_shape=jax.ShapeDtypeStruct(out.shape, out.dtype),
+        input_output_aliases={4: 0},
+        scratch_shapes=[
+            pltpu.VMEM(out.shape, out.dtype),
+            pltpu.SemaphoreType.DMA((leaves,)),
+        ],
         compiler_params=pltpu.CompilerParams(vmem_limit_bytes=32 * 2**20),
         cost_estimate=pl.CostEstimate(flops=0, bytes_accessed=0, transcendentals=0),
-        name="near_low",
-    )(near_index, blocks, low_first, low_second, acc)
+        name="near_low_second",
+    )(places, blocks, low, acc, out)
 
 
 def local(
@@ -381,7 +467,7 @@
     parts = gather_sub(short)
     first, high_vec, _ = lax.optimization_barrier((first, high_vec, long))
     low_first = shift(first, 1)
-    acc, blocks = near(near_index, near_blocks, own, high_vec)
+    acc, blocks, places = near(near_index, near_blocks, own, high_vec)
 
     second, parts, low_part, high_part, acc = lax.optimization_barrier((second, parts, low_part, high_part, acc))
     low_second = shift(second, 1)
@@ -391,10 +477,11 @@
     stack, top = cluster_sums(pair, low_part, high_part, parts)
     cols = gather_col(top)
     field = far(leaf_far, near_index, leaf_coupling, low_part, coefs, high_part)
-    acc = down(
+    acc, out = down(
         cluster_partner, top_partner, stack, cols, couple, top_couple, cluster, transfer, field, basis, acc
     )
-    return last(near_index, blocks, low_first, low_second, acc)
+    acc = near_low(places, blocks, low_first, acc)
+    return last(places, blocks, low_second, acc, out)
 
 
 def solution(mesh):

time: 66.9 us -> 63.3 us (0.946)
  waiting for transfers between devices: 17.5 us -> 23.4 us
  starting transfers between devices: 24.9 us -> 19.3 us
  Pallas kernels: 23.9 us -> 19.6 us
    ppermute x1, waiting for transfers between devices: 0.01 us -> 5.75 us  [gather_sub(): parts.append(lax.ppermute(value, 'sub', [(0, count - 1), (count - 1, 0)]))]
    ppermute x1, waiting for transfers between devices: 5.49 us -> 0.83 us  [gather_sub(): parts.append(lax.ppermute(value, 'sub', pairs))]
    ppermute x5, waiting for transfers between devices: 9.57 us -> 14.1 us  [shift(): return lax.ppermute(value, BOTH, pairs)]
    ppermute x3, starting transfers between devices: 7.09 us -> 3.66 us  [gather_col(): value = join(value, lax.ppermute(value, 'col', pairs))]
    ppermute x1, starting transfers between devices: 2.5 us -> 0.07 us  [gather_sub(): parts.append(lax.ppermute(value, 'sub', pairs))]
    ppermute x1, starting transfers between devices: 5.16 us -> 7.49 us  [gather_sub(): parts.append(lax.ppermute(value, 'sub', [(0, count - 1), (count - 1, 0)]))]
    pallas_call x3 -> x4, Pallas kernels: 15.7 us -> 13.4 us  [the longest x1 5.53 us: near(): pl.pallas_call(near_body, in_specs=[SMEM, HBM, VMEM, VMEM], out_specs=[VM...]
    pallas_call x1, Pallas kernels: 5.53 us -> 3.46 us  [far(): call(far_body, [SMEM] * 2 + [HBM] + [VMEM] * 3, [(own.shape, jnp.float32)...]
  transfers between devices with their start and end apart: 10 -> 10, of which waited for: 5 -> 6; matrix products, arithmetic and copies ran while one was open for 0% -> 0% of each run, Pallas kernels for 26% -> 27%
where the time goes in v4:
time: 63.3 us; the launch traced here: 62.6 us
  waiting for transfers between devices  23.4 us (37%)
  Pallas kernels  19.6 us (31%)
  starting transfers between devices  19.3 us (30%)
    ppermute x5, waiting for transfers between devices, shift(): return lax.ppermute(value, BOTH, pairs)  14.1 us
    ppermute x5, starting transfers between devices, shift(): return lax.ppermute(value, BOTH, pairs)  8.14 us
    ppermute x1, starting transfers between devices, gather_sub(): parts.append(lax.ppermute(value, 'sub', [(0, count - 1), (count - 1, 0)]))  7.49 us
    ppermute x1, waiting for transfers between devices, gather_sub(): parts.append(lax.ppermute(value, 'sub', [(0, count - 1), (count - 1, 0)]))  5.75 us
    pallas_call x1, Pallas kernels, near(): pl.pallas_call(near_body, in_specs=[SMEM, HBM, VMEM, VMEM], out_specs=[VM...  5.53 us
    ppermute x3, starting transfers between devices, gather_col(): value = join(value, lax.ppermute(value, 'col', pairs))  3.66 us
    pallas_call x1, Pallas kernels, far(): call(far_body, [SMEM] * 2 + [HBM] + [VMEM] * 3, [(own.shape, jnp.float32)...  3.46 us
    pallas_call x1, Pallas kernels, down(): pl.pallas_call(functools.partial(down_body, bool(count & count - 1)), in_...  3.33 us
  transfers between devices with their start and end apart: 10, of which 6 were waited for; matrix products, arithmetic and copies ran while one was open for 0% of the time, Pallas kernels for 27%

profile of v4, /device:TPU:31, one launch (start us, length us, event | category | flops | bytes accessed | tf_op | source)
XLA Modules:
  0.0 62.6 jit_solution(6408881215435295464)
XLA Ops:
  0.0 0.0 copy-start
  0.0 2.3 %collective-permute-start = (bf16[4096,128]{1,0:T(8,128)(2,1)}, bf16[4096,128]{1,0:T(8,128)(2,1)S(1)}, u32[]{:S(2)}, u32[]{:S(2)}) collective-permute-start(bf16[4096,128]{1,0:T(8,128)(2,1)} %refs_0_.1), channel_id=1, source_target_pairs={{1,0},{2,1},{3,2},{4,3},{5,4},{6,5},{7,6},{8,7},{9,8},{10,9},{11,1... | collective-permute-start | bytes 3145736 | tf_op jit(solution)/shard_map/ppermute | solution.py:36
  2.3 2.6 %leaf_and_cluster_coefs.1 = (bf16[4096,128]{1,0:T(8,128)(2,1)S(1)}, bf16[16,32,256]{2,1,0:T(8,128)(2,1)S(1)}, f32[16,32,32]{2,1,0:T(8,128)S(1)}, f32[1,32,32]{2,...) custom-call(bf16[4096,128]{1,0:T(8,128)(2,1)} %refs_0_.1, ...), custom_call_target="tpu_custom_call" | custom-call | tf_op jit(solution)/shard_map/leaf_and_cluster_coefs/pallas_call | solution.py:98
  4.9 2.0 %collective-permute-start.4 = (f16[608,128]{1,0:T(8,128)(2,1)S(1)}, f16[608,128]{1,0:T(8,128)(2,1)S(1)}, u32[]{:S(2)}, u32[]{:S(2)}) collective-permute-start(f16[608,128]{1,0:T(8,128)(2,1)S(1)} %convert_element_type.18), channel_id=1, source_target_pairs={{1,0},{2,1},{3,2},{4,3},{5,4},{6,5},{7,6},{8,7},{9,8},{10,9},{11,1... | collective-permute-start | bytes 466952 | tf_op jit(solution)/shard_map/ppermute | solution.py:36
  7.0 1.3 %collective-permute-start.3 = (f16[608,128]{1,0:T(8,128)(2,1)S(1)}, f16[608,128]{1,0:T(8,128)(2,1)S(1)}, u32[]{:S(2)}, u32[]{:S(2)}) collective-permute-start(f16[608,128]{1,0:T(8,128)(2,1)S(1)} %convert_element_type.18), channel_id=1, source_target_pairs={{0,1},{1,2},{2,3},{3,4},{4,5},{5,6},{6,7},{7,8},{8,9},{9,10},{10,1... | collective-permute-start | bytes 466952 | tf_op jit(solution)/shard_map/ppermute | solution.py:36
  8.3 7.5 %collective-permute-start.2 = (f16[80,128]{1,0:T(8,128)(2,1)S(1)}, f16[80,128]{1,0:T(8,128)(2,1)S(1)}, u32[]{:S(2)}, u32[]{:S(2)}) collective-permute-start(f16[80,128]{1,0:T(8,128)(2,1)S(1)} %convert_element_type.19), channel_id=1, source_target_pairs={{0,3},{3,0},{4,7},{7,4},{8,11},{11,8},{12,15},{15,12},{16,19},{19,... | collective-permute-start | bytes 61448 | tf_op jit(solution)/shard_map/ppermute | solution.py:173
  15.8 0.1 collective-permute-start.1
  15.8 8.5 %collective-permute-done.high_ref = bf16[4096,128]{1,0:T(8,128)(2,1)S(1)} collective-permute-done((bf16[4096,128]{1,0:T(8,128)(2,1)}, bf16[4096,128]{1,0:T(8,128)(2,1)S(1)}, u32[]{:S(2)}, u32[]{:S(2)}) %collective-permute-start) | collective-permute-done | bytes 1048608 | tf_op jit(solution)/shard_map/ppermute | solution.py:36
  24.3 1.3 %collective-permute-start.6 = (bf16[2064,128]{1,0:T(8,128)(2,1)S(1)}, bf16[2064,128]{1,0:T(8,128)(2,1)S(1)}, u32[]{:S(2)}, u32[]{:S(2)}) collective-permute-start(bf16[2064,128]{1,0:T(8,128)(2,1)S(1)} %get-tuple-element.42), channel_id=1, source_target_pairs={{0,1},{1,2},{2,3},{3,4},{4,5},{5,6},{6,7},{7,8},{8,9},{9,10},{10,1... | collective-permute-start | bytes 1585160 | tf_op jit(solution)/shard_map/ppermute | solution.py:36
  25.6 0.0 copy-done
  25.6 0.0 copy-start.1
  25.6 5.5 %near_own_and_high.1 = (f32[4096,128]{1,0:T(8,128)S(1)}, bf16[16,4,256,256]{3,2,1,0:T(8,128)(2,1)S(1)}, s32[6,72]{1,0:T(8,128)S(1)}) custom-call(s32[4,16]{1,0:T(4,128)S(1)} %bitcast.2, bf16[16,4,256,256]{3,2,1,0:T(8,128)(2,1)} %blocks_ref.1, bf16[4096,128]{1,0:T(8,128)(2,1)S(1)} %get-tuple-element.32.own_ref, ...), custom_call_target="tpu_custom_call" | custom-call | tf_op jit(solution)/shard_map/near_own_and_high/pallas_call | solution.py:296
  31.2 5.8 %collective-permute-done.2 = f16[80,128]{1,0:T(8,128)(2,1)S(1)} collective-permute-done((f16[80,128]{1,0:T(8,128)(2,1)S(1)}, f16[80,128]{1,0:T(8,128)(2,1)S(1)}, u32[]{:S(2)}, u32[]{:S(2)}) %collective-permute-start.2) | collective-permute-done | bytes 20512 | tf_op jit(solution)/shard_map/ppermute | solution.py:173
  36.9 0.8 %collective-permute-done.1 = f16[80,128]{1,0:T(8,128)(2,1)S(1)} collective-permute-done((f16[80,128]{1,0:T(8,128)(2,1)S(1)}, f16[80,128]{1,0:T(8,128)(2,1)S(1)}, u32[]{:S(2)}, u32[]{:S(2)}) %collective-permute-start.1) | collective-permute-done | bytes 20512 | tf_op jit(solution)/shard_map/ppermute | solution.py:171
  37.8 0.0 collective-permute-done.4
  37.8 0.0 collective-permute-done.3
  37.8 1.3 %collective-permute-start.5 = (bf16[2048,128]{1,0:T(8,128)(2,1)S(1)}, bf16[2048,128]{1,0:T(8,128)(2,1)S(1)}, u32[]{:S(2)}, u32[]{:S(2)}) collective-permute-start(bf16[2048,128]{1,0:T(8,128)(2,1)S(1)} %get-tuple-element.41), channel_id=1, source_target_pairs={{0,1},{1,2},{2,3},{3,4},{4,5},{5,6},{6,7},{7,8},{8,9},{9,10},{10,1... | collective-permute-start | bytes 1572872 | tf_op jit(solution)/shard_map/ppermute | solution.py:36
  39.1 0.0 copy-start.2
  39.2 0.0 copy-start.3
  39.2 1.1 %collective-permute-start.7 = (f32[1,32,128]{2,1,0:T(8,128)S(1)}, f32[1,32,128]{2,1,0:T(8,128)S(1)}, u32[]{:S(2)}, u32[]{:S(2)}) collective-permute-start(f32[1,32,128]{2,1,0:T(8,128)S(1)} %get-tuple-element.49.first_ref), channel_id=1, source_target_pairs={{0,4},{4,0},{8,12},{12,8},{16,20},{20,16},{24,28},{28,24},{1,5},{5... | collective-permute-start | bytes 49160 | tf_op jit(solution)/shard_map/ppermute | solution.py:184
  40.4 0.8 %collective-permute-done.7.second_ref = f32[1,32,128]{2,1,0:T(8,128)S(1)} collective-permute-done((f32[1,32,128]{2,1,0:T(8,128)S(1)}, f32[1,32,128]{2,1,0:T(8,128)S(1)}, u32[]{:S(2)}, u32[]{:S(2)}) %collective-permute-start.7) | collective-permute-done | bytes 16416 | tf_op jit(solution)/shard_map/ppermute | solution.py:184
  41.2 1.2 %collective-permute-start.8 = (f32[2,32,128]{2,1,0:T(8,128)S(1)}, f32[2,32,128]{2,1,0:T(8,128)S(1)}, u32[]{:S(2)}, u32[]{:S(2)}) collective-permute-start(f32[2,32,128]{2,1,0:T(8,128)S(1)} %join_cols.3.first_ref), channel_id=1, source_target_pairs={{0,8},{4,12},{8,0},{12,4},{16,24},{20,28},{24,16},{28,20},{1,9},{5... | collective-permute-start | bytes 98312 | tf_op jit(solution)/shard_map/ppermute | solution.py:184
  42.4 1.9 %collective-permute-done.8.second_ref = f32[2,32,128]{2,1,0:T(8,128)S(1)} collective-permute-done((f32[2,32,128]{2,1,0:T(8,128)S(1)}, f32[2,32,128]{2,1,0:T(8,128)S(1)}, u32[]{:S(2)}, u32[]{:S(2)}) %collective-permute-start.8) | collective-permute-done | bytes 32800 | tf_op jit(solution)/shard_map/ppermute | solution.py:184
  44.3 1.3 %collective-permute-start.9 = (f32[4,32,128]{2,1,0:T(8,128)S(1)}, f32[4,32,128]{2,1,0:T(8,128)S(1)}, u32[]{:S(2)}, u32[]{:S(2)}) collective-permute-start(f32[4,32,128]{2,1,0:T(8,128)S(1)} %join_cols.4.first_ref), channel_id=1, source_target_pairs={{0,16},{4,20},{8,24},{12,28},{16,0},{20,4},{24,8},{28,12},{1,17},{... | collective-permute-start | bytes 196616 | tf_op jit(solution)/shard_map/ppermute | solution.py:184
  45.6 0.0 copy-done.1
  45.6 3.5 %far_field_of_leaves.1.field_ref = f32[512,128]{1,0:T(8,128)S(1)} custom-call(s32[8,16]{1,0:T(8,128)S(1)} %bitcast.4, s32[4,16]{1,0:T(4,128)S(1)} %bitcast.3, f32[16,8,32,32]{3,2,1,0:T(8,128)} %coupling_in.1, f32[608,128]{1,0:T(8,128)S(1)} %convert_element_type.20.low_ref, f32[512,128]{1,0:T(8,128)S(1)} %get-tuple-element.54.own_ref, ...), custom_call_target="tpu_custom_call" | custom-call | tf_op jit(solution)/shard_map/far_field_of_leaves/pallas_call | solution.py:220
  49.1 0.0 collective-permute-done.9.second_ref
  49.1 0.0 copy-done.2
  49.1 0.0 copy-done.3
  49.1 3.3 %fields_down.1 = (f32[4096,128]{1,0:T(8,128)S(1)}, bf16[4096,128]{1,0:T(8,128)(2,1)}) custom-call(s32[1,4]{1,0:T(1,128)S(1)} %copy-done.2, s32[1,8]{1,0:T(1,128)S(1)} %copy-done.3, f32[4,32,128]{2,1,0:T(8,128)S(1)} %get-tuple-element.48.stack_ref, f32[8,32,128]{2,1,0:T(8,128)S(1)} %join_cols.5.cols_ref, f32[1,4,32,32]{3,2,1,0:T(8,128)S(1)} %get-tuple-element.50.coupling_ref, ...), custom_call_target="tpu_custom_call" | custom-call | tf_op jit(solution)/shard_map/fields_down/pallas_call | solution.py:349
  52.5 0.0 collective-permute-done.6.low_ref
  52.5 1.7 %near_low_first.1.acc_ref = f32[4096,128]{1,0:T(8,128)S(1)} custom-call(s32[6,72]{1,0:T(8,128)S(1)} %get-tuple-element.36.list_ref, bf16[16,4,256,256]{3,2,1,0:T(8,128)(2,1)S(1)} %get-tuple-element.37.blocks_ref, bf16[2064,128]{1,0:T(8,128)(2,1)S(1)} %collective-permute-done.6.low_ref, ...), custom_call_target="tpu_custom_call", output_to_operand_aliasing={{}: (3, {})} | custom-call | tf_op jit(solution)/shard_map/near_low_first/pallas_call | solution.py:391
  54.2 5.6 %collective-permute-done.5.low_ref = bf16[2048,128]{1,0:T(8,128)(2,1)S(1)} collective-permute-done((bf16[2048,128]{1,0:T(8,128)(2,1)S(1)}, bf16[2048,128]{1,0:T(8,128)(2,1)S(1)}, u32[]{:S(2)}, u32[]{:S(2)}) %collective-permute-start.5) | collective-permute-done | bytes 524320 | tf_op jit(solution)/shard_map/ppermute | solution.py:36
  59.8 2.9 %near_low_second.1 = bf16[4096,128]{1,0:T(8,128)(2,1)} custom-call(s32[6,72]{1,0:T(8,128)S(1)} %get-tuple-element.36.list_ref, bf16[16,4,256,256]{3,2,1,0:T(8,128)(2,1)S(1)} %get-tuple-element.37.blocks_ref, bf16[2048,128]{1,0:T(8,128)(2,1)S(1)} %collective-permute-done.5.low_ref, ...), custom_call_target="tpu_custom_call", output_to_operand_aliasing={{}: (4, {})} | custom-call | tf_op jit(solution)/shard_map/near_low_second/pallas_call | solution.py:428
  (10 shorter events, 0.2 us)
Async XLA Ops:
  0.0 25.6 %copy-start = (s32[16,4]{0,1:T(4,128)S(1)}, s32[16,4]{0,1:T(4,128)}, u32[]{:S(2)}) copy-start(s32[16,4]{0,1:T(4,128)} %param.14) | copy-start | bytes 772
  0.0 24.3 %collective-permute-start = (bf16[4096,128]{1,0:T(8,128)(2,1)}, bf16[4096,128]{1,0:T(8,128)(2,1)S(1)}, u32[]{:S(2)}, u32[]{:S(2)}) collective-permute-start(bf16[4096,128]{1,0:T(8,128)(2,1)} %refs_0_.1), channel_id=1, source_target_pairs={{1,0},{2,1},{3,2},{4,3},{5,4},{6,5},{7,6},{8,7},{9,8},{10,9},{11,1... | collective-permute-start | bytes 3145736 | tf_op jit(solution)/shard_map/ppermute | solution.py:36
  4.9 32.8 %collective-permute-start.4 = (f16[608,128]{1,0:T(8,128)(2,1)S(1)}, f16[608,128]{1,0:T(8,128)(2,1)S(1)}, u32[]{:S(2)}, u32[]{:S(2)}) collective-permute-start(f16[608,128]{1,0:T(8,128)(2,1)S(1)} %convert_element_type.18), channel_id=1, source_target_pairs={{1,0},{2,1},{3,2},{4,3},{5,4},{6,5},{7,6},{8,7},{9,8},{10,9},{11,1... | collective-permute-start | bytes 466952 | tf_op jit(solution)/shard_map/ppermute | solution.py:36
  7.0 30.8 %collective-permute-start.3 = (f16[608,128]{1,0:T(8,128)(2,1)S(1)}, f16[608,128]{1,0:T(8,128)(2,1)S(1)}, u32[]{:S(2)}, u32[]{:S(2)}) collective-permute-start(f16[608,128]{1,0:T(8,128)(2,1)S(1)} %convert_element_type.18), channel_id=1, source_target_pairs={{0,1},{1,2},{2,3},{3,4},{4,5},{5,6},{6,7},{7,8},{8,9},{9,10},{10,1... | collective-permute-start | bytes 466952 | tf_op jit(solution)/shard_map/ppermute | solution.py:36
  8.3 28.7 %collective-permute-start.2 = (f16[80,128]{1,0:T(8,128)(2,1)S(1)}, f16[80,128]{1,0:T(8,128)(2,1)S(1)}, u32[]{:S(2)}, u32[]{:S(2)}) collective-permute-start(f16[80,128]{1,0:T(8,128)(2,1)S(1)} %convert_element_type.19), channel_id=1, source_target_pairs={{0,3},{3,0},{4,7},{7,4},{8,11},{11,8},{12,15},{15,12},{16,19},{19,... | collective-permute-start | bytes 61448 | tf_op jit(solution)/shard_map/ppermute | solution.py:173
  15.8 22.0 %collective-permute-start.1 = (f16[80,128]{1,0:T(8,128)(2,1)S(1)}, f16[80,128]{1,0:T(8,128)(2,1)S(1)}, u32[]{:S(2)}, u32[]{:S(2)}) collective-permute-start(f16[80,128]{1,0:T(8,128)(2,1)S(1)} %convert_element_type.19), channel_id=1, source_target_pairs={{0,2},{1,3},{2,0},{3,1},{4,6},{5,7},{6,4},{7,5},{8,10},{9,11},{10,... | collective-permute-start | bytes 61448 | tf_op jit(solution)/shard_map/ppermute | solution.py:171
  24.3 28.1 %collective-permute-start.6 = (bf16[2064,128]{1,0:T(8,128)(2,1)S(1)}, bf16[2064,128]{1,0:T(8,128)(2,1)S(1)}, u32[]{:S(2)}, u32[]{:S(2)}) collective-permute-start(bf16[2064,128]{1,0:T(8,128)(2,1)S(1)} %get-tuple-element.42), channel_id=1, source_target_pairs={{0,1},{1,2},{2,3},{3,4},{4,5},{5,6},{6,7},{7,8},{8,9},{9,10},{10,1... | collective-permute-start | bytes 1585160 | tf_op jit(solution)/shard_map/ppermute | solution.py:36
  25.6 20.0 %copy-start.1 = (s32[16,8]{0,1:T(8,128)S(1)}, s32[16,8]{0,1:T(8,128)}, u32[]{:S(2)}) copy-start(s32[16,8]{0,1:T(8,128)} %param.18) | copy-start | bytes 1540
  37.8 22.0 %collective-permute-start.5 = (bf16[2048,128]{1,0:T(8,128)(2,1)S(1)}, bf16[2048,128]{1,0:T(8,128)(2,1)S(1)}, u32[]{:S(2)}, u32[]{:S(2)}) collective-permute-start(bf16[2048,128]{1,0:T(8,128)(2,1)S(1)} %get-tuple-element.41), channel_id=1, source_target_pairs={{0,1},{1,2},{2,3},{3,4},{4,5},{5,6},{6,7},{7,8},{8,9},{9,10},{10,1... | collective-permute-start | bytes 1572872 | tf_op jit(solution)/shard_map/ppermute | solution.py:36
  39.1 10.0 %copy-start.2 = (s32[1,4]{1,0:T(1,128)S(1)}, s32[1,4]{1,0:T(1,128)}, u32[]{:S(2)}) copy-start(s32[1,4]{1,0:T(1,128)} %partner_ref.1) | copy-start | bytes 52
  39.2 10.0 %copy-start.3 = (s32[1,8]{1,0:T(1,128)S(1)}, s32[1,8]{1,0:T(1,128)}, u32[]{:S(2)}) copy-start(s32[1,8]{1,0:T(1,128)} %top_partner_ref.1) | copy-start | bytes 100
  39.2 2.0 %collective-permute-start.7 = (f32[1,32,128]{2,1,0:T(8,128)S(1)}, f32[1,32,128]{2,1,0:T(8,128)S(1)}, u32[]{:S(2)}, u32[]{:S(2)}) collective-permute-start(f32[1,32,128]{2,1,0:T(8,128)S(1)} %get-tuple-element.49.first_ref), channel_id=1, source_target_pairs={{0,4},{4,0},{8,12},{12,8},{16,20},{20,16},{24,28},{28,24},{1,5},{5... | collective-permute-start | bytes 49160 | tf_op jit(solution)/shard_map/ppermute | solution.py:184
  41.2 3.1 %collective-permute-start.8 = (f32[2,32,128]{2,1,0:T(8,128)S(1)}, f32[2,32,128]{2,1,0:T(8,128)S(1)}, u32[]{:S(2)}, u32[]{:S(2)}) collective-permute-start(f32[2,32,128]{2,1,0:T(8,128)S(1)} %join_cols.3.first_ref), channel_id=1, source_target_pairs={{0,8},{4,12},{8,0},{12,4},{16,24},{20,28},{24,16},{28,20},{1,9},{5... | collective-permute-start | bytes 98312 | tf_op jit(solution)/shard_map/ppermute | solution.py:184
  44.3 4.8 %collective-permute-start.9 = (f32[4,32,128]{2,1,0:T(8,128)S(1)}, f32[4,32,128]{2,1,0:T(8,128)S(1)}, u32[]{:S(2)}, u32[]{:S(2)}) collective-permute-start(f32[4,32,128]{2,1,0:T(8,128)S(1)} %join_cols.4.first_ref), channel_id=1, source_target_pairs={{0,16},{4,20},{8,24},{12,28},{16,0},{20,4},{24,8},{28,12},{1,17},{... | collective-permute-start | bytes 196616 | tf_op jit(solution)/shard_map/ppermute | solution.py:184

commit v5 on v4

--- a/solution.py
+++ b/solution.py
@@ -36,6 +36,11 @@
     return lax.ppermute(value, BOTH, pairs)
 
 
+def shift_around(value, by):
+    count = lax.axis_size(BOTH)
+    return lax.ppermute(value, BOTH, [(i, (i + by) % count) for i in range(count)])
+
+
 def exact(a, b, contract=(1, 0)):
     dims = (((contract[0],), (contract[1],)), ((), ()))
     return lax.dot_general(a, b, dims, precision=HIGHEST, preferred_element_type=jnp.float32)
@@ -58,8 +63,8 @@
     leaves, rank, rows = basis_ref.shape
     columns = vec_ref.shape[1]
     pairs = list(zip(sources, targets))
-    pairs.append((sources[0].at[: first_ref.shape[0], :], first_ref))
-    pairs.append((sources[0].at[vec_ref.shape[0] - second_ref.shape[0] :, :], second_ref))
+    pairs.append((sources[0].at[vec_ref.shape[0] - first_ref.shape[0] :, :], first_ref))
+    pairs.append((sources[0].at[: second_ref.shape[0], :], second_ref))
     copies = [pltpu.make_async_copy(source, target, sems.at[i]) for i, (source, target) in enumerate(pairs)]
     for copy in copies:
         copy.start()
@@ -165,13 +170,27 @@
 
 def gather_sub(value):
     count = lax.axis_size("sub")
-    parts = []
-    for step in range(2, count - 1):
-        pairs = [(i, (i + step) % count) for i in range(count)]
-        parts.append(lax.ppermute(value, "sub", pairs))
-    if count > 2:
-        parts.append(lax.ppermute(value, "sub", [(0, count - 1), (count - 1, 0)]))
-    return parts
+    return [
+        lax.ppermute(value, "sub", [(i, (i + step) % count) for i in range(count)])
+        for step in range(2, count - 1)
+    ]
+
+
+def onward_body(low_ref, high_ref, out_ref):
+    at = low_ref.shape[0] - out_ref.shape[0]
+    out_ref[...] = jnp.where(lax.axis_index("sub") == 0, low_ref[at:, :], high_ref[at:, :])
+
+
+def around(low, high, length):
+    subs, cols = lax.axis_size("sub"), lax.axis_size("col")
+    onward = call(
+        onward_body, [VMEM] * 2, [((length, low.shape[1]), jnp.float32)], name="passed_on"
+    )(low, high)[0]
+    pairs = []
+    for col in range(cols):
+        pairs.append((col * subs, (col - 1) % cols * subs))
+        pairs.append((col * subs + subs - 1, (col + 1) % cols * subs + subs - 1))
+    return lax.ppermute(onward.astype(jnp.float16), BOTH, pairs)
 
 
 def gather_col(value):
@@ -230,86 +249,99 @@
     )(leaf_far, near_index, in_hbm(coupling), low, own, high)[0]
 
 
-def near_body(near_ref, blocks_ref, own_ref, high_ref, acc_ref, held_ref, list_ref, window, sems):
+def load_body(blocks_ref, held_ref, sem):
+    copy = pltpu.make_async_copy(blocks_ref, held_ref, sem)
+    copy.start()
+    copy.wait()
+
+
+def load(blocks):
+    return pl.pallas_call(
+        load_body,
+        in_specs=[HBM],
+        out_specs=VMEM,
+        out_shape=pltpu.VMEM(blocks.shape, blocks.dtype),
+        scratch_shapes=[pltpu.SemaphoreType.DMA],
+        cost_estimate=pl.CostEstimate(flops=0, bytes_accessed=0, transcendentals=0),
+        compiler_params=pltpu.CompilerParams(vmem_limit_bytes=16 * 2**20),
+        name="load_near_blocks",
+    )(in_hbm(blocks))
+
+
+def near_body(
+    near_ref, blocks_ref, own_ref, high_ref, acc_ref, list_ref, found_ref, window
+):
     leaves, slots, rows, _ = blocks_ref.shape
-
-    def copy(leaf):
-        return pltpu.make_async_copy(blocks_ref.at[leaf], held_ref.at[leaf], sems.at[leaf])
-
-    for leaf in range(leaves):
-        copy(leaf).start()
 
     window[: leaves * rows, :] = own_ref[...]
     window[leaves * rows : 2 * leaves * rows, :] = high_ref[...]
     window[2 * leaves * rows :, :] = jnp.zeros((rows, high_ref.shape[1]), window.dtype)
     first = near_ref[0, 0]
-    room = list_ref.shape[1]
-
-    @pl.loop(0, room)
-    def _(i):
-        for row in range(4):
-            list_ref[row, i] = 0
 
     half = leaves // 2
-
-    def note(leaf, counts):
-        found = jnp.int32(0)
+    room = list_ref.shape[0] // 2
+    lane = lax.broadcasted_iota(jnp.int32, (1, list_ref.shape[1]), 1)
+    list_ref[...] = jnp.zeros_like(list_ref)
+
+    def note(leaf, carry):
+        found, counts = carry
         for k in range(1, slots):
             place = near_ref[k, leaf] - first + leaves
             after = []
-            for i, valid in enumerate((place < half, (place >= half) & (place < leaves))):
+            for i, valid in enumerate((place >= half, place < half)):
+                valid = valid & (place < leaves)
+                at = jnp.maximum(place - (1 - i) * half, 0)
+                entry = jnp.where(lane == 0, leaf * slots + k, jnp.where(lane == 1, at, 0))
 
                 @pl.when(valid)
-                def _(i=i, place=place, k=k, count=counts[i]):
-                    list_ref[2 * i, count] = leaf * slots + k
-                    list_ref[2 * i + 1, count] = jnp.maximum(place - i * half, 0)
-
-                after.append(counts[i] + valid.astype(jnp.int32))
-                found = found + valid.astype(jnp.int32)
+                def _(entry=entry, spot=i * room + counts[i]):
+                    list_ref[pl.ds(spot, 1), :] = entry
+
+                one = valid.astype(jnp.int32)
+                after.append(counts[i] + one)
+                found = found + jnp.where(lane == leaf, one, 0)
             counts = tuple(after)
-        list_ref[4, leaf] = found
-        return counts
-
-    counts = lax.fori_loop(0, leaves, note, (jnp.int32(0), jnp.int32(0)))
-    list_ref[5, 0] = counts[0]
-    list_ref[5, 1] = counts[1]
-
-    for group in range(0, leaves, GROUP):
-        for leaf in range(group, group + GROUP):
-            copy(leaf).wait()
-        for leaf in range(group, group + GROUP):
-            acc = None
-            for k in range(slots):
-                place = near_ref[k, leaf] - first
-                place = jnp.where(place < 0, 2 * leaves, jnp.minimum(place, 2 * leaves - 1))
-                start = pl.multiple_of(place * rows, rows)
-                term = jnp.dot(
-                    held_ref[leaf, k], window[pl.ds(start, rows), :], preferred_element_type=jnp.float32
-                )
-                acc = term if acc is None else acc + term
-            acc_ref[leaf * rows : (leaf + 1) * rows, :] = acc
+        return found, counts
+
+    found, counts = lax.fori_loop(
+        0, leaves, note, (jnp.zeros(lane.shape, jnp.int32), (jnp.int32(0), jnp.int32(0)))
+    )
+    found_ref[0:1, :] = found
+    found_ref[1:2, :] = jnp.where(lane == 0, counts[0], counts[1])
+
+    for leaf in range(leaves):
+        acc = None
+        for k in range(slots):
+            place = near_ref[k, leaf] - first
+            place = jnp.where(place < 0, 2 * leaves, jnp.minimum(place, 2 * leaves - 1))
+            start = pl.multiple_of(place * rows, rows)
+            term = jnp.dot(
+                blocks_ref[leaf, k], window[pl.ds(start, rows), :], preferred_element_type=jnp.float32
+            )
+            acc = term if acc is None else acc + term
+        acc_ref[leaf * rows : (leaf + 1) * rows, :] = acc
 
 
 def near(near_index, blocks, own, high):
     leaves, slots, rows, _ = blocks.shape
     room = leaves * slots + BATCH
+    lanes = -(-max(leaves, 2) // 128) * 128
     return pl.pallas_call(
         near_body,
-        in_specs=[SMEM, HBM, VMEM, VMEM],
-        out_specs=[VMEM, VMEM, SMEM],
+        in_specs=[SMEM] + [VMEM] * 3,
+        out_specs=[VMEM] * 3,
         out_shape=[
-            jax.ShapeDtypeStruct(own.shape, jnp.float32),
-            jax.ShapeDtypeStruct(blocks.shape, blocks.dtype),
-            jax.ShapeDtypeStruct((6, room), jnp.int32),
+            pltpu.VMEM(own.shape, jnp.float32),
+            jax.ShapeDtypeStruct((2 * room, lanes), jnp.int32),
+            jax.ShapeDtypeStruct((8, lanes), jnp.int32),
         ],
         scratch_shapes=[
             pltpu.VMEM(((2 * leaves + 1) * rows, own.shape[1]), own.dtype),
-            pltpu.SemaphoreType.DMA((leaves,)),
         ],
         compiler_params=pltpu.CompilerParams(vmem_limit_bytes=32 * 2**20),
         cost_estimate=pl.CostEstimate(flops=0, bytes_accessed=0, transcendentals=0),
         name="near_own_and_high",
-    )(near_index, in_hbm(blocks), own, high)
+    )(near_index, blocks, own, high)
 
 
 def down_body(
@@ -339,9 +371,8 @@
         )
         sum_ref[here, :] = total
         held[here, :] = total.astype(held.dtype)
-    copy = pltpu.make_async_copy(held, out_ref, sem)
-    copy.start()
-    copy.wait()
+        pltpu.make_async_copy(held.at[here, :], out_ref.at[here, :], sem).start()
+    pltpu.make_async_copy(held, out_ref, sem).wait()
 
 
 def down(partner, top_partner, stack, cols, coupling, top_coupling, cluster_transfer, transfer, field, basis, acc):
@@ -362,47 +393,50 @@
     )(partner, top_partner, stack, cols, coupling, top_coupling, cluster_transfer, transfer, field, basis, acc)
 
 
-def add_listed(list_ref, part, blocks_ref, low_ref, acc_ref):
+def add_listed(list_ref, found_ref, part, batch_size, blocks_ref, low_ref, acc_ref):
     _, slots, rows, _ = blocks_ref.shape
-    count = list_ref[5, part]
-
-    @pl.loop(0, pl.cdiv(count, BATCH))
+    count = found_ref[1, part]
+    room = list_ref.shape[0] // 2
+
+    @pl.loop(0, pl.cdiv(count, batch_size))
     def _(batch):
-        terms = []
-        for i in range(BATCH):
-            at = list_ref[2 * part, batch * BATCH + i]
-            start = pl.multiple_of(list_ref[2 * part + 1, batch * BATCH + i] * rows, rows)
+        terms, ats = [], []
+        spots = [part * room + batch * batch_size + i for i in range(batch_size)]
+        entries = [(list_ref[spot, 0], list_ref[spot, 1]) for spot in spots]
+        for at, place in entries:
+            start = pl.multiple_of(place * rows, rows)
             block = blocks_ref[at // slots, lax.rem(at, slots)]
             terms.append(jnp.dot(block, low_ref[pl.ds(start, rows), :], preferred_element_type=jnp.float32))
-        for i in range(BATCH):
-            at = batch * BATCH + i
-
-            @pl.when(at < count)
-            def _(i=i, at=at):
-                start = pl.multiple_of(list_ref[2 * part, at] // slots * rows, rows)
+            ats.append(at)
+        for i in range(batch_size):
+
+            @pl.when(batch * batch_size + i < count)
+            def _(i=i):
+                start = pl.multiple_of(ats[i] // slots * rows, rows)
                 acc_ref[pl.ds(start, rows), :] += terms[i]
 
 
-def low_body(list_ref, blocks_ref, low_ref, acc_in, acc_ref):
-    add_listed(list_ref, 0, blocks_ref, low_ref, acc_ref)
-
-
-def near_low(places, blocks, low, acc):
+def low_body(list_ref, found_ref, blocks_ref, low_ref, acc_in, acc_ref):
+    add_listed(list_ref, found_ref, 0, BATCH, blocks_ref, low_ref.at[SPARE:, :], acc_ref)
+
+
+def near_low(places, found, blocks, low, acc):
     return pl.pallas_call(
         low_body,
-        in_specs=[SMEM] + [VMEM] * 3,
+        in_specs=[VMEM] * 5,
         out_specs=VMEM,
         out_shape=jax.ShapeDtypeStruct(acc.shape, acc.dtype),
-        input_output_aliases={3: 0},
+        input_output_aliases={4: 0},
         compiler_params=pltpu.CompilerParams(vmem_limit_bytes=16 * 2**20),
         cost_estimate=pl.CostEstimate(flops=0, bytes_accessed=0, transcendentals=0),
         name="near_low_first",
-    )(places, blocks, low, acc)
-
-
-def last_body(list_ref, blocks_ref, low_ref, acc_ref, out_in, out_ref, held, sems):
+    )(places, found, blocks, low, acc)
+
+
+def last_body(list_ref, found_ref, blocks_ref, low_ref, acc_ref, out_in, out_ref, held, sems):
     leaves, _, rows, _ = blocks_ref.shape
-    add_listed(list_ref, 1, blocks_ref, low_ref, acc_ref)
+    touched = [found_ref[0, leaf] for leaf in range(leaves)]
+    add_listed(list_ref, found_ref, 1, GROUP, blocks_ref, low_ref, acc_ref)
 
     def copy(leaf):
         here = slice(leaf * rows, (leaf + 1) * rows)
@@ -410,7 +444,7 @@
 
     for leaf in range(leaves):
 
-        @pl.when(list_ref[4, leaf] > 0)
+        @pl.when(touched[leaf] > 0)
         def _(leaf=leaf):
             here = slice(leaf * rows, (leaf + 1) * rows)
             held[here, :] = acc_ref[here, :].astype(held.dtype)
@@ -418,19 +452,19 @@
 
     for leaf in range(leaves):
 
-        @pl.when(list_ref[4, leaf] > 0)
+        @pl.when(touched[leaf] > 0)
         def _(leaf=leaf):
             copy(leaf).wait()
 
 
-def last(places, blocks, low, acc, out):
+def last(places, found, blocks, low, acc, out):
     leaves = blocks.shape[0]
     return pl.pallas_call(
         last_body,
-        in_specs=[SMEM] + [VMEM] * 3 + [HBM],
+        in_specs=[VMEM] * 5 + [HBM],
         out_specs=HBM,
         out_shape=jax.ShapeDtypeStruct(out.shape, out.dtype),
-        input_output_aliases={4: 0},
+        input_output_aliases={5: 0},
         scratch_shapes=[
             pltpu.VMEM(out.shape, out.dtype),
             pltpu.SemaphoreType.DMA((leaves,)),
@@ -438,7 +472,7 @@
         compiler_params=pltpu.CompilerParams(vmem_limit_bytes=32 * 2**20),
         cost_estimate=pl.CostEstimate(flops=0, bytes_accessed=0, transcendentals=0),
         name="near_low_second",
-    )(places, blocks, low, acc, out)
+    )(places, found, blocks, low, acc, out)
 
 
 def local(
@@ -462,26 +496,29 @@
         vectors, leaf_basis, leaf_transfer, cluster_transfer, cluster_coupling, top_coupling
     )
     long, short = long.astype(jnp.float16), short.astype(jnp.float16)
-    low_part = shift(long, 1)
-    high_part = shift(long, -1)
+    low_part = shift_around(long, 1)
+    high_part = shift_around(long, -1)
     parts = gather_sub(short)
-    first, high_vec, _ = lax.optimization_barrier((first, high_vec, long))
+    first, near_blocks, _ = lax.optimization_barrier((first, near_blocks, long))
+    blocks = load(near_blocks)
     low_first = shift(first, 1)
-    acc, blocks, places = near(near_index, near_blocks, own, high_vec)
+    acc, places, found = near(near_index, blocks, own, high_vec)
 
     second, parts, low_part, high_part, acc = lax.optimization_barrier((second, parts, low_part, high_part, acc))
     low_second = shift(second, 1)
 
+    low_part, high_part = low_part.astype(jnp.float32), high_part.astype(jnp.float32)
+    if lax.axis_size("sub") > 2:
+        parts = parts + [around(low_part, high_part, short.shape[0])]
     parts = [part.astype(jnp.float32) for part in parts]
-    low_part, high_part = low_part.astype(jnp.float32), high_part.astype(jnp.float32)
     stack, top = cluster_sums(pair, low_part, high_part, parts)
     cols = gather_col(top)
     field = far(leaf_far, near_index, leaf_coupling, low_part, coefs, high_part)
     acc, out = down(
         cluster_partner, top_partner, stack, cols, couple, top_couple, cluster, transfer, field, basis, acc
     )
-    acc = near_low(places, blocks, low_first, acc)
-    return last(places, blocks, low_second, acc, out)
+    acc = near_low(places, found, blocks, low_first, acc)
+    return last(places, found, blocks, low_second, acc, out)
 
 
 def solution(mesh):

time: 63.3 us -> 62.1 us (0.981)
  starting transfers between devices: 19.3 us -> 16.5 us
  waiting for transfers between devices: 23.4 us -> 24.4 us
  Pallas kernels: 19.6 us -> 20.5 us
    ppermute x2 -> x4, waiting for transfers between devices: 6.58 us -> 10 us  [the longest x1 8.96 us: gather_sub(): lax.ppermute(value, 'sub', [(i, (i + step) % count) for i in range(count)])]
    ppermute x5 -> x3, starting transfers between devices: 8.14 us -> 4.7 us  [shift(): return lax.ppermute(value, BOTH, pairs)]
    ppermute x5 -> x3, waiting for transfers between devices: 14.1 us -> 11.5 us  [shift(): return lax.ppermute(value, BOTH, pairs)]
    pallas_call x3 -> x5, Pallas kernels: 10.1 us -> 11.3 us  [the longest x1 4.01 us: near(): pl.pallas_call(near_body, in_specs=[SMEM] + [VMEM] * 3, out_specs=[VMEM]...]
    ppermute x2 -> x4, starting transfers between devices: 7.56 us -> 7.97 us  [the longest x2 5.4 us: shift_around(): lax.ppermute(value, BOTH, [(i, (i + by) % count) for i in range(count)])]
  transfers between devices with their start and end apart: 10 -> 10, of which waited for: 6 -> 6; matrix products, arithmetic and copies ran while one was open for 0% -> 0% of each run, Pallas kernels for 27% -> 29%
where the time goes in v5:
time: 62.1 us; the launch traced here: 61.7 us
  waiting for transfers between devices  24.4 us (39%)
  Pallas kernels  20.5 us (33%)
  starting transfers between devices  16.5 us (27%)
    ppermute x3, waiting for transfers between devices, shift(): return lax.ppermute(value, BOTH, pairs)  11.5 us
    ppermute x1, waiting for transfers between devices, gather_sub(): lax.ppermute(value, 'sub', [(i, (i + step) % count) for i in range(count)])  8.96 us
    ppermute x2, starting transfers between devices, shift_around(): lax.ppermute(value, BOTH, [(i, (i + by) % count) for i in range(count)])  5.4 us
    ppermute x3, starting transfers between devices, shift(): return lax.ppermute(value, BOTH, pairs)  4.7 us
    pallas_call x1, Pallas kernels, near(): pl.pallas_call(near_body, in_specs=[SMEM] + [VMEM] * 3, out_specs=[VMEM]...  4.01 us
    ppermute x3, starting transfers between devices, gather_col(): value = join(value, lax.ppermute(value, 'col', pairs))  3.83 us
    pallas_call x1, Pallas kernels, far(): call(far_body, [SMEM] * 2 + [HBM] + [VMEM] * 3, [(own.shape, jnp.float32)...  3.46 us
    pallas_call x1, Pallas kernels, load(): pl.pallas_call(load_body, in_specs=[HBM], out_specs=VMEM, out_shape=pltpu...  3.39 us
  transfers between devices with their start and end apart: 10, of which 6 were waited for; matrix products, arithmetic and copies ran while one was open for 0% of the time, Pallas kernels for 29%

profile of v5, /device:TPU:31, one launch (start us, length us, event | category | flops | bytes accessed | tf_op | source)
XLA Modules:
  0.0 61.7 jit_solution(3943149373432710556)
XLA Ops:
  0.0 2.1 %collective-permute-start = (bf16[4096,128]{1,0:T(8,128)(2,1)}, bf16[4096,128]{1,0:T(8,128)(2,1)S(1)}, u32[]{:S(2)}, u32[]{:S(2)}) collective-permute-start(bf16[4096,128]{1,0:T(8,128)(2,1)} %refs_0_.1), channel_id=1, source_target_pairs={{1,0},{2,1},{3,2},{4,3},{5,4},{6,5},{7,6},{8,7},{9,8},{10,9},{11,1... | collective-permute-start | bytes 3145736 | tf_op jit(solution)/shard_map/ppermute | solution.py:36
  2.1 2.6 %leaf_and_cluster_coefs.1 = (bf16[4096,128]{1,0:T(8,128)(2,1)S(1)}, bf16[16,32,256]{2,1,0:T(8,128)(2,1)S(1)}, f32[16,32,32]{2,1,0:T(8,128)S(1)}, f32[1,32,32]{2,...) custom-call(bf16[4096,128]{1,0:T(8,128)(2,1)} %refs_0_.1, ...), custom_call_target="tpu_custom_call" | custom-call | tf_op jit(solution)/shard_map/leaf_and_cluster_coefs/pallas_call | solution.py:103
  4.8 0.2 collective-permute-start.3
  5.0 5.2 %collective-permute-start.2 = (f16[608,128]{1,0:T(8,128)(2,1)S(1)}, f16[608,128]{1,0:T(8,128)(2,1)S(1)}, u32[]{:S(2)}, u32[]{:S(2)}) collective-permute-start(f16[608,128]{1,0:T(8,128)(2,1)S(1)} %convert_element_type.21), channel_id=1, source_target_pairs={{0,1},{1,2},{2,3},{3,4},{4,5},{5,6},{6,7},{7,8},{8,9},{9,10},{10,1... | collective-permute-start | bytes 466952 | tf_op jit(solution)/shard_map/ppermute | solution.py:41
  10.2 0.0 collective-permute-start.1
  10.2 0.0 copy-start
  10.2 1.3 %collective-permute-start.5 = (bf16[2064,128]{1,0:T(8,128)(2,1)S(1)}, bf16[2064,128]{1,0:T(8,128)(2,1)S(1)}, u32[]{:S(2)}, u32[]{:S(2)}) collective-permute-start(bf16[2064,128]{1,0:T(8,128)(2,1)S(1)} %get-tuple-element.41), channel_id=1, source_target_pairs={{0,1},{1,2},{2,3},{3,4},{4,5},{5,6},{6,7},{7,8},{8,9},{9,10},{10,1... | collective-permute-start | bytes 1585160 | tf_op jit(solution)/shard_map/ppermute | solution.py:36
  11.5 3.4 %load_near_blocks.1.blocks_ref = bf16[16,4,256,256]{3,2,1,0:T(8,128)(2,1)S(1)} custom-call(bf16[16,4,256,256]{3,2,1,0:T(8,128)(2,1)} %blocks_ref), custom_call_target="tpu_custom_call" | custom-call | tf_op jit(solution)/shard_map/load_near_blocks/pallas_call | solution.py:259
  14.9 9.3 %collective-permute-done.high_ref = bf16[4096,128]{1,0:T(8,128)(2,1)S(1)} collective-permute-done((bf16[4096,128]{1,0:T(8,128)(2,1)}, bf16[4096,128]{1,0:T(8,128)(2,1)S(1)}, u32[]{:S(2)}, u32[]{:S(2)}) %collective-permute-start) | collective-permute-done | bytes 1048608 | tf_op jit(solution)/shard_map/ppermute | solution.py:36
  24.2 0.0 copy-done
  24.2 4.0 %near_own_and_high.1 = (f32[4096,128]{1,0:T(8,128)S(1)}, s32[144,128]{1,0:T(8,128)S(1)}, s32[8,128]{1,0:T(8,128)S(1)}) custom-call(s32[4,16]{1,0:T(4,128)S(1)} %bitcast.2, bf16[16,4,256,256]{3,2,1,0:T(8,128)(2,1)S(1)} %load_near_blocks.1.blocks_ref, bf16[4096,128]{1,0:T(8,128)(2,1)S(1)} %get-tuple-element.34.own_ref, ...), custom_call_target="tpu_custom_call" | custom-call | tf_op jit(solution)/shard_map/near_own_and_high/pallas_call | solution.py:329
  28.2 0.0 copy-start.1
  28.2 9.0 %collective-permute-done.1 = f16[80,128]{1,0:T(8,128)(2,1)S(1)} collective-permute-done((f16[80,128]{1,0:T(8,128)(2,1)S(1)}, f16[80,128]{1,0:T(8,128)(2,1)S(1)}, u32[]{:S(2)}, u32[]{:S(2)}) %collective-permute-start.1) | collective-permute-done | bytes 20512 | tf_op jit(solution)/shard_map/ppermute | solution.py:174
  37.2 0.0 collective-permute-done.3
  37.2 0.0 collective-permute-done.2
  37.2 1.3 %collective-permute-start.4 = (bf16[2048,128]{1,0:T(8,128)(2,1)S(1)}, bf16[2048,128]{1,0:T(8,128)(2,1)S(1)}, u32[]{:S(2)}, u32[]{:S(2)}) collective-permute-start(bf16[2048,128]{1,0:T(8,128)(2,1)S(1)} %get-tuple-element.40), channel_id=1, source_target_pairs={{0,1},{1,2},{2,3},{3,4},{4,5},{5,6},{6,7},{7,8},{8,9},{9,10},{10,1... | collective-permute-start | bytes 1572872 | tf_op jit(solution)/shard_map/ppermute | solution.py:36
  38.6 2.6 %collective-permute-start.6 = (f16[80,128]{1,0:T(8,128)(2,1)S(1)}, f16[80,128]{1,0:T(8,128)(2,1)S(1)}, u32[]{:S(2)}, u32[]{:S(2)}) collective-permute-start(f16[80,128]{1,0:T(8,128)(2,1)S(1)} %convert_element_type.26), channel_id=1, source_target_pairs={{0,28},{3,7},{4,0},{7,11},{8,4},{11,15},{12,8},{15,19},{16,12},{19... | collective-permute-start | bytes 61448 | tf_op jit(solution)/shard_map/ppermute | solution.py:193
  41.2 1.1 %collective-permute-done.6 = f16[80,128]{1,0:T(8,128)(2,1)S(1)} collective-permute-done((f16[80,128]{1,0:T(8,128)(2,1)S(1)}, f16[80,128]{1,0:T(8,128)(2,1)S(1)}, u32[]{:S(2)}, u32[]{:S(2)}) %collective-permute-start.6) | collective-permute-done | bytes 20512 | tf_op jit(solution)/shard_map/ppermute | solution.py:193
  42.2 0.0 copy-start.2
  42.2 0.0 copy-start.3
  42.3 2.6 %collective-permute-start.7 = (f32[1,32,128]{2,1,0:T(8,128)S(1)}, f32[1,32,128]{2,1,0:T(8,128)S(1)}, u32[]{:S(2)}, u32[]{:S(2)}) collective-permute-start(f32[1,32,128]{2,1,0:T(8,128)S(1)} %get-tuple-element.47.first_ref), channel_id=1, source_target_pairs={{0,4},{4,0},{8,12},{12,8},{16,20},{20,16},{24,28},{28,24},{1,5},{5... | collective-permute-start | bytes 49160 | tf_op jit(solution)/shard_map/ppermute | solution.py:203
  44.9 0.8 %collective-permute-done.7.second_ref = f32[1,32,128]{2,1,0:T(8,128)S(1)} collective-permute-done((f32[1,32,128]{2,1,0:T(8,128)S(1)}, f32[1,32,128]{2,1,0:T(8,128)S(1)}, u32[]{:S(2)}, u32[]{:S(2)}) %collective-permute-start.7) | collective-permute-done | bytes 16416 | tf_op jit(solution)/shard_map/ppermute | solution.py:203
  45.7 1.0 %collective-permute-start.8 = (f32[2,32,128]{2,1,0:T(8,128)S(1)}, f32[2,32,128]{2,1,0:T(8,128)S(1)}, u32[]{:S(2)}, u32[]{:S(2)}) collective-permute-start(f32[2,32,128]{2,1,0:T(8,128)S(1)} %join_cols.3.first_ref), channel_id=1, source_target_pairs={{0,8},{4,12},{8,0},{12,4},{16,24},{20,28},{24,16},{28,20},{1,9},{5... | collective-permute-start | bytes 98312 | tf_op jit(solution)/shard_map/ppermute | solution.py:203
  46.8 2.0 %collective-permute-done.8.second_ref = f32[2,32,128]{2,1,0:T(8,128)S(1)} collective-permute-done((f32[2,32,128]{2,1,0:T(8,128)S(1)}, f32[2,32,128]{2,1,0:T(8,128)S(1)}, u32[]{:S(2)}, u32[]{:S(2)}) %collective-permute-start.8) | collective-permute-done | bytes 32800 | tf_op jit(solution)/shard_map/ppermute | solution.py:203
  48.8 0.2 collective-permute-start.9
  49.0 0.0 copy-done.1
  49.0 3.5 %far_field_of_leaves.1.field_ref = f32[512,128]{1,0:T(8,128)S(1)} custom-call(s32[8,16]{1,0:T(8,128)S(1)} %bitcast.4, s32[4,16]{1,0:T(4,128)S(1)} %bitcast.3, f32[16,8,32,32]{3,2,1,0:T(8,128)} %coupling_in.1, f32[608,128]{1,0:T(8,128)S(1)} %convert_element_type.23.low_ref, f32[512,128]{1,0:T(8,128)S(1)} %get-tuple-element.52.own_ref, ...), custom_call_target="tpu_custom_call" | custom-call | tf_op jit(solution)/shard_map/far_field_of_leaves/pallas_call | solution.py:239
  52.5 0.0 collective-permute-done.9.second_ref
  52.5 0.0 copy-done.2
  52.5 0.0 copy-done.3
  52.5 3.0 %fields_down.1 = (f32[4096,128]{1,0:T(8,128)S(1)}, bf16[4096,128]{1,0:T(8,128)(2,1)}) custom-call(s32[1,4]{1,0:T(1,128)S(1)} %copy-done.2, s32[1,8]{1,0:T(1,128)S(1)} %copy-done.3, f32[4,32,128]{2,1,0:T(8,128)S(1)} %get-tuple-element.46.stack_ref, f32[8,32,128]{2,1,0:T(8,128)S(1)} %join_cols.5.cols_ref, f32[1,4,32,32]{3,2,1,0:T(8,128)S(1)} %get-tuple-element.48.coupling_ref, ...), custom_call_target="tpu_custom_call" | custom-call | tf_op jit(solution)/shard_map/fields_down/pallas_call | solution.py:380
  55.6 0.0 collective-permute-done.5.low_ref
  55.6 1.4 %near_low_first.1.acc_ref = f32[4096,128]{1,0:T(8,128)S(1)} custom-call(s32[144,128]{1,0:T(8,128)S(1)} %get-tuple-element.35.list_ref, s32[8,128]{1,0:T(8,128)S(1)} %get-tuple-element.36.found_ref, bf16[16,4,256,256]{3,2,1,0:T(8,128)(2,1)S(1)} %load_near_blocks.1.blocks_ref, ...), custom_call_target="tpu_custom_call", output_to_operand_aliasing={{}: (4, {})} | custom-call | tf_op jit(solution)/shard_map/near_low_first/pallas_call | solution.py:424
  56.9 2.2 %collective-permute-done.4.low_ref = bf16[2048,128]{1,0:T(8,128)(2,1)S(1)} collective-permute-done((bf16[2048,128]{1,0:T(8,128)(2,1)S(1)}, bf16[2048,128]{1,0:T(8,128)(2,1)S(1)}, u32[]{:S(2)}, u32[]{:S(2)}) %collective-permute-start.4) | collective-permute-done | bytes 524320 | tf_op jit(solution)/shard_map/ppermute | solution.py:36
  59.2 2.6 %near_low_second.1 = bf16[4096,128]{1,0:T(8,128)(2,1)} custom-call(s32[144,128]{1,0:T(8,128)S(1)} %get-tuple-element.35.list_ref, s32[8,128]{1,0:T(8,128)S(1)} %get-tuple-element.36.found_ref, bf16[16,4,256,256]{3,2,1,0:T(8,128)(2,1)S(1)} %load_near_blocks.1.blocks_ref, ...), custom_call_target="tpu_custom_call", output_to_operand_aliasing={{}: (5, {})} | custom-call | tf_op jit(solution)/shard_map/near_low_second/pallas_call | solution.py:462
  (12 shorter events, 0.2 us)
Async XLA Ops:
  0.0 24.2 %collective-permute-start = (bf16[4096,128]{1,0:T(8,128)(2,1)}, bf16[4096,128]{1,0:T(8,128)(2,1)S(1)}, u32[]{:S(2)}, u32[]{:S(2)}) collective-permute-start(bf16[4096,128]{1,0:T(8,128)(2,1)} %refs_0_.1), channel_id=1, source_target_pairs={{1,0},{2,1},{3,2},{4,3},{5,4},{6,5},{7,6},{8,7},{9,8},{10,9},{11,1... | collective-permute-start | bytes 3145736 | tf_op jit(solution)/shard_map/ppermute | solution.py:36
  4.8 32.4 %collective-permute-start.3 = (f16[608,128]{1,0:T(8,128)(2,1)S(1)}, f16[608,128]{1,0:T(8,128)(2,1)S(1)}, u32[]{:S(2)}, u32[]{:S(2)}) collective-permute-start(f16[608,128]{1,0:T(8,128)(2,1)S(1)} %convert_element_type.21), channel_id=1, source_target_pairs={{0,31},{1,0},{2,1},{3,2},{4,3},{5,4},{6,5},{7,6},{8,7},{9,8},{10,9... | collective-permute-start | bytes 466952 | tf_op jit(solution)/shard_map/ppermute | solution.py:41
  5.0 32.2 %collective-permute-start.2 = (f16[608,128]{1,0:T(8,128)(2,1)S(1)}, f16[608,128]{1,0:T(8,128)(2,1)S(1)}, u32[]{:S(2)}, u32[]{:S(2)}) collective-permute-start(f16[608,128]{1,0:T(8,128)(2,1)S(1)} %convert_element_type.21), channel_id=1, source_target_pairs={{0,1},{1,2},{2,3},{3,4},{4,5},{5,6},{6,7},{7,8},{8,9},{9,10},{10,1... | collective-permute-start | bytes 466952 | tf_op jit(solution)/shard_map/ppermute | solution.py:41
  10.2 27.0 %collective-permute-start.1 = (f16[80,128]{1,0:T(8,128)(2,1)S(1)}, f16[80,128]{1,0:T(8,128)(2,1)S(1)}, u32[]{:S(2)}, u32[]{:S(2)}) collective-permute-start(f16[80,128]{1,0:T(8,128)(2,1)S(1)} %convert_element_type.22), channel_id=1, source_target_pairs={{0,2},{1,3},{2,0},{3,1},{4,6},{5,7},{6,4},{7,5},{8,10},{9,11},{10,... | collective-permute-start | bytes 61448 | tf_op jit(solution)/shard_map/ppermute | solution.py:174
  10.2 14.0 %copy-start = (s32[16,4]{0,1:T(4,128)S(1)}, s32[16,4]{0,1:T(4,128)}, u32[]{:S(2)}) copy-start(s32[16,4]{0,1:T(4,128)} %param.14) | copy-start | bytes 772
  10.2 45.4 %collective-permute-start.5 = (bf16[2064,128]{1,0:T(8,128)(2,1)S(1)}, bf16[2064,128]{1,0:T(8,128)(2,1)S(1)}, u32[]{:S(2)}, u32[]{:S(2)}) collective-permute-start(bf16[2064,128]{1,0:T(8,128)(2,1)S(1)} %get-tuple-element.41), channel_id=1, source_target_pairs={{0,1},{1,2},{2,3},{3,4},{4,5},{5,6},{6,7},{7,8},{8,9},{9,10},{10,1... | collective-permute-start | bytes 1585160 | tf_op jit(solution)/shard_map/ppermute | solution.py:36
  28.2 20.8 %copy-start.1 = (s32[16,8]{0,1:T(8,128)S(1)}, s32[16,8]{0,1:T(8,128)}, u32[]{:S(2)}) copy-start(s32[16,8]{0,1:T(8,128)} %param.18) | copy-start | bytes 1540
  37.2 22.0 %collective-permute-start.4 = (bf16[2048,128]{1,0:T(8,128)(2,1)S(1)}, bf16[2048,128]{1,0:T(8,128)(2,1)S(1)}, u32[]{:S(2)}, u32[]{:S(2)}) collective-permute-start(bf16[2048,128]{1,0:T(8,128)(2,1)S(1)} %get-tuple-element.40), channel_id=1, source_target_pairs={{0,1},{1,2},{2,3},{3,4},{4,5},{5,6},{6,7},{7,8},{8,9},{9,10},{10,1... | collective-permute-start | bytes 1572872 | tf_op jit(solution)/shard_map/ppermute | solution.py:36
  38.6 3.7 %collective-permute-start.6 = (f16[80,128]{1,0:T(8,128)(2,1)S(1)}, f16[80,128]{1,0:T(8,128)(2,1)S(1)}, u32[]{:S(2)}, u32[]{:S(2)}) collective-permute-start(f16[80,128]{1,0:T(8,128)(2,1)S(1)} %convert_element_type.26), channel_id=1, source_target_pairs={{0,28},{3,7},{4,0},{7,11},{8,4},{11,15},{12,8},{15,19},{16,12},{19... | collective-permute-start | bytes 61448 | tf_op jit(solution)/shard_map/ppermute | solution.py:193
  42.2 10.3 %copy-start.2 = (s32[1,4]{1,0:T(1,128)S(1)}, s32[1,4]{1,0:T(1,128)}, u32[]{:S(2)}) copy-start(s32[1,4]{1,0:T(1,128)} %partner_ref.1) | copy-start | bytes 52
  42.2 10.3 %copy-start.3 = (s32[1,8]{1,0:T(1,128)S(1)}, s32[1,8]{1,0:T(1,128)}, u32[]{:S(2)}) copy-start(s32[1,8]{1,0:T(1,128)} %top_partner_ref.1) | copy-start | bytes 100
  42.3 3.4 %collective-permute-start.7 = (f32[1,32,128]{2,1,0:T(8,128)S(1)}, f32[1,32,128]{2,1,0:T(8,128)S(1)}, u32[]{:S(2)}, u32[]{:S(2)}) collective-permute-start(f32[1,32,128]{2,1,0:T(8,128)S(1)} %get-tuple-element.47.first_ref), channel_id=1, source_target_pairs={{0,4},{4,0},{8,12},{12,8},{16,20},{20,16},{24,28},{28,24},{1,5},{5... | collective-permute-start | bytes 49160 | tf_op jit(solution)/shard_map/ppermute | solution.py:203
  45.7 3.1 %collective-permute-start.8 = (f32[2,32,128]{2,1,0:T(8,128)S(1)}, f32[2,32,128]{2,1,0:T(8,128)S(1)}, u32[]{:S(2)}, u32[]{:S(2)}) collective-permute-start(f32[2,32,128]{2,1,0:T(8,128)S(1)} %join_cols.3.first_ref), channel_id=1, source_target_pairs={{0,8},{4,12},{8,0},{12,4},{16,24},{20,28},{24,16},{28,20},{1,9},{5... | collective-permute-start | bytes 98312 | tf_op jit(solution)/shard_map/ppermute | solution.py:203
  48.8 3.7 %collective-permute-start.9 = (f32[4,32,128]{2,1,0:T(8,128)S(1)}, f32[4,32,128]{2,1,0:T(8,128)S(1)}, u32[]{:S(2)}, u32[]{:S(2)}) collective-permute-start(f32[4,32,128]{2,1,0:T(8,128)S(1)} %join_cols.4.first_ref), channel_id=1, source_target_pairs={{0,16},{4,20},{8,24},{12,28},{16,0},{20,4},{24,8},{28,12},{1,17},{... | collective-permute-start | bytes 196616 | tf_op jit(solution)/shard_map/ppermute | solution.py:203

commit v6 on v5

--- a/solution.py
+++ b/solution.py
@@ -10,6 +10,7 @@
 HIGHEST = lax.Precision.HIGHEST
 BOTH = ("col", "sub")
 SPARE = 16
+TAIL = 8
 GROUP = 4
 BATCH = 8
 VMEM = pl.BlockSpec(memory_space=pltpu.VMEM)
@@ -46,10 +47,22 @@
     return lax.dot_general(a, b, dims, precision=HIGHEST, preferred_element_type=jnp.float32)
 
 
-def scale(value):
-    most = jnp.max(jnp.abs(value), axis=(0, 1), keepdims=True)
-    power = jnp.floor(jnp.log2(jnp.maximum(most, 1e-30)))
-    return value * jnp.exp2(14.0 - power), power
+def pack(ref, parts):
+    at = 0
+    row = lax.broadcasted_iota(jnp.int32, (TAIL, ref.shape[1]), 0)
+    powers = jnp.zeros(row.shape, jnp.float32)
+    for i, part in enumerate(parts):
+        most = jnp.max(jnp.abs(part), axis=(0, 1), keepdims=True)
+        power = jnp.floor(jnp.log2(jnp.maximum(most, 1e-30)))
+        ref[at : at + part.shape[0], :] = part * jnp.exp2(14.0 - power)
+        powers = jnp.where(row == i, power, powers)
+        at += part.shape[0]
+    ref[at:, :] = powers
+
+
+def unpack(ref, at, length, i):
+    row = ref.shape[0] - TAIL + i
+    return ref[at : at + length, :] * jnp.exp2(ref[row : row + 1, :] - 14.0)
 
 
 def in_hbm(value):
@@ -80,18 +93,11 @@
     top = exact(cluster_ref[0], low, (0, 0))
     pair_ref[0] = low
     pair_ref[1] = top
-    half = (SPARE // 2, columns)
-    low, low_power = scale(low)
-    top, top_power = scale(top)
-    short_ref[:rank, :] = low
-    short_ref[rank : 2 * rank, :] = top
-    short_ref[2 * rank : 2 * rank + SPARE // 2, :] = jnp.broadcast_to(low_power, half)
-    short_ref[2 * rank + SPARE // 2 :, :] = jnp.broadcast_to(top_power, half)
-    whole, power = scale(whole)
-    length = leaves * rank
-    long_ref[:length, :] = whole
-    long_ref[length : length + SPARE, :] = jnp.broadcast_to(power, (SPARE, columns))
-    long_ref[length + SPARE :, :] = short_ref[...]
+    matrix = cluster_ref[0]
+    height = rank * rank // columns
+    wide = jnp.concatenate([matrix[i : i + height, :] for i in range(0, rank, height)], axis=1)
+    pack(long_ref, (whole, low, wide))
+    short_ref[...] = long_ref[leaves * rank :, :]
 
 
 def upward(vectors, basis, transfer, cluster_transfer, cluster_coupling, top_coupling):
@@ -99,7 +105,7 @@
     points, columns = vectors.shape
     f32 = jnp.float32
     arrays = (vectors, basis, transfer, cluster_transfer, cluster_coupling, top_coupling)
-    short = 2 * rank + SPARE
+    short = rank + rank * rank // columns + TAIL
     return call(
         upward_body,
         [HBM] * 6,
@@ -108,7 +114,7 @@
             ((points // 2 + SPARE, columns), vectors.dtype),
             ((points // 2, columns), vectors.dtype),
             ((leaves * rank, columns), f32),
-            ((leaves * rank + SPARE + short, columns), f32),
+            ((leaves * rank + short, columns), f32),
             ((short, columns), f32),
             ((2, rank, columns), f32),
         ],
@@ -121,20 +127,23 @@
     part_refs, (stack_ref, top_ref) = refs[:-2], refs[-2:]
     rank = own_ref.shape[1]
     sub = lax.axis_index("sub")
-    tops = [own_ref[1]]
+    matrices, lows = [], []
+
+    columns = own_ref.shape[2]
+    height = rank * rank // columns
 
     def put(valid, place, ref):
-        at = ref.shape[0] - 2 * rank - SPARE
-        values = []
-        for i in range(2):
-            power = ref[at + 2 * rank + i * SPARE // 2 : at + 2 * rank + i * SPARE // 2 + 1, :]
-            values.append(ref[at + i * rank : at + (i + 1) * rank, :] * jnp.exp2(power - 14.0))
+        at = ref.shape[0] - rank - height - TAIL
+        low = unpack(ref, at, rank, 1)
+        wide = unpack(ref, at + rank, height, 2)
+        matrix = jnp.concatenate([wide[:, i : i + rank] for i in range(0, columns, rank)], axis=0)
 
         @pl.when(valid)
         def _():
-            stack_ref[place] = values[0]
-
-        tops.append(jnp.where(valid, values[1], 0.0))
+            stack_ref[place] = low
+
+        matrices.append(matrix)
+        lows.append(jnp.where(valid, low, 0.0))
 
     stack_ref[sub] = own_ref[0]
     put(sub > 0, sub - 1, low_ref)
@@ -143,7 +152,7 @@
         put(sub >= 0, lax.rem(sub - 2 - i + subs, subs), ref)
     if part_refs:
         put((sub == 0) | (sub == subs - 1), subs - 1 - sub, part_refs[-1])
-    top_ref[0] = functools.reduce(jnp.add, tops)
+    top_ref[0] = own_ref[1] + exact(jnp.concatenate(matrices, axis=0), jnp.concatenate(lows, axis=0), (0, 0))
 
 
 def cluster_sums(own, low, high, parts):
@@ -205,7 +214,12 @@
     return value
 
 
-def far_body(far_ref, near_ref, coupling_in, low_ref, own_ref, high_ref, field_ref, coupling_ref, window, sems):
+def split(value):
+    head = value.astype(jnp.bfloat16)
+    return head, (value - head.astype(jnp.float32)).astype(jnp.bfloat16)
+
+
+def far_body(far_ref, near_ref, coupling_in, low_ref, own_ref, high_ref, field_ref, coupling_ref, heads, rests, sems):
     leaves, slots, rank, _ = coupling_ref.shape
     rows = leaves * rank
 
@@ -218,9 +232,9 @@
 
     first = near_ref[0, 0] - leaves
     for place, ref in ((0, low_ref), (2, high_ref)):
-        scale = jnp.exp2(ref[rows : rows + 1, :] - 14.0)
-        window[place * rows : (place + 1) * rows, :] = ref[:rows, :] * scale
-    window[rows : 2 * rows, :] = own_ref[...]
+        here = slice(place * rows, (place + 1) * rows)
+        heads[here, :], rests[here, :] = split(unpack(ref, 0, rows, 0))
+    heads[rows : 2 * rows, :], rests[rows : 2 * rows, :] = split(own_ref[...])
 
     for leaf in range(leaves):
         copy(leaf).wait()
@@ -228,10 +242,16 @@
         picked = []
         for k in range(slots):
             place = jnp.clip(far_ref[k, leaf] - first, 0, 3 * leaves - 1)
-            picked.append(window[pl.ds(pl.multiple_of(place * rank, rank), rank), :])
+            picked.append(pl.ds(pl.multiple_of(place * rank, rank), rank))
+        head = jnp.concatenate([heads[at, :] for at in picked], axis=0)
+        rest = jnp.concatenate([rests[at, :] for at in picked], axis=0)
         here = coupling_ref[leaf]
-        wide = jnp.concatenate([here[k] for k in range(slots)], axis=1)
-        field_ref[leaf * rank : (leaf + 1) * rank, :] = exact(wide, jnp.concatenate(picked, axis=0))
+        wide_head, wide_rest = split(jnp.concatenate([here[k] for k in range(slots)], axis=1))
+        both = jnp.dot(
+            jnp.concatenate([wide_head, wide_rest], axis=0), head, preferred_element_type=jnp.float32
+        )
+        last = jnp.dot(wide_head, rest, preferred_element_type=jnp.float32)
+        field_ref[leaf * rank : (leaf + 1) * rank, :] = both[:rank] + (both[rank:] + last)
 
 
 def far(leaf_far, near_index, coupling, low, own, high):
@@ -242,7 +262,8 @@
         [(own.shape, jnp.float32)],
         scratch=[
             pltpu.VMEM(coupling.shape, coupling.dtype),
-            pltpu.VMEM((3 * leaves * rank, own.shape[1]), jnp.float32),
+            pltpu.VMEM((3 * leaves * rank, own.shape[1]), jnp.bfloat16),
+            pltpu.VMEM((3 * leaves * rank, own.shape[1]), jnp.bfloat16),
             pltpu.SemaphoreType.DMA((leaves,)),
         ],
         name="far_field_of_leaves",
@@ -299,8 +320,8 @@
 
                 one = valid.astype(jnp.int32)
                 after.append(counts[i] + one)
-                found = found + jnp.where(lane == leaf, one, 0)
             counts = tuple(after)
+            found = found + jnp.where((lane == leaf) & (place < half), 1, 0)
         return found, counts
 
     found, counts = lax.fori_loop(
@@ -346,33 +367,31 @@
 
 def down_body(
     straight, partner_ref, top_partner_ref, stack_ref, cols_ref, coupling_ref, top_coupling_ref, cluster_ref,
-    transfer_ref, field_ref, basis_ref, acc_ref, sum_ref, out_ref, fields, held, sem,
+    transfer_ref, field_ref, basis_ref, acc_ref, sum_ref, fields,
 ):
     leaves, rank, rows = basis_ref.shape
     col = lax.axis_index("col")
-    top = None
-    for k in range(top_coupling_ref.shape[1]):
+    slots = top_coupling_ref.shape[1]
+    picked = []
+    for k in range(slots):
         place = top_partner_ref[0, k]
-        place = place if straight else lax.bitwise_xor(place, col)
-        term = exact(top_coupling_ref[0, k], cols_ref[place])
-        top = term if top is None else top + term
-    cluster = exact(cluster_ref[0], top)
-    for k in range(coupling_ref.shape[1]):
-        cluster = cluster + exact(coupling_ref[0, k], stack_ref[partner_ref[0, k]])
+        picked.append(cols_ref[place if straight else lax.bitwise_xor(place, col)])
+    wide = jnp.concatenate([top_coupling_ref[0, k] for k in range(slots)], axis=1)
+    top = exact(wide, jnp.concatenate(picked, axis=0))
+    slots = coupling_ref.shape[1]
+    picked = [stack_ref[partner_ref[0, k]] for k in range(slots)] + [top]
+    wide = jnp.concatenate([coupling_ref[0, k] for k in range(slots)] + [cluster_ref[0]], axis=1)
+    cluster = exact(wide, jnp.concatenate(picked, axis=0))
     transfer = transfer_ref[...].reshape(leaves * rank, rank)
     fields[...] = (field_ref[...] + exact(transfer, cluster)).astype(fields.dtype)
     for leaf in range(leaves):
         here = slice(leaf * rows, (leaf + 1) * rows)
-        total = acc_ref[here, :] + lax.dot_general(
+        sum_ref[here, :] = acc_ref[here, :] + lax.dot_general(
             basis_ref[leaf],
             fields[leaf * rank : (leaf + 1) * rank, :],
             (((0,), (0,)), ((), ())),
             preferred_element_type=jnp.float32,
         )
-        sum_ref[here, :] = total
-        held[here, :] = total.astype(held.dtype)
-        pltpu.make_async_copy(held.at[here, :], out_ref.at[here, :], sem).start()
-    pltpu.make_async_copy(held, out_ref, sem).wait()
 
 
 def down(partner, top_partner, stack, cols, coupling, top_coupling, cluster_transfer, transfer, field, basis, acc):
@@ -380,13 +399,9 @@
     return pl.pallas_call(
         functools.partial(down_body, bool(count & (count - 1))),
         in_specs=[SMEM] * 2 + [VMEM] * 9,
-        out_specs=[VMEM, HBM],
-        out_shape=[jax.ShapeDtypeStruct(acc.shape, jnp.float32), pltpu.HBM(acc.shape, jnp.bfloat16)],
-        scratch_shapes=[
-            pltpu.VMEM(field.shape, jnp.bfloat16),
-            pltpu.VMEM(acc.shape, jnp.bfloat16),
-            pltpu.SemaphoreType.DMA,
-        ],
+        out_specs=VMEM,
+        out_shape=pltpu.VMEM(acc.shape, jnp.float32),
+        scratch_shapes=[pltpu.VMEM(field.shape, jnp.bfloat16)],
         compiler_params=pltpu.CompilerParams(vmem_limit_bytes=16 * 2**20),
         cost_estimate=pl.CostEstimate(flops=0, bytes_accessed=0, transcendentals=0),
         name="fields_down",
@@ -416,17 +431,47 @@
                 acc_ref[pl.ds(start, rows), :] += terms[i]
 
 
-def low_body(list_ref, found_ref, blocks_ref, low_ref, acc_in, acc_ref):
+def write(leaves, chosen, acc_ref, out_ref, held, sems):
+    rows = acc_ref.shape[0] // leaves
+
+    def copy(leaf):
+        here = slice(leaf * rows, (leaf + 1) * rows)
+        return pltpu.make_async_copy(held.at[here, :], out_ref.at[here, :], sems.at[leaf])
+
+    for leaf in range(leaves):
+
+        @pl.when(chosen[leaf])
+        def _(leaf=leaf):
+            here = slice(leaf * rows, (leaf + 1) * rows)
+            held[here, :] = acc_ref[here, :].astype(held.dtype)
+            copy(leaf).start()
+
+    for leaf in range(leaves):
+
+        @pl.when(chosen[leaf])
+        def _(leaf=leaf):
+            copy(leaf).wait()
+
+
+def first_body(list_ref, found_ref, blocks_ref, low_ref, acc_in, acc_ref, out_ref, held, sems):
+    leaves = blocks_ref.shape[0]
+    final = [found_ref[0, leaf] == 0 for leaf in range(leaves)]
     add_listed(list_ref, found_ref, 0, BATCH, blocks_ref, low_ref.at[SPARE:, :], acc_ref)
+    write(leaves, final, acc_ref, out_ref, held, sems)
 
 
 def near_low(places, found, blocks, low, acc):
+    leaves = blocks.shape[0]
     return pl.pallas_call(
-        low_body,
+        first_body,
         in_specs=[VMEM] * 5,
-        out_specs=VMEM,
-        out_shape=jax.ShapeDtypeStruct(acc.shape, acc.dtype),
+        out_specs=[VMEM, HBM],
+        out_shape=[pltpu.VMEM(acc.shape, acc.dtype), pltpu.HBM(acc.shape, low.dtype)],
         input_output_aliases={4: 0},
+        scratch_shapes=[
+            pltpu.VMEM(acc.shape, low.dtype),
+            pltpu.SemaphoreType.DMA((leaves,)),
+        ],
         compiler_params=pltpu.CompilerParams(vmem_limit_bytes=16 * 2**20),
         cost_estimate=pl.CostEstimate(flops=0, bytes_accessed=0, transcendentals=0),
         name="near_low_first",
@@ -434,27 +479,10 @@
 
 
 def last_body(list_ref, found_ref, blocks_ref, low_ref, acc_ref, out_in, out_ref, held, sems):
-    leaves, _, rows, _ = blocks_ref.shape
-    touched = [found_ref[0, leaf] for leaf in range(leaves)]
+    leaves = blocks_ref.shape[0]
+    touched = [found_ref[0, leaf] > 0 for leaf in range(leaves)]
     add_listed(list_ref, found_ref, 1, GROUP, blocks_ref, low_ref, acc_ref)
-
-    def copy(leaf):
-        here = slice(leaf * rows, (leaf + 1) * rows)
-        return pltpu.make_async_copy(held.at[here, :], out_ref.at[here, :], sems.at[leaf])
-
-    for leaf in range(leaves):
-
-        @pl.when(touched[leaf] > 0)
-        def _(leaf=leaf):
-            here = slice(leaf * rows, (leaf + 1) * rows)
-            held[here, :] = acc_ref[here, :].astype(held.dtype)
-            copy(leaf).start()
-
-    for leaf in range(leaves):
-
-        @pl.when(touched[leaf] > 0)
-        def _(leaf=leaf):
-            copy(leaf).wait()
+    write(leaves, touched, acc_ref, out_ref, held, sems)
 
 
 def last(places, found, blocks, low, acc, out):
@@ -469,7 +497,7 @@
             pltpu.VMEM(out.shape, out.dtype),
             pltpu.SemaphoreType.DMA((leaves,)),
         ],
-        compiler_params=pltpu.CompilerParams(vmem_limit_bytes=32 * 2**20),
+        compiler_params=pltpu.CompilerParams(vmem_limit_bytes=16 * 2**20),
         cost_estimate=pl.CostEstimate(flops=0, bytes_accessed=0, transcendentals=0),
         name="near_low_second",
     )(places, found, blocks, low, acc, out)
@@ -514,10 +542,10 @@
     stack, top = cluster_sums(pair, low_part, high_part, parts)
     cols = gather_col(top)
     field = far(leaf_far, near_index, leaf_coupling, low_part, coefs, high_part)
-    acc, out = down(
+    acc = down(
         cluster_partner, top_partner, stack, cols, couple, top_couple, cluster, transfer, field, basis, acc
     )
-    acc = near_low(places, found, blocks, low_first, acc)
+    acc, out = near_low(places, found, blocks, low_first, acc)
     return last(places, found, blocks, low_second, acc, out)
 
 

time: 62.1 us -> 61.1 us (0.984)
  starting transfers between devices: 16.5 us -> 14.2 us
  waiting for transfers between devices: 24.4 us -> 26 us
    ppermute x2, starting transfers between devices: 5.4 us -> 1.52 us  [shift_around(): lax.ppermute(value, BOTH, [(i, (i + by) % count) for i in range(count)])]
    ppermute x1, starting transfers between devices: 0.01 us -> 2.5 us  [gather_sub(): lax.ppermute(value, 'sub', [(i, (i + step) % count) for i in range(count)])]
    ppermute x3, waiting for transfers between devices: 11.5 us -> 13 us  [shift(): return lax.ppermute(value, BOTH, pairs)]
    pallas_call x1, Pallas kernels: 1.36 us -> 2.43 us  [near_low(): pl.pallas_call(first_body, in_specs=[VMEM] * 5, out_specs=[VMEM, HBM], ou...]
    ppermute x1, waiting for transfers between devices: 8.96 us -> 7.92 us  [gather_sub(): lax.ppermute(value, 'sub', [(i, (i + step) % count) for i in range(count)])]
    pallas_call x1, Pallas kernels: 3.02 us -> 2.02 us  [down(): pl.pallas_call(functools.partial(down_body, bool(count & count - 1)), in_...]
    ppermute x1, waiting for transfers between devices: 1.07 us -> 1.85 us  [around(): return lax.ppermute(onward.astype(jnp.float16), BOTH, pairs)]
    ppermute x1, starting transfers between devices: 2.57 us -> 1.92 us  [around(): return lax.ppermute(onward.astype(jnp.float16), BOTH, pairs)]
  transfers between devices with their start and end apart: 10 -> 10, of which waited for: 6 -> 7; matrix products, arithmetic and copies ran while one was open for 0% -> 0% of each run, Pallas kernels for 29% -> 30%
where the time goes in v6:
time: 61.1 us; the launch traced here: 60.9 us
  waiting for transfers between devices  26 us (43%)
  Pallas kernels  20.4 us (33%)
  starting transfers between devices  14.2 us (23%)
    ppermute x3, waiting for transfers between devices, shift(): return lax.ppermute(value, BOTH, pairs)  13 us
    ppermute x1, waiting for transfers between devices, gather_sub(): lax.ppermute(value, 'sub', [(i, (i + step) % count) for i in range(count)])  7.92 us
    ppermute x3, starting transfers between devices, shift(): return lax.ppermute(value, BOTH, pairs)  4.82 us
    pallas_call x1, Pallas kernels, near(): pl.pallas_call(near_body, in_specs=[SMEM] + [VMEM] * 3, out_specs=[VMEM]...  4.07 us
    ppermute x3, starting transfers between devices, gather_col(): value = join(value, lax.ppermute(value, 'col', pairs))  3.4 us
    pallas_call x1, Pallas kernels, load(): pl.pallas_call(load_body, in_specs=[HBM], out_specs=VMEM, out_shape=pltpu...  3.39 us
    ppermute x3, waiting for transfers between devices, gather_col(): value = join(value, lax.ppermute(value, 'col', pairs))  3.26 us
    pallas_call x1, Pallas kernels, far(): call(far_body, [SMEM] * 2 + [HBM] + [VMEM] * 3, [(own.shape, jnp.float32)...  3.09 us
  transfers between devices with their start and end apart: 10, of which 7 were waited for; matrix products, arithmetic and copies ran while one was open for 0% of the time, Pallas kernels for 30%

profile of v6, /device:TPU:31, one launch (start us, length us, event | category | flops | bytes accessed | tf_op | source)
XLA Modules:
  0.0 60.9 jit_solution(13762065876922697026)
XLA Ops:
  0.0 2.1 %collective-permute-start = (bf16[4096,128]{1,0:T(8,128)(2,1)}, bf16[4096,128]{1,0:T(8,128)(2,1)S(1)}, u32[]{:S(2)}, u32[]{:S(2)}) collective-permute-start(bf16[4096,128]{1,0:T(8,128)(2,1)} %refs_0_.1), channel_id=1, source_target_pairs={{1,0},{2,1},{3,2},{4,3},{5,4},{6,5},{7,6},{8,7},{9,8},{10,9},{11,1... | collective-permute-start | bytes 3145736 | tf_op jit(solution)/shard_map/ppermute | solution.py:37
  2.1 2.5 %leaf_and_cluster_coefs.1 = (bf16[4096,128]{1,0:T(8,128)(2,1)S(1)}, bf16[16,32,256]{2,1,0:T(8,128)(2,1)S(1)}, f32[16,32,32]{2,1,0:T(8,128)S(1)}, f32[1,32,32]{2,...) custom-call(bf16[4096,128]{1,0:T(8,128)(2,1)} %refs_0_.1, ...), custom_call_target="tpu_custom_call" | custom-call | tf_op jit(solution)/shard_map/leaf_and_cluster_coefs/pallas_call | solution.py:109
  4.6 0.1 collective-permute-start.2
  4.7 1.5 %collective-permute-start.3 = (f16[560,128]{1,0:T(8,128)(2,1)S(1)}, f16[560,128]{1,0:T(8,128)(2,1)S(1)}, u32[]{:S(2)}, u32[]{:S(2)}) collective-permute-start(f16[560,128]{1,0:T(8,128)(2,1)S(1)} %convert_element_type.21), channel_id=1, source_target_pairs={{0,31},{1,0},{2,1},{3,2},{4,3},{5,4},{6,5},{7,6},{8,7},{9,8},{10,9... | collective-permute-start | bytes 430088 | tf_op jit(solution)/shard_map/ppermute | solution.py:42
  6.2 2.5 %collective-permute-start.1 = (f16[48,128]{1,0:T(8,128)(2,1)S(1)}, f16[48,128]{1,0:T(8,128)(2,1)S(1)}, u32[]{:S(2)}, u32[]{:S(2)}) collective-permute-start(f16[48,128]{1,0:T(8,128)(2,1)S(1)} %convert_element_type.22), channel_id=1, source_target_pairs={{0,2},{1,3},{2,0},{3,1},{4,6},{5,7},{6,4},{7,5},{8,10},{9,11},{10,... | collective-permute-start | bytes 36872 | tf_op jit(solution)/shard_map/ppermute | solution.py:183
  8.7 0.0 copy-start
  8.7 1.4 %collective-permute-start.5 = (bf16[2064,128]{1,0:T(8,128)(2,1)S(1)}, bf16[2064,128]{1,0:T(8,128)(2,1)S(1)}, u32[]{:S(2)}, u32[]{:S(2)}) collective-permute-start(bf16[2064,128]{1,0:T(8,128)(2,1)S(1)} %get-tuple-element.41), channel_id=1, source_target_pairs={{0,1},{1,2},{2,3},{3,4},{4,5},{5,6},{6,7},{7,8},{8,9},{9,10},{10,1... | collective-permute-start | bytes 1585160 | tf_op jit(solution)/shard_map/ppermute | solution.py:37
  10.1 3.4 %load_near_blocks.1.blocks_ref = bf16[16,4,256,256]{3,2,1,0:T(8,128)(2,1)S(1)} custom-call(bf16[16,4,256,256]{3,2,1,0:T(8,128)(2,1)} %blocks_ref), custom_call_target="tpu_custom_call" | custom-call | tf_op jit(solution)/shard_map/load_near_blocks/pallas_call | solution.py:280
  13.5 10.7 %collective-permute-done.high_ref = bf16[4096,128]{1,0:T(8,128)(2,1)S(1)} collective-permute-done((bf16[4096,128]{1,0:T(8,128)(2,1)}, bf16[4096,128]{1,0:T(8,128)(2,1)S(1)}, u32[]{:S(2)}, u32[]{:S(2)}) %collective-permute-start) | collective-permute-done | bytes 1048608 | tf_op jit(solution)/shard_map/ppermute | solution.py:37
  24.2 0.0 copy-done
  24.2 4.1 %near_own_and_high.1 = (f32[4096,128]{1,0:T(8,128)S(1)}, s32[144,128]{1,0:T(8,128)S(1)}, s32[8,128]{1,0:T(8,128)S(1)}) custom-call(s32[4,16]{1,0:T(4,128)S(1)} %bitcast.2, bf16[16,4,256,256]{3,2,1,0:T(8,128)(2,1)S(1)} %load_near_blocks.1.blocks_ref, bf16[4096,128]{1,0:T(8,128)(2,1)S(1)} %get-tuple-element.34.own_ref, ...), custom_call_target="tpu_custom_call" | custom-call | tf_op jit(solution)/shard_map/near_own_and_high/pallas_call | solution.py:350
  28.3 0.0 copy-start.1
  28.3 7.9 %collective-permute-done.1 = f16[48,128]{1,0:T(8,128)(2,1)S(1)} collective-permute-done((f16[48,128]{1,0:T(8,128)(2,1)S(1)}, f16[48,128]{1,0:T(8,128)(2,1)S(1)}, u32[]{:S(2)}, u32[]{:S(2)}) %collective-permute-start.1) | collective-permute-done | bytes 12320 | tf_op jit(solution)/shard_map/ppermute | solution.py:183
  36.2 0.0 collective-permute-done.2
  36.2 0.0 collective-permute-done.3
  36.2 1.3 %collective-permute-start.4 = (bf16[2048,128]{1,0:T(8,128)(2,1)S(1)}, bf16[2048,128]{1,0:T(8,128)(2,1)S(1)}, u32[]{:S(2)}, u32[]{:S(2)}) collective-permute-start(bf16[2048,128]{1,0:T(8,128)(2,1)S(1)} %get-tuple-element.40), channel_id=1, source_target_pairs={{0,1},{1,2},{2,3},{3,4},{4,5},{5,6},{6,7},{7,8},{8,9},{9,10},{10,1... | collective-permute-start | bytes 1572872 | tf_op jit(solution)/shard_map/ppermute | solution.py:37
  37.6 1.9 %collective-permute-start.6 = (f16[48,128]{1,0:T(8,128)(2,1)S(1)}, f16[48,128]{1,0:T(8,128)(2,1)S(1)}, u32[]{:S(2)}, u32[]{:S(2)}) collective-permute-start(f16[48,128]{1,0:T(8,128)(2,1)S(1)} %convert_element_type.26), channel_id=1, source_target_pairs={{0,28},{3,7},{4,0},{7,11},{8,4},{11,15},{12,8},{15,19},{16,12},{19... | collective-permute-start | bytes 36872 | tf_op jit(solution)/shard_map/ppermute | solution.py:202
  39.5 1.8 %collective-permute-done.6 = f16[48,128]{1,0:T(8,128)(2,1)S(1)} collective-permute-done((f16[48,128]{1,0:T(8,128)(2,1)S(1)}, f16[48,128]{1,0:T(8,128)(2,1)S(1)}, u32[]{:S(2)}, u32[]{:S(2)}) %collective-permute-start.6) | collective-permute-done | bytes 12320 | tf_op jit(solution)/shard_map/ppermute | solution.py:202
  41.4 0.0 copy-start.2
  41.4 0.0 copy-start.3
  41.4 0.5 sums_over_sub.1
  41.9 2.5 %collective-permute-start.7 = (f32[1,32,128]{2,1,0:T(8,128)S(1)}, f32[1,32,128]{2,1,0:T(8,128)S(1)}, u32[]{:S(2)}, u32[]{:S(2)}) collective-permute-start(f32[1,32,128]{2,1,0:T(8,128)S(1)} %get-tuple-element.47.first_ref), channel_id=1, source_target_pairs={{0,4},{4,0},{8,12},{12,8},{16,20},{20,16},{24,28},{28,24},{1,5},{5... | collective-permute-start | bytes 49160 | tf_op jit(solution)/shard_map/ppermute | solution.py:212
  44.4 0.8 %collective-permute-done.7.second_ref = f32[1,32,128]{2,1,0:T(8,128)S(1)} collective-permute-done((f32[1,32,128]{2,1,0:T(8,128)S(1)}, f32[1,32,128]{2,1,0:T(8,128)S(1)}, u32[]{:S(2)}, u32[]{:S(2)}) %collective-permute-start.7) | collective-permute-done | bytes 16416 | tf_op jit(solution)/shard_map/ppermute | solution.py:212
  45.2 0.7 %collective-permute-start.8 = (f32[2,32,128]{2,1,0:T(8,128)S(1)}, f32[2,32,128]{2,1,0:T(8,128)S(1)}, u32[]{:S(2)}, u32[]{:S(2)}) collective-permute-start(f32[2,32,128]{2,1,0:T(8,128)S(1)} %join_cols.3.first_ref), channel_id=1, source_target_pairs={{0,8},{4,12},{8,0},{12,4},{16,24},{20,28},{24,16},{28,20},{1,9},{5... | collective-permute-start | bytes 98312 | tf_op jit(solution)/shard_map/ppermute | solution.py:212
  46.0 2.3 %collective-permute-done.8.second_ref = f32[2,32,128]{2,1,0:T(8,128)S(1)} collective-permute-done((f32[2,32,128]{2,1,0:T(8,128)S(1)}, f32[2,32,128]{2,1,0:T(8,128)S(1)}, u32[]{:S(2)}, u32[]{:S(2)}) %collective-permute-start.8) | collective-permute-done | bytes 32800 | tf_op jit(solution)/shard_map/ppermute | solution.py:212
  48.3 0.2 collective-permute-start.9
  48.5 0.0 copy-done.1
  48.5 3.1 %far_field_of_leaves.1.field_ref = f32[512,128]{1,0:T(8,128)S(1)} custom-call(s32[8,16]{1,0:T(8,128)S(1)} %bitcast.4, s32[4,16]{1,0:T(4,128)S(1)} %bitcast.3, f32[16,8,32,32]{3,2,1,0:T(8,128)} %coupling_in.1, f32[560,128]{1,0:T(8,128)S(1)} %convert_element_type.23.low_ref, f32[512,128]{1,0:T(8,128)S(1)} %get-tuple-element.52.own_ref, ...), custom_call_target="tpu_custom_call" | custom-call | tf_op jit(solution)/shard_map/far_field_of_leaves/pallas_call | solution.py:259
  51.6 0.1 collective-permute-done.9.second_ref
  51.7 0.0 copy-done.2
  51.7 0.0 copy-done.3
  51.7 2.0 %fields_down.1.acc_in = f32[4096,128]{1,0:T(8,128)S(1)} custom-call(s32[1,4]{1,0:T(1,128)S(1)} %copy-done.2, s32[1,8]{1,0:T(1,128)S(1)} %copy-done.3, f32[4,32,128]{2,1,0:T(8,128)S(1)} %get-tuple-element.46.stack_ref, f32[8,32,128]{2,1,0:T(8,128)S(1)} %join_cols.5.cols_ref, f32[1,4,32,32]{3,2,1,0:T(8,128)S(1)} %get-tuple-element.48.coupling_ref, ...), custom_call_target="tpu_custom_call" | custom-call | tf_op jit(solution)/shard_map/fields_down/pallas_call | solution.py:399
  53.8 0.0 collective-permute-done.5.low_ref
  53.8 2.4 %near_low_first.1 = (f32[4096,128]{1,0:T(8,128)S(1)}, bf16[4096,128]{1,0:T(8,128)(2,1)}) custom-call(s32[144,128]{1,0:T(8,128)S(1)} %get-tuple-element.35.list_ref, s32[8,128]{1,0:T(8,128)S(1)} %get-tuple-element.36.found_ref, bf16[16,4,256,256]{3,2,1,0:T(8,128)(2,1)S(1)} %load_near_blocks.1.blocks_ref, ...), custom_call_target="tpu_custom_call", output_to_operand_aliasing={{0}: (4, {})} | custom-call | tf_op jit(solution)/shard_map/near_low_first/pallas_call | solution.py:465
  56.2 2.2 %collective-permute-done.4.low_ref = bf16[2048,128]{1,0:T(8,128)(2,1)S(1)} collective-permute-done((bf16[2048,128]{1,0:T(8,128)(2,1)S(1)}, bf16[2048,128]{1,0:T(8,128)(2,1)S(1)}, u32[]{:S(2)}, u32[]{:S(2)}) %collective-permute-start.4) | collective-permute-done | bytes 524320 | tf_op jit(solution)/shard_map/ppermute | solution.py:37
  58.5 2.4 %near_low_second.1 = bf16[4096,128]{1,0:T(8,128)(2,1)} custom-call(s32[144,128]{1,0:T(8,128)S(1)} %get-tuple-element.35.list_ref, s32[8,128]{1,0:T(8,128)S(1)} %get-tuple-element.36.found_ref, bf16[16,4,256,256]{3,2,1,0:T(8,128)(2,1)S(1)} %load_near_blocks.1.blocks_ref, ...), custom_call_target="tpu_custom_call", output_to_operand_aliasing={{}: (5, {})} | custom-call | tf_op jit(solution)/shard_map/near_low_second/pallas_call | solution.py:490
  (11 shorter events, 0.1 us)
Async XLA Ops:
  0.0 24.2 %collective-permute-start = (bf16[4096,128]{1,0:T(8,128)(2,1)}, bf16[4096,128]{1,0:T(8,128)(2,1)S(1)}, u32[]{:S(2)}, u32[]{:S(2)}) collective-permute-start(bf16[4096,128]{1,0:T(8,128)(2,1)} %refs_0_.1), channel_id=1, source_target_pairs={{1,0},{2,1},{3,2},{4,3},{5,4},{6,5},{7,6},{8,7},{9,8},{10,9},{11,1... | collective-permute-start | bytes 3145736 | tf_op jit(solution)/shard_map/ppermute | solution.py:37
  4.6 31.6 %collective-permute-start.2 = (f16[560,128]{1,0:T(8,128)(2,1)S(1)}, f16[560,128]{1,0:T(8,128)(2,1)S(1)}, u32[]{:S(2)}, u32[]{:S(2)}) collective-permute-start(f16[560,128]{1,0:T(8,128)(2,1)S(1)} %convert_element_type.21), channel_id=1, source_target_pairs={{0,1},{1,2},{2,3},{3,4},{4,5},{5,6},{6,7},{7,8},{8,9},{9,10},{10,1... | collective-permute-start | bytes 430088 | tf_op jit(solution)/shard_map/ppermute | solution.py:42
  4.7 31.5 %collective-permute-start.3 = (f16[560,128]{1,0:T(8,128)(2,1)S(1)}, f16[560,128]{1,0:T(8,128)(2,1)S(1)}, u32[]{:S(2)}, u32[]{:S(2)}) collective-permute-start(f16[560,128]{1,0:T(8,128)(2,1)S(1)} %convert_element_type.21), channel_id=1, source_target_pairs={{0,31},{1,0},{2,1},{3,2},{4,3},{5,4},{6,5},{7,6},{8,7},{9,8},{10,9... | collective-permute-start | bytes 430088 | tf_op jit(solution)/shard_map/ppermute | solution.py:42
  6.2 30.0 %collective-permute-start.1 = (f16[48,128]{1,0:T(8,128)(2,1)S(1)}, f16[48,128]{1,0:T(8,128)(2,1)S(1)}, u32[]{:S(2)}, u32[]{:S(2)}) collective-permute-start(f16[48,128]{1,0:T(8,128)(2,1)S(1)} %convert_element_type.22), channel_id=1, source_target_pairs={{0,2},{1,3},{2,0},{3,1},{4,6},{5,7},{6,4},{7,5},{8,10},{9,11},{10,... | collective-permute-start | bytes 36872 | tf_op jit(solution)/shard_map/ppermute | solution.py:183
  8.7 15.5 %copy-start = (s32[16,4]{0,1:T(4,128)S(1)}, s32[16,4]{0,1:T(4,128)}, u32[]{:S(2)}) copy-start(s32[16,4]{0,1:T(4,128)} %param.14) | copy-start | bytes 772
  8.7 45.1 %collective-permute-start.5 = (bf16[2064,128]{1,0:T(8,128)(2,1)S(1)}, bf16[2064,128]{1,0:T(8,128)(2,1)S(1)}, u32[]{:S(2)}, u32[]{:S(2)}) collective-permute-start(bf16[2064,128]{1,0:T(8,128)(2,1)S(1)} %get-tuple-element.41), channel_id=1, source_target_pairs={{0,1},{1,2},{2,3},{3,4},{4,5},{5,6},{6,7},{7,8},{8,9},{9,10},{10,1... | collective-permute-start | bytes 1585160 | tf_op jit(solution)/shard_map/ppermute | solution.py:37
  28.3 20.2 %copy-start.1 = (s32[16,8]{0,1:T(8,128)S(1)}, s32[16,8]{0,1:T(8,128)}, u32[]{:S(2)}) copy-start(s32[16,8]{0,1:T(8,128)} %param.18) | copy-start | bytes 1540
  36.2 22.3 %collective-permute-start.4 = (bf16[2048,128]{1,0:T(8,128)(2,1)S(1)}, bf16[2048,128]{1,0:T(8,128)(2,1)S(1)}, u32[]{:S(2)}, u32[]{:S(2)}) collective-permute-start(bf16[2048,128]{1,0:T(8,128)(2,1)S(1)} %get-tuple-element.40), channel_id=1, source_target_pairs={{0,1},{1,2},{2,3},{3,4},{4,5},{5,6},{6,7},{7,8},{8,9},{9,10},{10,1... | collective-permute-start | bytes 1572872 | tf_op jit(solution)/shard_map/ppermute | solution.py:37
  37.6 3.8 %collective-permute-start.6 = (f16[48,128]{1,0:T(8,128)(2,1)S(1)}, f16[48,128]{1,0:T(8,128)(2,1)S(1)}, u32[]{:S(2)}, u32[]{:S(2)}) collective-permute-start(f16[48,128]{1,0:T(8,128)(2,1)S(1)} %convert_element_type.26), channel_id=1, source_target_pairs={{0,28},{3,7},{4,0},{7,11},{8,4},{11,15},{12,8},{15,19},{16,12},{19... | collective-permute-start | bytes 36872 | tf_op jit(solution)/shard_map/ppermute | solution.py:202
  41.4 10.3 %copy-start.2 = (s32[1,4]{1,0:T(1,128)S(1)}, s32[1,4]{1,0:T(1,128)}, u32[]{:S(2)}) copy-start(s32[1,4]{1,0:T(1,128)} %partner_ref.1) | copy-start | bytes 52
  41.4 10.3 %copy-start.3 = (s32[1,8]{1,0:T(1,128)S(1)}, s32[1,8]{1,0:T(1,128)}, u32[]{:S(2)}) copy-start(s32[1,8]{1,0:T(1,128)} %top_partner_ref.1) | copy-start | bytes 100
  41.9 3.3 %collective-permute-start.7 = (f32[1,32,128]{2,1,0:T(8,128)S(1)}, f32[1,32,128]{2,1,0:T(8,128)S(1)}, u32[]{:S(2)}, u32[]{:S(2)}) collective-permute-start(f32[1,32,128]{2,1,0:T(8,128)S(1)} %get-tuple-element.47.first_ref), channel_id=1, source_target_pairs={{0,4},{4,0},{8,12},{12,8},{16,20},{20,16},{24,28},{28,24},{1,5},{5... | collective-permute-start | bytes 49160 | tf_op jit(solution)/shard_map/ppermute | solution.py:212
  45.2 3.1 %collective-permute-start.8 = (f32[2,32,128]{2,1,0:T(8,128)S(1)}, f32[2,32,128]{2,1,0:T(8,128)S(1)}, u32[]{:S(2)}, u32[]{:S(2)}) collective-permute-start(f32[2,32,128]{2,1,0:T(8,128)S(1)} %join_cols.3.first_ref), channel_id=1, source_target_pairs={{0,8},{4,12},{8,0},{12,4},{16,24},{20,28},{24,16},{28,20},{1,9},{5... | collective-permute-start | bytes 98312 | tf_op jit(solution)/shard_map/ppermute | solution.py:212
  48.3 3.4 %collective-permute-start.9 = (f32[4,32,128]{2,1,0:T(8,128)S(1)}, f32[4,32,128]{2,1,0:T(8,128)S(1)}, u32[]{:S(2)}, u32[]{:S(2)}) collective-permute-start(f32[4,32,128]{2,1,0:T(8,128)S(1)} %join_cols.4.first_ref), channel_id=1, source_target_pairs={{0,16},{4,20},{8,24},{12,28},{16,0},{20,4},{24,8},{28,12},{1,17},{... | collective-permute-start | bytes 196616 | tf_op jit(solution)/shard_map/ppermute | solution.py:212

commit v7 on v6

--- a/solution.py
+++ b/solution.py
@@ -305,7 +305,7 @@
     list_ref[...] = jnp.zeros_like(list_ref)
 
     def note(leaf, carry):
-        found, counts = carry
+        mask, counts = carry
         for k in range(1, slots):
             place = near_ref[k, leaf] - first + leaves
             after = []
@@ -321,13 +321,12 @@
                 one = valid.astype(jnp.int32)
                 after.append(counts[i] + one)
             counts = tuple(after)
-            found = found + jnp.where((lane == leaf) & (place < half), 1, 0)
-        return found, counts
-
-    found, counts = lax.fori_loop(
-        0, leaves, note, (jnp.zeros(lane.shape, jnp.int32), (jnp.int32(0), jnp.int32(0)))
-    )
-    found_ref[0:1, :] = found
+            mask = mask | jnp.where(place < half, lax.shift_left(jnp.int32(1), leaf), 0)
+        return mask, counts
+
+    zero = jnp.int32(0)
+    mask, counts = lax.fori_loop(0, leaves, note, (zero, (zero, zero)))
+    found_ref[0:1, :] = jnp.broadcast_to(mask, lane.shape)
     found_ref[1:2, :] = jnp.where(lane == 0, counts[0], counts[1])
 
     for leaf in range(leaves):
@@ -345,7 +344,7 @@
 
 def near(near_index, blocks, own, high):
     leaves, slots, rows, _ = blocks.shape
-    room = leaves * slots + BATCH
+    room = leaves * slots + 2 * BATCH
     lanes = -(-max(leaves, 2) // 128) * 128
     return pl.pallas_call(
         near_body,
@@ -413,22 +412,24 @@
     count = found_ref[1, part]
     room = list_ref.shape[0] // 2
 
-    @pl.loop(0, pl.cdiv(count, batch_size))
-    def _(batch):
-        terms, ats = [], []
+    def read(batch):
         spots = [part * room + batch * batch_size + i for i in range(batch_size)]
-        entries = [(list_ref[spot, 0], list_ref[spot, 1]) for spot in spots]
+        return [(list_ref[spot, 0], list_ref[spot, 1]) for spot in spots]
+
+    def add(batch, entries):
+        coming = read(batch + 1)
+        terms = []
         for at, place in entries:
             start = pl.multiple_of(place * rows, rows)
             block = blocks_ref[at // slots, lax.rem(at, slots)]
             terms.append(jnp.dot(block, low_ref[pl.ds(start, rows), :], preferred_element_type=jnp.float32))
-            ats.append(at)
-        for i in range(batch_size):
-
-            @pl.when(batch * batch_size + i < count)
-            def _(i=i):
-                start = pl.multiple_of(ats[i] // slots * rows, rows)
-                acc_ref[pl.ds(start, rows), :] += terms[i]
+        for i, (at, _) in enumerate(entries):
+            start = pl.multiple_of(at // slots * rows, rows)
+            term = jnp.where(batch * batch_size + i < count, terms[i], 0.0)
+            acc_ref[pl.ds(start, rows), :] += term
+        return coming
+
+    lax.fori_loop(0, pl.cdiv(count, batch_size), add, read(0))
 
 
 def write(leaves, chosen, acc_ref, out_ref, held, sems):
@@ -455,7 +456,8 @@
 
 def first_body(list_ref, found_ref, blocks_ref, low_ref, acc_in, acc_ref, out_ref, held, sems):
     leaves = blocks_ref.shape[0]
-    final = [found_ref[0, leaf] == 0 for leaf in range(leaves)]
+    mask = found_ref[0, 0]
+    final = [mask & (1 << leaf) == 0 for leaf in range(leaves)]
     add_listed(list_ref, found_ref, 0, BATCH, blocks_ref, low_ref.at[SPARE:, :], acc_ref)
     write(leaves, final, acc_ref, out_ref, held, sems)
 
@@ -480,7 +482,8 @@
 
 def last_body(list_ref, found_ref, blocks_ref, low_ref, acc_ref, out_in, out_ref, held, sems):
     leaves = blocks_ref.shape[0]
-    touched = [found_ref[0, leaf] > 0 for leaf in range(leaves)]
+    mask = found_ref[0, 0]
+    touched = [mask & (1 << leaf) != 0 for leaf in range(leaves)]
     add_listed(list_ref, found_ref, 1, GROUP, blocks_ref, low_ref, acc_ref)
     write(leaves, touched, acc_ref, out_ref, held, sems)
 

time: 61.1 us -> 60.7 us (level)
  Pallas kernels: 20.4 us -> 19.6 us
  transfers between devices with their start and end apart: 10 -> 10, of which waited for: 7 -> 7; matrix products, arithmetic and copies ran while one was open for 0% -> 0% of each run, Pallas kernels for 30% -> 29%
where the time goes in v7:
time: 60.7 us; the launch traced here: 60.4 us
  waiting for transfers between devices  26.4 us (43%)
  Pallas kernels  19.6 us (32%)
  starting transfers between devices  14.2 us (23%)
    ppermute x3, waiting for transfers between devices, shift(): return lax.ppermute(value, BOTH, pairs)  13.3 us
    ppermute x1, waiting for transfers between devices, gather_sub(): lax.ppermute(value, 'sub', [(i, (i + step) % count) for i in range(count)])  7.92 us
    ppermute x3, starting transfers between devices, shift(): return lax.ppermute(value, BOTH, pairs)  4.82 us
    pallas_call x1, Pallas kernels, near(): pl.pallas_call(near_body, in_specs=[SMEM] + [VMEM] * 3, out_specs=[VMEM]...  4.07 us
    ppermute x3, starting transfers between devices, gather_col(): value = join(value, lax.ppermute(value, 'col', pairs))  3.4 us
    pallas_call x1, Pallas kernels, load(): pl.pallas_call(load_body, in_specs=[HBM], out_specs=VMEM, out_shape=pltpu...  3.39 us
    ppermute x3, waiting for transfers between devices, gather_col(): value = join(value, lax.ppermute(value, 'col', pairs))  3.27 us
    pallas_call x1, Pallas kernels, far(): call(far_body, [SMEM] * 2 + [HBM] + [VMEM] * 3, [(own.shape, jnp.float32)...  3.08 us
  transfers between devices with their start and end apart: 10, of which 7 were waited for; matrix products, arithmetic and copies ran while one was open for 0% of the time, Pallas kernels for 29%

profile of v7, /device:TPU:31, one launch (start us, length us, event | category | flops | bytes accessed | tf_op | source)
XLA Modules:
  0.0 60.4 jit_solution(12762879427912371271)
XLA Ops:
  0.0 2.1 %collective-permute-start = (bf16[4096,128]{1,0:T(8,128)(2,1)}, bf16[4096,128]{1,0:T(8,128)(2,1)S(1)}, u32[]{:S(2)}, u32[]{:S(2)}) collective-permute-start(bf16[4096,128]{1,0:T(8,128)(2,1)} %refs_0_.1), channel_id=1, source_target_pairs={{1,0},{2,1},{3,2},{4,3},{5,4},{6,5},{7,6},{8,7},{9,8},{10,9},{11,1... | collective-permute-start | bytes 3145736 | tf_op jit(solution)/shard_map/ppermute | solution.py:37
  2.1 2.5 %leaf_and_cluster_coefs.1 = (bf16[4096,128]{1,0:T(8,128)(2,1)S(1)}, bf16[16,32,256]{2,1,0:T(8,128)(2,1)S(1)}, f32[16,32,32]{2,1,0:T(8,128)S(1)}, f32[1,32,32]{2,...) custom-call(bf16[4096,128]{1,0:T(8,128)(2,1)} %refs_0_.1, ...), custom_call_target="tpu_custom_call" | custom-call | tf_op jit(solution)/shard_map/leaf_and_cluster_coefs/pallas_call | solution.py:109
  4.6 0.1 collective-permute-start.2
  4.7 1.5 %collective-permute-start.3 = (f16[560,128]{1,0:T(8,128)(2,1)S(1)}, f16[560,128]{1,0:T(8,128)(2,1)S(1)}, u32[]{:S(2)}, u32[]{:S(2)}) collective-permute-start(f16[560,128]{1,0:T(8,128)(2,1)S(1)} %convert_element_type.21), channel_id=1, source_target_pairs={{0,31},{1,0},{2,1},{3,2},{4,3},{5,4},{6,5},{7,6},{8,7},{9,8},{10,9... | collective-permute-start | bytes 430088 | tf_op jit(solution)/shard_map/ppermute | solution.py:42
  6.2 2.5 %collective-permute-start.1 = (f16[48,128]{1,0:T(8,128)(2,1)S(1)}, f16[48,128]{1,0:T(8,128)(2,1)S(1)}, u32[]{:S(2)}, u32[]{:S(2)}) collective-permute-start(f16[48,128]{1,0:T(8,128)(2,1)S(1)} %convert_element_type.22), channel_id=1, source_target_pairs={{0,2},{1,3},{2,0},{3,1},{4,6},{5,7},{6,4},{7,5},{8,10},{9,11},{10,... | collective-permute-start | bytes 36872 | tf_op jit(solution)/shard_map/ppermute | solution.py:183
  8.7 0.0 copy-start
  8.7 1.4 %collective-permute-start.5 = (bf16[2064,128]{1,0:T(8,128)(2,1)S(1)}, bf16[2064,128]{1,0:T(8,128)(2,1)S(1)}, u32[]{:S(2)}, u32[]{:S(2)}) collective-permute-start(bf16[2064,128]{1,0:T(8,128)(2,1)S(1)} %get-tuple-element.41), channel_id=1, source_target_pairs={{0,1},{1,2},{2,3},{3,4},{4,5},{5,6},{6,7},{7,8},{8,9},{9,10},{10,1... | collective-permute-start | bytes 1585160 | tf_op jit(solution)/shard_map/ppermute | solution.py:37
  10.1 3.4 %load_near_blocks.1.blocks_ref = bf16[16,4,256,256]{3,2,1,0:T(8,128)(2,1)S(1)} custom-call(bf16[16,4,256,256]{3,2,1,0:T(8,128)(2,1)} %blocks_ref), custom_call_target="tpu_custom_call" | custom-call | tf_op jit(solution)/shard_map/load_near_blocks/pallas_call | solution.py:280
  13.5 10.7 %collective-permute-done.high_ref = bf16[4096,128]{1,0:T(8,128)(2,1)S(1)} collective-permute-done((bf16[4096,128]{1,0:T(8,128)(2,1)}, bf16[4096,128]{1,0:T(8,128)(2,1)S(1)}, u32[]{:S(2)}, u32[]{:S(2)}) %collective-permute-start) | collective-permute-done | bytes 1048608 | tf_op jit(solution)/shard_map/ppermute | solution.py:37
  24.2 0.0 copy-done
  24.2 4.1 %near_own_and_high.1 = (f32[4096,128]{1,0:T(8,128)S(1)}, s32[160,128]{1,0:T(8,128)S(1)}, s32[8,128]{1,0:T(8,128)S(1)}) custom-call(s32[4,16]{1,0:T(4,128)S(1)} %bitcast.2, bf16[16,4,256,256]{3,2,1,0:T(8,128)(2,1)S(1)} %load_near_blocks.1.blocks_ref, bf16[4096,128]{1,0:T(8,128)(2,1)S(1)} %get-tuple-element.34.own_ref, ...), custom_call_target="tpu_custom_call" | custom-call | tf_op jit(solution)/shard_map/near_own_and_high/pallas_call | solution.py:349
  28.3 0.0 copy-start.1
  28.3 7.9 %collective-permute-done.1 = f16[48,128]{1,0:T(8,128)(2,1)S(1)} collective-permute-done((f16[48,128]{1,0:T(8,128)(2,1)S(1)}, f16[48,128]{1,0:T(8,128)(2,1)S(1)}, u32[]{:S(2)}, u32[]{:S(2)}) %collective-permute-start.1) | collective-permute-done | bytes 12320 | tf_op jit(solution)/shard_map/ppermute | solution.py:183
  36.2 0.0 collective-permute-done.2
  36.2 0.0 collective-permute-done.3
  36.2 1.3 %collective-permute-start.4 = (bf16[2048,128]{1,0:T(8,128)(2,1)S(1)}, bf16[2048,128]{1,0:T(8,128)(2,1)S(1)}, u32[]{:S(2)}, u32[]{:S(2)}) collective-permute-start(bf16[2048,128]{1,0:T(8,128)(2,1)S(1)} %get-tuple-element.40), channel_id=1, source_target_pairs={{0,1},{1,2},{2,3},{3,4},{4,5},{5,6},{6,7},{7,8},{8,9},{9,10},{10,1... | collective-permute-start | bytes 1572872 | tf_op jit(solution)/shard_map/ppermute | solution.py:37
  37.6 1.9 %collective-permute-start.6 = (f16[48,128]{1,0:T(8,128)(2,1)S(1)}, f16[48,128]{1,0:T(8,128)(2,1)S(1)}, u32[]{:S(2)}, u32[]{:S(2)}) collective-permute-start(f16[48,128]{1,0:T(8,128)(2,1)S(1)} %convert_element_type.26), channel_id=1, source_target_pairs={{0,28},{3,7},{4,0},{7,11},{8,4},{11,15},{12,8},{15,19},{16,12},{19... | collective-permute-start | bytes 36872 | tf_op jit(solution)/shard_map/ppermute | solution.py:202
  39.5 1.8 %collective-permute-done.6 = f16[48,128]{1,0:T(8,128)(2,1)S(1)} collective-permute-done((f16[48,128]{1,0:T(8,128)(2,1)S(1)}, f16[48,128]{1,0:T(8,128)(2,1)S(1)}, u32[]{:S(2)}, u32[]{:S(2)}) %collective-permute-start.6) | collective-permute-done | bytes 12320 | tf_op jit(solution)/shard_map/ppermute | solution.py:202
  41.4 0.0 copy-start.2
  41.4 0.0 copy-start.3
  41.4 0.5 sums_over_sub.1
  41.9 2.5 %collective-permute-start.7 = (f32[1,32,128]{2,1,0:T(8,128)S(1)}, f32[1,32,128]{2,1,0:T(8,128)S(1)}, u32[]{:S(2)}, u32[]{:S(2)}) collective-permute-start(f32[1,32,128]{2,1,0:T(8,128)S(1)} %get-tuple-element.47.first_ref), channel_id=1, source_target_pairs={{0,4},{4,0},{8,12},{12,8},{16,20},{20,16},{24,28},{28,24},{1,5},{5... | collective-permute-start | bytes 49160 | tf_op jit(solution)/shard_map/ppermute | solution.py:212
  44.4 0.8 %collective-permute-done.7.second_ref = f32[1,32,128]{2,1,0:T(8,128)S(1)} collective-permute-done((f32[1,32,128]{2,1,0:T(8,128)S(1)}, f32[1,32,128]{2,1,0:T(8,128)S(1)}, u32[]{:S(2)}, u32[]{:S(2)}) %collective-permute-start.7) | collective-permute-done | bytes 16416 | tf_op jit(solution)/shard_map/ppermute | solution.py:212
  45.2 0.7 %collective-permute-start.8 = (f32[2,32,128]{2,1,0:T(8,128)S(1)}, f32[2,32,128]{2,1,0:T(8,128)S(1)}, u32[]{:S(2)}, u32[]{:S(2)}) collective-permute-start(f32[2,32,128]{2,1,0:T(8,128)S(1)} %join_cols.3.first_ref), channel_id=1, source_target_pairs={{0,8},{4,12},{8,0},{12,4},{16,24},{20,28},{24,16},{28,20},{1,9},{5... | collective-permute-start | bytes 98312 | tf_op jit(solution)/shard_map/ppermute | solution.py:212
  46.0 2.3 %collective-permute-done.8.second_ref = f32[2,32,128]{2,1,0:T(8,128)S(1)} collective-permute-done((f32[2,32,128]{2,1,0:T(8,128)S(1)}, f32[2,32,128]{2,1,0:T(8,128)S(1)}, u32[]{:S(2)}, u32[]{:S(2)}) %collective-permute-start.8) | collective-permute-done | bytes 32800 | tf_op jit(solution)/shard_map/ppermute | solution.py:212
  48.3 0.2 collective-permute-start.9
  48.5 0.0 copy-done.1
  48.5 3.1 %far_field_of_leaves.1.field_ref = f32[512,128]{1,0:T(8,128)S(1)} custom-call(s32[8,16]{1,0:T(8,128)S(1)} %bitcast.4, s32[4,16]{1,0:T(4,128)S(1)} %bitcast.3, f32[16,8,32,32]{3,2,1,0:T(8,128)} %coupling_in.1, f32[560,128]{1,0:T(8,128)S(1)} %convert_element_type.23.low_ref, f32[512,128]{1,0:T(8,128)S(1)} %get-tuple-element.52.own_ref, ...), custom_call_target="tpu_custom_call" | custom-call | tf_op jit(solution)/shard_map/far_field_of_leaves/pallas_call | solution.py:259
  51.6 0.1 collective-permute-done.9.second_ref
  51.7 0.0 copy-done.2
  51.7 0.0 copy-done.3
  51.7 2.0 %fields_down.1.acc_in = f32[4096,128]{1,0:T(8,128)S(1)} custom-call(s32[1,4]{1,0:T(1,128)S(1)} %copy-done.2, s32[1,8]{1,0:T(1,128)S(1)} %copy-done.3, f32[4,32,128]{2,1,0:T(8,128)S(1)} %get-tuple-element.46.stack_ref, f32[8,32,128]{2,1,0:T(8,128)S(1)} %join_cols.5.cols_ref, f32[1,4,32,32]{3,2,1,0:T(8,128)S(1)} %get-tuple-element.48.coupling_ref, ...), custom_call_target="tpu_custom_call" | custom-call | tf_op jit(solution)/shard_map/fields_down/pallas_call | solution.py:398
  53.8 0.0 collective-permute-done.5.low_ref
  53.8 2.1 %near_low_first.1 = (f32[4096,128]{1,0:T(8,128)S(1)}, bf16[4096,128]{1,0:T(8,128)(2,1)}) custom-call(s32[160,128]{1,0:T(8,128)S(1)} %get-tuple-element.35.list_ref, s32[8,128]{1,0:T(8,128)S(1)} %get-tuple-element.36.found_ref, bf16[16,4,256,256]{3,2,1,0:T(8,128)(2,1)S(1)} %load_near_blocks.1.blocks_ref, ...), custom_call_target="tpu_custom_call", output_to_operand_aliasing={{0}: (4, {})} | custom-call | tf_op jit(solution)/shard_map/near_low_first/pallas_call | solution.py:467
  55.8 2.6 %collective-permute-done.4.low_ref = bf16[2048,128]{1,0:T(8,128)(2,1)S(1)} collective-permute-done((bf16[2048,128]{1,0:T(8,128)(2,1)S(1)}, bf16[2048,128]{1,0:T(8,128)(2,1)S(1)}, u32[]{:S(2)}, u32[]{:S(2)}) %collective-permute-start.4) | collective-permute-done | bytes 524320 | tf_op jit(solution)/shard_map/ppermute | solution.py:37
  58.5 1.9 %near_low_second.1 = bf16[4096,128]{1,0:T(8,128)(2,1)} custom-call(s32[160,128]{1,0:T(8,128)S(1)} %get-tuple-element.35.list_ref, s32[8,128]{1,0:T(8,128)S(1)} %get-tuple-element.36.found_ref, bf16[16,4,256,256]{3,2,1,0:T(8,128)(2,1)S(1)} %load_near_blocks.1.blocks_ref, ...), custom_call_target="tpu_custom_call", output_to_operand_aliasing={{}: (5, {})} | custom-call | tf_op jit(solution)/shard_map/near_low_second/pallas_call | solution.py:493
  (11 shorter events, 0.1 us)
Async XLA Ops:
  0.0 24.2 %collective-permute-start = (bf16[4096,128]{1,0:T(8,128)(2,1)}, bf16[4096,128]{1,0:T(8,128)(2,1)S(1)}, u32[]{:S(2)}, u32[]{:S(2)}) collective-permute-start(bf16[4096,128]{1,0:T(8,128)(2,1)} %refs_0_.1), channel_id=1, source_target_pairs={{1,0},{2,1},{3,2},{4,3},{5,4},{6,5},{7,6},{8,7},{9,8},{10,9},{11,1... | collective-permute-start | bytes 3145736 | tf_op jit(solution)/shard_map/ppermute | solution.py:37
  4.6 31.6 %collective-permute-start.2 = (f16[560,128]{1,0:T(8,128)(2,1)S(1)}, f16[560,128]{1,0:T(8,128)(2,1)S(1)}, u32[]{:S(2)}, u32[]{:S(2)}) collective-permute-start(f16[560,128]{1,0:T(8,128)(2,1)S(1)} %convert_element_type.21), channel_id=1, source_target_pairs={{0,1},{1,2},{2,3},{3,4},{4,5},{5,6},{6,7},{7,8},{8,9},{9,10},{10,1... | collective-permute-start | bytes 430088 | tf_op jit(solution)/shard_map/ppermute | solution.py:42
  4.7 31.5 %collective-permute-start.3 = (f16[560,128]{1,0:T(8,128)(2,1)S(1)}, f16[560,128]{1,0:T(8,128)(2,1)S(1)}, u32[]{:S(2)}, u32[]{:S(2)}) collective-permute-start(f16[560,128]{1,0:T(8,128)(2,1)S(1)} %convert_element_type.21), channel_id=1, source_target_pairs={{0,31},{1,0},{2,1},{3,2},{4,3},{5,4},{6,5},{7,6},{8,7},{9,8},{10,9... | collective-permute-start | bytes 430088 | tf_op jit(solution)/shard_map/ppermute | solution.py:42
  6.2 30.0 %collective-permute-start.1 = (f16[48,128]{1,0:T(8,128)(2,1)S(1)}, f16[48,128]{1,0:T(8,128)(2,1)S(1)}, u32[]{:S(2)}, u32[]{:S(2)}) collective-permute-start(f16[48,128]{1,0:T(8,128)(2,1)S(1)} %convert_element_type.22), channel_id=1, source_target_pairs={{0,2},{1,3},{2,0},{3,1},{4,6},{5,7},{6,4},{7,5},{8,10},{9,11},{10,... | collective-permute-start | bytes 36872 | tf_op jit(solution)/shard_map/ppermute | solution.py:183
  8.7 15.5 %copy-start = (s32[16,4]{0,1:T(4,128)S(1)}, s32[16,4]{0,1:T(4,128)}, u32[]{:S(2)}) copy-start(s32[16,4]{0,1:T(4,128)} %param.14) | copy-start | bytes 772
  8.7 45.1 %collective-permute-start.5 = (bf16[2064,128]{1,0:T(8,128)(2,1)S(1)}, bf16[2064,128]{1,0:T(8,128)(2,1)S(1)}, u32[]{:S(2)}, u32[]{:S(2)}) collective-permute-start(bf16[2064,128]{1,0:T(8,128)(2,1)S(1)} %get-tuple-element.41), channel_id=1, source_target_pairs={{0,1},{1,2},{2,3},{3,4},{4,5},{5,6},{6,7},{7,8},{8,9},{9,10},{10,1... | collective-permute-start | bytes 1585160 | tf_op jit(solution)/shard_map/ppermute | solution.py:37
  28.3 20.2 %copy-start.1 = (s32[16,8]{0,1:T(8,128)S(1)}, s32[16,8]{0,1:T(8,128)}, u32[]{:S(2)}) copy-start(s32[16,8]{0,1:T(8,128)} %param.18) | copy-start | bytes 1540
  36.2 22.3 %collective-permute-start.4 = (bf16[2048,128]{1,0:T(8,128)(2,1)S(1)}, bf16[2048,128]{1,0:T(8,128)(2,1)S(1)}, u32[]{:S(2)}, u32[]{:S(2)}) collective-permute-start(bf16[2048,128]{1,0:T(8,128)(2,1)S(1)} %get-tuple-element.40), channel_id=1, source_target_pairs={{0,1},{1,2},{2,3},{3,4},{4,5},{5,6},{6,7},{7,8},{8,9},{9,10},{10,1... | collective-permute-start | bytes 1572872 | tf_op jit(solution)/shard_map/ppermute | solution.py:37
  37.6 3.8 %collective-permute-start.6 = (f16[48,128]{1,0:T(8,128)(2,1)S(1)}, f16[48,128]{1,0:T(8,128)(2,1)S(1)}, u32[]{:S(2)}, u32[]{:S(2)}) collective-permute-start(f16[48,128]{1,0:T(8,128)(2,1)S(1)} %convert_element_type.26), channel_id=1, source_target_pairs={{0,28},{3,7},{4,0},{7,11},{8,4},{11,15},{12,8},{15,19},{16,12},{19... | collective-permute-start | bytes 36872 | tf_op jit(solution)/shard_map/ppermute | solution.py:202
  41.4 10.3 %copy-start.2 = (s32[1,4]{1,0:T(1,128)S(1)}, s32[1,4]{1,0:T(1,128)}, u32[]{:S(2)}) copy-start(s32[1,4]{1,0:T(1,128)} %partner_ref.1) | copy-start | bytes 52
  41.4 10.3 %copy-start.3 = (s32[1,8]{1,0:T(1,128)S(1)}, s32[1,8]{1,0:T(1,128)}, u32[]{:S(2)}) copy-start(s32[1,8]{1,0:T(1,128)} %top_partner_ref.1) | copy-start | bytes 100
  41.9 3.3 %collective-permute-start.7 = (f32[1,32,128]{2,1,0:T(8,128)S(1)}, f32[1,32,128]{2,1,0:T(8,128)S(1)}, u32[]{:S(2)}, u32[]{:S(2)}) collective-permute-start(f32[1,32,128]{2,1,0:T(8,128)S(1)} %get-tuple-element.47.first_ref), channel_id=1, source_target_pairs={{0,4},{4,0},{8,12},{12,8},{16,20},{20,16},{24,28},{28,24},{1,5},{5... | collective-permute-start | bytes 49160 | tf_op jit(solution)/shard_map/ppermute | solution.py:212
  45.2 3.1 %collective-permute-start.8 = (f32[2,32,128]{2,1,0:T(8,128)S(1)}, f32[2,32,128]{2,1,0:T(8,128)S(1)}, u32[]{:S(2)}, u32[]{:S(2)}) collective-permute-start(f32[2,32,128]{2,1,0:T(8,128)S(1)} %join_cols.3.first_ref), channel_id=1, source_target_pairs={{0,8},{4,12},{8,0},{12,4},{16,24},{20,28},{24,16},{28,20},{1,9},{5... | collective-permute-start | bytes 98312 | tf_op jit(solution)/shard_map/ppermute | solution.py:212
  48.3 3.4 %collective-permute-start.9 = (f32[4,32,128]{2,1,0:T(8,128)S(1)}, f32[4,32,128]{2,1,0:T(8,128)S(1)}, u32[]{:S(2)}, u32[]{:S(2)}) collective-permute-start(f32[4,32,128]{2,1,0:T(8,128)S(1)} %join_cols.4.first_ref), channel_id=1, source_target_pairs={{0,16},{4,20},{8,24},{12,28},{16,0},{20,4},{24,8},{28,12},{1,17},{... | collective-permute-start | bytes 196616 | tf_op jit(solution)/shard_map/ppermute | solution.py:212

commit v8 on v7

--- a/solution.py
+++ b/solution.py
@@ -72,7 +72,7 @@
 def upward_body(*refs):
     sources, targets, refs = refs[:6], refs[6:12], refs[12:]
     vec_ref, basis_ref, transfer_ref, cluster_ref, _, _ = targets
-    first_ref, second_ref, coefs_ref, long_ref, short_ref, pair_ref, sems = refs
+    first_ref, second_ref, coefs_ref, long_ref, short_ref, own_ref, sems = refs
     leaves, rank, rows = basis_ref.shape
     columns = vec_ref.shape[1]
     pairs = list(zip(sources, targets))
@@ -81,7 +81,7 @@
     copies = [pltpu.make_async_copy(source, target, sems.at[i]) for i, (source, target) in enumerate(pairs)]
     for copy in copies:
         copy.start()
-    for copy in copies:
+    for copy in copies[:4]:
         copy.wait()
     for leaf in range(leaves):
         coefs_ref[leaf * rank : (leaf + 1) * rank, :] = jnp.dot(
@@ -90,14 +90,14 @@
     whole = coefs_ref[...]
     transfer = transfer_ref[...].reshape(leaves * rank, rank)
     low = exact(transfer, whole, (0, 0))
-    top = exact(cluster_ref[0], low, (0, 0))
-    pair_ref[0] = low
-    pair_ref[1] = top
+    own_ref[...] = low
     matrix = cluster_ref[0]
     height = rank * rank // columns
     wide = jnp.concatenate([matrix[i : i + height, :] for i in range(0, rank, height)], axis=1)
     pack(long_ref, (whole, low, wide))
     short_ref[...] = long_ref[leaves * rank :, :]
+    for copy in copies[4:]:
+        copy.wait()
 
 
 def upward(vectors, basis, transfer, cluster_transfer, cluster_coupling, top_coupling):
@@ -116,20 +116,20 @@
             ((leaves * rank, columns), f32),
             ((leaves * rank + short, columns), f32),
             ((short, columns), f32),
-            ((2, rank, columns), f32),
+            ((rank, columns), f32),
         ],
         scratch=[pltpu.SemaphoreType.DMA((8,))],
         name="leaf_and_cluster_coefs",
     )(*[in_hbm(array) for array in arrays])
 
 
-def cluster_body(subs, own_ref, low_ref, high_ref, *refs):
+def cluster_body(subs, own_ref, matrix_ref, low_ref, high_ref, *refs):
     part_refs, (stack_ref, top_ref) = refs[:-2], refs[-2:]
-    rank = own_ref.shape[1]
+    rank = own_ref.shape[0]
     sub = lax.axis_index("sub")
-    matrices, lows = [], []
-
-    columns = own_ref.shape[2]
+    matrices, lows = [matrix_ref[0]], [own_ref[...]]
+
+    columns = own_ref.shape[1]
     height = rank * rank // columns
 
     def put(valid, place, ref):
@@ -145,25 +145,25 @@
         matrices.append(matrix)
         lows.append(jnp.where(valid, low, 0.0))
 
-    stack_ref[sub] = own_ref[0]
+    stack_ref[sub] = own_ref[...]
     put(sub > 0, sub - 1, low_ref)
     put(sub < subs - 1, sub + 1, high_ref)
     for i, ref in enumerate(part_refs[:-1]):
         put(sub >= 0, lax.rem(sub - 2 - i + subs, subs), ref)
     if part_refs:
         put((sub == 0) | (sub == subs - 1), subs - 1 - sub, part_refs[-1])
-    top_ref[0] = own_ref[1] + exact(jnp.concatenate(matrices, axis=0), jnp.concatenate(lows, axis=0), (0, 0))
-
-
-def cluster_sums(own, low, high, parts):
-    _, rank, columns = own.shape
+    top_ref[0] = exact(jnp.concatenate(matrices, axis=0), jnp.concatenate(lows, axis=0), (0, 0))
+
+
+def cluster_sums(own, matrix, low, high, parts):
+    rank, columns = own.shape
     subs = lax.axis_size("sub")
     return call(
         functools.partial(cluster_body, subs),
-        [VMEM] * (3 + len(parts)),
+        [VMEM] * (4 + len(parts)),
         [((subs, rank, columns), jnp.float32), ((1, rank, columns), jnp.float32)],
         name="sums_over_sub",
-    )(own, low, high, *parts)
+    )(own, matrix, low, high, *parts)
 
 
 def join_body(first_ref, second_ref, out_ref):
@@ -523,7 +523,7 @@
     high_vec = shift(vectors, -1)
     near_index, leaf_far = near_index.T, leaf_far.T
 
-    own, basis, transfer, cluster, couple, top_couple, first, second, coefs, long, short, pair = upward(
+    own, basis, transfer, cluster, couple, top_couple, first, second, coefs, long, short, own_low = upward(
         vectors, leaf_basis, leaf_transfer, cluster_transfer, cluster_coupling, top_coupling
     )
     long, short = long.astype(jnp.float16), short.astype(jnp.float16)
@@ -542,7 +542,7 @@
     if lax.axis_size("sub") > 2:
         parts = parts + [around(low_part, high_part, short.shape[0])]
     parts = [part.astype(jnp.float32) for part in parts]
-    stack, top = cluster_sums(pair, low_part, high_part, parts)
+    stack, top = cluster_sums(own_low, cluster, low_part, high_part, parts)
     cols = gather_col(top)
     field = far(leaf_far, near_index, leaf_coupling, low_part, coefs, high_part)
     acc = down(

time: 60.7 us -> 60.6 us (level)
  starting transfers between devices: 14.2 us -> 16.1 us
  waiting for transfers between devices: 26.4 us -> 24.5 us
    ppermute x1, waiting for transfers between devices: 7.92 us -> 3.55 us  [gather_sub(): lax.ppermute(value, 'sub', [(i, (i + step) % count) for i in range(count)])]
    ppermute x1, waiting for transfers between devices: 1.85 us -> 3.83 us  [around(): return lax.ppermute(onward.astype(jnp.float16), BOTH, pairs)]
    ppermute x1, starting transfers between devices: 1.92 us -> 3.85 us  [around(): return lax.ppermute(onward.astype(jnp.float16), BOTH, pairs)]
  transfers between devices with their start and end apart: 10 -> 10, of which waited for: 7 -> 8; matrix products, arithmetic and copies ran while one was open for 0% -> 0% of each run, Pallas kernels for 29% -> 29%
where the time goes in v8:
time: 60.6 us; the launch traced here: 60 us
  waiting for transfers between devices  24.5 us (40%)
  Pallas kernels  19.2 us (32%)
  starting transfers between devices  16.1 us (27%)
    ppermute x3, waiting for transfers between devices, shift(): return lax.ppermute(value, BOTH, pairs)  13.3 us
    ppermute x3, starting transfers between devices, shift(): return lax.ppermute(value, BOTH, pairs)  4.82 us
    pallas_call x1, Pallas kernels, near(): pl.pallas_call(near_body, in_specs=[SMEM] + [VMEM] * 3, out_specs=[VMEM]...  4.06 us
    ppermute x1, starting transfers between devices, around(): return lax.ppermute(onward.astype(jnp.float16), BOTH, pairs)  3.85 us
    ppermute x1, waiting for transfers between devices, around(): return lax.ppermute(onward.astype(jnp.float16), BOTH, pairs)  3.83 us
    ppermute x1, waiting for transfers between devices, gather_sub(): lax.ppermute(value, 'sub', [(i, (i + step) % count) for i in range(count)])  3.55 us
    ppermute x3, starting transfers between devices, gather_col(): value = join(value, lax.ppermute(value, 'col', pairs))  3.4 us
    pallas_call x1, Pallas kernels, load(): pl.pallas_call(load_body, in_specs=[HBM], out_specs=VMEM, out_shape=pltpu...  3.39 us
  transfers between devices with their start and end apart: 10, of which 8 were waited for; matrix products, arithmetic and copies ran while one was open for 0% of the time, Pallas kernels for 29%

profile of v8, /device:TPU:31, one launch (start us, length us, event | category | flops | bytes accessed | tf_op | source)
XLA Modules:
  0.0 60.0 jit_solution(7983761309799959736)
XLA Ops:
  0.0 2.1 %collective-permute-start = (bf16[4096,128]{1,0:T(8,128)(2,1)}, bf16[4096,128]{1,0:T(8,128)(2,1)S(1)}, u32[]{:S(2)}, u32[]{:S(2)}) collective-permute-start(bf16[4096,128]{1,0:T(8,128)(2,1)} %refs_0_.1), channel_id=1, source_target_pairs={{1,0},{2,1},{3,2},{4,3},{5,4},{6,5},{7,6},{8,7},{9,8},{10,9},{11,1... | collective-permute-start | bytes 3145736 | tf_op jit(solution)/shard_map/ppermute | solution.py:37
  2.1 2.0 %leaf_and_cluster_coefs.1 = (bf16[4096,128]{1,0:T(8,128)(2,1)S(1)}, bf16[16,32,256]{2,1,0:T(8,128)(2,1)S(1)}, f32[16,32,32]{2,1,0:T(8,128)S(1)}, f32[1,32,32]{2,...) custom-call(bf16[4096,128]{1,0:T(8,128)(2,1)} %refs_0_.1, ...), custom_call_target="tpu_custom_call" | custom-call | tf_op jit(solution)/shard_map/leaf_and_cluster_coefs/pallas_call | solution.py:109
  4.2 0.1 collective-permute-start.2
  4.3 1.5 %collective-permute-start.3 = (f16[560,128]{1,0:T(8,128)(2,1)S(1)}, f16[560,128]{1,0:T(8,128)(2,1)S(1)}, u32[]{:S(2)}, u32[]{:S(2)}) collective-permute-start(f16[560,128]{1,0:T(8,128)(2,1)S(1)} %convert_element_type.21), channel_id=1, source_target_pairs={{0,31},{1,0},{2,1},{3,2},{4,3},{5,4},{6,5},{7,6},{8,7},{9,8},{10,9... | collective-permute-start | bytes 430088 | tf_op jit(solution)/shard_map/ppermute | solution.py:42
  5.7 2.5 %collective-permute-start.1 = (f16[48,128]{1,0:T(8,128)(2,1)S(1)}, f16[48,128]{1,0:T(8,128)(2,1)S(1)}, u32[]{:S(2)}, u32[]{:S(2)}) collective-permute-start(f16[48,128]{1,0:T(8,128)(2,1)S(1)} %convert_element_type.22), channel_id=1, source_target_pairs={{0,2},{1,3},{2,0},{3,1},{4,6},{5,7},{6,4},{7,5},{8,10},{9,11},{10,... | collective-permute-start | bytes 36872 | tf_op jit(solution)/shard_map/ppermute | solution.py:183
  8.2 0.0 copy-start
  8.2 1.4 %collective-permute-start.5 = (bf16[2064,128]{1,0:T(8,128)(2,1)S(1)}, bf16[2064,128]{1,0:T(8,128)(2,1)S(1)}, u32[]{:S(2)}, u32[]{:S(2)}) collective-permute-start(bf16[2064,128]{1,0:T(8,128)(2,1)S(1)} %get-tuple-element.41), channel_id=1, source_target_pairs={{0,1},{1,2},{2,3},{3,4},{4,5},{5,6},{6,7},{7,8},{8,9},{9,10},{10,1... | collective-permute-start | bytes 1585160 | tf_op jit(solution)/shard_map/ppermute | solution.py:37
  9.7 3.4 %load_near_blocks.1.blocks_ref = bf16[16,4,256,256]{3,2,1,0:T(8,128)(2,1)S(1)} custom-call(bf16[16,4,256,256]{3,2,1,0:T(8,128)(2,1)} %blocks_ref), custom_call_target="tpu_custom_call" | custom-call | tf_op jit(solution)/shard_map/load_near_blocks/pallas_call | solution.py:280
  13.1 11.1 %collective-permute-done.high_ref = bf16[4096,128]{1,0:T(8,128)(2,1)S(1)} collective-permute-done((bf16[4096,128]{1,0:T(8,128)(2,1)}, bf16[4096,128]{1,0:T(8,128)(2,1)S(1)}, u32[]{:S(2)}, u32[]{:S(2)}) %collective-permute-start) | collective-permute-done | bytes 1048608 | tf_op jit(solution)/shard_map/ppermute | solution.py:37
  24.2 0.0 copy-done
  24.2 4.1 %near_own_and_high.1 = (f32[4096,128]{1,0:T(8,128)S(1)}, s32[160,128]{1,0:T(8,128)S(1)}, s32[8,128]{1,0:T(8,128)S(1)}) custom-call(s32[4,16]{1,0:T(4,128)S(1)} %bitcast.2, bf16[16,4,256,256]{3,2,1,0:T(8,128)(2,1)S(1)} %load_near_blocks.1.blocks_ref, bf16[4096,128]{1,0:T(8,128)(2,1)S(1)} %get-tuple-element.34.own_ref, ...), custom_call_target="tpu_custom_call" | custom-call | tf_op jit(solution)/shard_map/near_own_and_high/pallas_call | solution.py:349
  28.3 0.0 copy-start.1
  28.3 3.5 %collective-permute-done.1 = f16[48,128]{1,0:T(8,128)(2,1)S(1)} collective-permute-done((f16[48,128]{1,0:T(8,128)(2,1)S(1)}, f16[48,128]{1,0:T(8,128)(2,1)S(1)}, u32[]{:S(2)}, u32[]{:S(2)}) %collective-permute-start.1) | collective-permute-done | bytes 12320 | tf_op jit(solution)/shard_map/ppermute | solution.py:183
  31.8 0.5 collective-permute-done.2
  32.3 0.0 collective-permute-done.3
  32.4 1.3 %collective-permute-start.4 = (bf16[2048,128]{1,0:T(8,128)(2,1)S(1)}, bf16[2048,128]{1,0:T(8,128)(2,1)S(1)}, u32[]{:S(2)}, u32[]{:S(2)}) collective-permute-start(bf16[2048,128]{1,0:T(8,128)(2,1)S(1)} %get-tuple-element.40), channel_id=1, source_target_pairs={{0,1},{1,2},{2,3},{3,4},{4,5},{5,6},{6,7},{7,8},{8,9},{9,10},{10,1... | collective-permute-start | bytes 1572872 | tf_op jit(solution)/shard_map/ppermute | solution.py:37
  33.7 3.8 %collective-permute-start.6 = (f16[48,128]{1,0:T(8,128)(2,1)S(1)}, f16[48,128]{1,0:T(8,128)(2,1)S(1)}, u32[]{:S(2)}, u32[]{:S(2)}) collective-permute-start(f16[48,128]{1,0:T(8,128)(2,1)S(1)} %convert_element_type.26), channel_id=1, source_target_pairs={{0,28},{3,7},{4,0},{7,11},{8,4},{11,15},{12,8},{15,19},{16,12},{19... | collective-permute-start | bytes 36872 | tf_op jit(solution)/shard_map/ppermute | solution.py:202
  37.6 3.8 %collective-permute-done.6 = f16[48,128]{1,0:T(8,128)(2,1)S(1)} collective-permute-done((f16[48,128]{1,0:T(8,128)(2,1)S(1)}, f16[48,128]{1,0:T(8,128)(2,1)S(1)}, u32[]{:S(2)}, u32[]{:S(2)}) %collective-permute-start.6) | collective-permute-done | bytes 12320 | tf_op jit(solution)/shard_map/ppermute | solution.py:202
  41.4 0.0 copy-start.2
  41.4 0.0 copy-start.3
  41.4 0.6 sums_over_sub.1
  42.0 2.5 %collective-permute-start.7 = (f32[1,32,128]{2,1,0:T(8,128)S(1)}, f32[1,32,128]{2,1,0:T(8,128)S(1)}, u32[]{:S(2)}, u32[]{:S(2)}) collective-permute-start(f32[1,32,128]{2,1,0:T(8,128)S(1)} %get-tuple-element.48.first_ref), channel_id=1, source_target_pairs={{0,4},{4,0},{8,12},{12,8},{16,20},{20,16},{24,28},{28,24},{1,5},{5... | collective-permute-start | bytes 49160 | tf_op jit(solution)/shard_map/ppermute | solution.py:212
  44.5 0.8 %collective-permute-done.7.second_ref = f32[1,32,128]{2,1,0:T(8,128)S(1)} collective-permute-done((f32[1,32,128]{2,1,0:T(8,128)S(1)}, f32[1,32,128]{2,1,0:T(8,128)S(1)}, u32[]{:S(2)}, u32[]{:S(2)}) %collective-permute-start.7) | collective-permute-done | bytes 16416 | tf_op jit(solution)/shard_map/ppermute | solution.py:212
  45.3 0.7 %collective-permute-start.8 = (f32[2,32,128]{2,1,0:T(8,128)S(1)}, f32[2,32,128]{2,1,0:T(8,128)S(1)}, u32[]{:S(2)}, u32[]{:S(2)}) collective-permute-start(f32[2,32,128]{2,1,0:T(8,128)S(1)} %join_cols.3.first_ref), channel_id=1, source_target_pairs={{0,8},{4,12},{8,0},{12,4},{16,24},{20,28},{24,16},{28,20},{1,9},{5... | collective-permute-start | bytes 98312 | tf_op jit(solution)/shard_map/ppermute | solution.py:212
  46.0 2.4 %collective-permute-done.8.second_ref = f32[2,32,128]{2,1,0:T(8,128)S(1)} collective-permute-done((f32[2,32,128]{2,1,0:T(8,128)S(1)}, f32[2,32,128]{2,1,0:T(8,128)S(1)}, u32[]{:S(2)}, u32[]{:S(2)}) %collective-permute-start.8) | collective-permute-done | bytes 32800 | tf_op jit(solution)/shard_map/ppermute | solution.py:212
  48.4 0.2 collective-permute-start.9
  48.6 0.0 copy-done.1
  48.6 3.1 %far_field_of_leaves.1.field_ref = f32[512,128]{1,0:T(8,128)S(1)} custom-call(s32[8,16]{1,0:T(8,128)S(1)} %bitcast.4, s32[4,16]{1,0:T(4,128)S(1)} %bitcast.3, f32[16,8,32,32]{3,2,1,0:T(8,128)} %coupling_in.1, f32[560,128]{1,0:T(8,128)S(1)} %convert_element_type.23.low_ref, f32[512,128]{1,0:T(8,128)S(1)} %get-tuple-element.52.own_ref, ...), custom_call_target="tpu_custom_call" | custom-call | tf_op jit(solution)/shard_map/far_field_of_leaves/pallas_call | solution.py:259
  51.7 0.1 collective-permute-done.9.second_ref
  51.8 0.0 copy-done.2
  51.8 0.0 copy-done.3
  51.8 2.0 %fields_down.1.acc_in = f32[4096,128]{1,0:T(8,128)S(1)} custom-call(s32[1,4]{1,0:T(1,128)S(1)} %copy-done.2, s32[1,8]{1,0:T(1,128)S(1)} %copy-done.3, f32[4,32,128]{2,1,0:T(8,128)S(1)} %get-tuple-element.47.stack_ref, f32[8,32,128]{2,1,0:T(8,128)S(1)} %join_cols.5.cols_ref, f32[1,4,32,32]{3,2,1,0:T(8,128)S(1)} %get-tuple-element.49.coupling_ref, ...), custom_call_target="tpu_custom_call" | custom-call | tf_op jit(solution)/shard_map/fields_down/pallas_call | solution.py:398
  53.9 0.0 collective-permute-done.5.low_ref
  53.9 2.0 %near_low_first.1 = (f32[4096,128]{1,0:T(8,128)S(1)}, bf16[4096,128]{1,0:T(8,128)(2,1)}) custom-call(s32[160,128]{1,0:T(8,128)S(1)} %get-tuple-element.35.list_ref, s32[8,128]{1,0:T(8,128)S(1)} %get-tuple-element.36.found_ref, bf16[16,4,256,256]{3,2,1,0:T(8,128)(2,1)S(1)} %load_near_blocks.1.blocks_ref, ...), custom_call_target="tpu_custom_call", output_to_operand_aliasing={{0}: (4, {})} | custom-call | tf_op jit(solution)/shard_map/near_low_first/pallas_call | solution.py:467
  55.9 2.2 %collective-permute-done.4.low_ref = bf16[2048,128]{1,0:T(8,128)(2,1)S(1)} collective-permute-done((bf16[2048,128]{1,0:T(8,128)(2,1)S(1)}, bf16[2048,128]{1,0:T(8,128)(2,1)S(1)}, u32[]{:S(2)}, u32[]{:S(2)}) %collective-permute-start.4) | collective-permute-done | bytes 524320 | tf_op jit(solution)/shard_map/ppermute | solution.py:37
  58.1 1.9 %near_low_second.1 = bf16[4096,128]{1,0:T(8,128)(2,1)} custom-call(s32[160,128]{1,0:T(8,128)S(1)} %get-tuple-element.35.list_ref, s32[8,128]{1,0:T(8,128)S(1)} %get-tuple-element.36.found_ref, bf16[16,4,256,256]{3,2,1,0:T(8,128)(2,1)S(1)} %load_near_blocks.1.blocks_ref, ...), custom_call_target="tpu_custom_call", output_to_operand_aliasing={{}: (5, {})} | custom-call | tf_op jit(solution)/shard_map/near_low_second/pallas_call | solution.py:493
  (11 shorter events, 0.1 us)
Async XLA Ops:
  0.0 24.2 %collective-permute-start = (bf16[4096,128]{1,0:T(8,128)(2,1)}, bf16[4096,128]{1,0:T(8,128)(2,1)S(1)}, u32[]{:S(2)}, u32[]{:S(2)}) collective-permute-start(bf16[4096,128]{1,0:T(8,128)(2,1)} %refs_0_.1), channel_id=1, source_target_pairs={{1,0},{2,1},{3,2},{4,3},{5,4},{6,5},{7,6},{8,7},{9,8},{10,9},{11,1... | collective-permute-start | bytes 3145736 | tf_op jit(solution)/shard_map/ppermute | solution.py:37
  4.2 28.1 %collective-permute-start.2 = (f16[560,128]{1,0:T(8,128)(2,1)S(1)}, f16[560,128]{1,0:T(8,128)(2,1)S(1)}, u32[]{:S(2)}, u32[]{:S(2)}) collective-permute-start(f16[560,128]{1,0:T(8,128)(2,1)S(1)} %convert_element_type.21), channel_id=1, source_target_pairs={{0,1},{1,2},{2,3},{3,4},{4,5},{5,6},{6,7},{7,8},{8,9},{9,10},{10,1... | collective-permute-start | bytes 430088 | tf_op jit(solution)/shard_map/ppermute | solution.py:42
  4.3 28.1 %collective-permute-start.3 = (f16[560,128]{1,0:T(8,128)(2,1)S(1)}, f16[560,128]{1,0:T(8,128)(2,1)S(1)}, u32[]{:S(2)}, u32[]{:S(2)}) collective-permute-start(f16[560,128]{1,0:T(8,128)(2,1)S(1)} %convert_element_type.21), channel_id=1, source_target_pairs={{0,31},{1,0},{2,1},{3,2},{4,3},{5,4},{6,5},{7,6},{8,7},{9,8},{10,9... | collective-permute-start | bytes 430088 | tf_op jit(solution)/shard_map/ppermute | solution.py:42
  5.7 26.1 %collective-permute-start.1 = (f16[48,128]{1,0:T(8,128)(2,1)S(1)}, f16[48,128]{1,0:T(8,128)(2,1)S(1)}, u32[]{:S(2)}, u32[]{:S(2)}) collective-permute-start(f16[48,128]{1,0:T(8,128)(2,1)S(1)} %convert_element_type.22), channel_id=1, source_target_pairs={{0,2},{1,3},{2,0},{3,1},{4,6},{5,7},{6,4},{7,5},{8,10},{9,11},{10,... | collective-permute-start | bytes 36872 | tf_op jit(solution)/shard_map/ppermute | solution.py:183
  8.2 16.0 %copy-start = (s32[16,4]{0,1:T(4,128)S(1)}, s32[16,4]{0,1:T(4,128)}, u32[]{:S(2)}) copy-start(s32[16,4]{0,1:T(4,128)} %param.14) | copy-start | bytes 772
  8.2 45.6 %collective-permute-start.5 = (bf16[2064,128]{1,0:T(8,128)(2,1)S(1)}, bf16[2064,128]{1,0:T(8,128)(2,1)S(1)}, u32[]{:S(2)}, u32[]{:S(2)}) collective-permute-start(bf16[2064,128]{1,0:T(8,128)(2,1)S(1)} %get-tuple-element.41), channel_id=1, source_target_pairs={{0,1},{1,2},{2,3},{3,4},{4,5},{5,6},{6,7},{7,8},{8,9},{9,10},{10,1... | collective-permute-start | bytes 1585160 | tf_op jit(solution)/shard_map/ppermute | solution.py:37
  28.3 20.4 %copy-start.1 = (s32[16,8]{0,1:T(8,128)S(1)}, s32[16,8]{0,1:T(8,128)}, u32[]{:S(2)}) copy-start(s32[16,8]{0,1:T(8,128)} %param.18) | copy-start | bytes 1540
  32.4 25.8 %collective-permute-start.4 = (bf16[2048,128]{1,0:T(8,128)(2,1)S(1)}, bf16[2048,128]{1,0:T(8,128)(2,1)S(1)}, u32[]{:S(2)}, u32[]{:S(2)}) collective-permute-start(bf16[2048,128]{1,0:T(8,128)(2,1)S(1)} %get-tuple-element.40), channel_id=1, source_target_pairs={{0,1},{1,2},{2,3},{3,4},{4,5},{5,6},{6,7},{7,8},{8,9},{9,10},{10,1... | collective-permute-start | bytes 1572872 | tf_op jit(solution)/shard_map/ppermute | solution.py:37
  33.7 7.7 %collective-permute-start.6 = (f16[48,128]{1,0:T(8,128)(2,1)S(1)}, f16[48,128]{1,0:T(8,128)(2,1)S(1)}, u32[]{:S(2)}, u32[]{:S(2)}) collective-permute-start(f16[48,128]{1,0:T(8,128)(2,1)S(1)} %convert_element_type.26), channel_id=1, source_target_pairs={{0,28},{3,7},{4,0},{7,11},{8,4},{11,15},{12,8},{15,19},{16,12},{19... | collective-permute-start | bytes 36872 | tf_op jit(solution)/shard_map/ppermute | solution.py:202
  41.4 10.4 %copy-start.2 = (s32[1,4]{1,0:T(1,128)S(1)}, s32[1,4]{1,0:T(1,128)}, u32[]{:S(2)}) copy-start(s32[1,4]{1,0:T(1,128)} %partner_ref.1) | copy-start | bytes 52
  41.4 10.4 %copy-start.3 = (s32[1,8]{1,0:T(1,128)S(1)}, s32[1,8]{1,0:T(1,128)}, u32[]{:S(2)}) copy-start(s32[1,8]{1,0:T(1,128)} %top_partner_ref.1) | copy-start | bytes 100
  42.0 3.3 %collective-permute-start.7 = (f32[1,32,128]{2,1,0:T(8,128)S(1)}, f32[1,32,128]{2,1,0:T(8,128)S(1)}, u32[]{:S(2)}, u32[]{:S(2)}) collective-permute-start(f32[1,32,128]{2,1,0:T(8,128)S(1)} %get-tuple-element.48.first_ref), channel_id=1, source_target_pairs={{0,4},{4,0},{8,12},{12,8},{16,20},{20,16},{24,28},{28,24},{1,5},{5... | collective-permute-start | bytes 49160 | tf_op jit(solution)/shard_map/ppermute | solution.py:212
  45.3 3.1 %collective-permute-start.8 = (f32[2,32,128]{2,1,0:T(8,128)S(1)}, f32[2,32,128]{2,1,0:T(8,128)S(1)}, u32[]{:S(2)}, u32[]{:S(2)}) collective-permute-start(f32[2,32,128]{2,1,0:T(8,128)S(1)} %join_cols.3.first_ref), channel_id=1, source_target_pairs={{0,8},{4,12},{8,0},{12,4},{16,24},{20,28},{24,16},{28,20},{1,9},{5... | collective-permute-start | bytes 98312 | tf_op jit(solution)/shard_map/ppermute | solution.py:212
  48.4 3.4 %collective-permute-start.9 = (f32[4,32,128]{2,1,0:T(8,128)S(1)}, f32[4,32,128]{2,1,0:T(8,128)S(1)}, u32[]{:S(2)}, u32[]{:S(2)}) collective-permute-start(f32[4,32,128]{2,1,0:T(8,128)S(1)} %join_cols.4.first_ref), channel_id=1, source_target_pairs={{0,16},{4,20},{8,24},{12,28},{16,0},{20,4},{24,8},{28,12},{1,17},{... | collective-permute-start | bytes 196616 | tf_op jit(solution)/shard_map/ppermute | solution.py:212

commit v9 on v8

--- a/solution.py
+++ b/solution.py
@@ -11,7 +11,7 @@
 BOTH = ("col", "sub")
 SPARE = 16
 TAIL = 8
-GROUP = 4
+GROUP = 6
 BATCH = 8
 VMEM = pl.BlockSpec(memory_space=pltpu.VMEM)
 SMEM = pl.BlockSpec(memory_space=pltpu.SMEM)

time: 60.6 us -> 60.5 us (level)
  no operation moved by 1% of the time
where the time goes in v9:
time: 60.5 us; the launch traced here: 59.9 us
  waiting for transfers between devices  24.5 us (40%)
  Pallas kernels  19 us (31%)
  starting transfers between devices  16.1 us (27%)
    ppermute x3, waiting for transfers between devices, shift(): return lax.ppermute(value, BOTH, pairs)  13.3 us
    ppermute x3, starting transfers between devices, shift(): return lax.ppermute(value, BOTH, pairs)  4.82 us
    pallas_call x1, Pallas kernels, near(): pl.pallas_call(near_body, in_specs=[SMEM] + [VMEM] * 3, out_specs=[VMEM]...  4.07 us
    ppermute x1, starting transfers between devices, around(): return lax.ppermute(onward.astype(jnp.float16), BOTH, pairs)  3.85 us
    ppermute x1, waiting for transfers between devices, around(): return lax.ppermute(onward.astype(jnp.float16), BOTH, pairs)  3.83 us
    ppermute x1, waiting for transfers between devices, gather_sub(): lax.ppermute(value, 'sub', [(i, (i + step) % count) for i in range(count)])  3.54 us
    ppermute x3, starting transfers between devices, gather_col(): value = join(value, lax.ppermute(value, 'col', pairs))  3.4 us
    pallas_call x1, Pallas kernels, load(): pl.pallas_call(load_body, in_specs=[HBM], out_specs=VMEM, out_shape=pltpu...  3.39 us
  transfers between devices with their start and end apart: 10, of which 8 were waited for; matrix products, arithmetic and copies ran while one was open for 0% of the time, Pallas kernels for 29%

profile of v9, /device:TPU:31, one launch (start us, length us, event | category | flops | bytes accessed | tf_op | source)
XLA Modules:
  0.0 59.9 jit_solution(6907300309798806886)
XLA Ops:
  0.0 2.1 %collective-permute-start = (bf16[4096,128]{1,0:T(8,128)(2,1)}, bf16[4096,128]{1,0:T(8,128)(2,1)S(1)}, u32[]{:S(2)}, u32[]{:S(2)}) collective-permute-start(bf16[4096,128]{1,0:T(8,128)(2,1)} %refs_0_.1), channel_id=1, source_target_pairs={{1,0},{2,1},{3,2},{4,3},{5,4},{6,5},{7,6},{8,7},{9,8},{10,9},{11,1... | collective-permute-start | bytes 3145736 | tf_op jit(solution)/shard_map/ppermute | solution.py:37
  2.1 2.0 %leaf_and_cluster_coefs.1 = (bf16[4096,128]{1,0:T(8,128)(2,1)S(1)}, bf16[16,32,256]{2,1,0:T(8,128)(2,1)S(1)}, f32[16,32,32]{2,1,0:T(8,128)S(1)}, f32[1,32,32]{2,...) custom-call(bf16[4096,128]{1,0:T(8,128)(2,1)} %refs_0_.1, ...), custom_call_target="tpu_custom_call" | custom-call | tf_op jit(solution)/shard_map/leaf_and_cluster_coefs/pallas_call | solution.py:109
  4.2 0.1 collective-permute-start.2
  4.3 1.5 %collective-permute-start.3 = (f16[560,128]{1,0:T(8,128)(2,1)S(1)}, f16[560,128]{1,0:T(8,128)(2,1)S(1)}, u32[]{:S(2)}, u32[]{:S(2)}) collective-permute-start(f16[560,128]{1,0:T(8,128)(2,1)S(1)} %convert_element_type.21), channel_id=1, source_target_pairs={{0,31},{1,0},{2,1},{3,2},{4,3},{5,4},{6,5},{7,6},{8,7},{9,8},{10,9... | collective-permute-start | bytes 430088 | tf_op jit(solution)/shard_map/ppermute | solution.py:42
  5.7 2.5 %collective-permute-start.1 = (f16[48,128]{1,0:T(8,128)(2,1)S(1)}, f16[48,128]{1,0:T(8,128)(2,1)S(1)}, u32[]{:S(2)}, u32[]{:S(2)}) collective-permute-start(f16[48,128]{1,0:T(8,128)(2,1)S(1)} %convert_element_type.22), channel_id=1, source_target_pairs={{0,2},{1,3},{2,0},{3,1},{4,6},{5,7},{6,4},{7,5},{8,10},{9,11},{10,... | collective-permute-start | bytes 36872 | tf_op jit(solution)/shard_map/ppermute | solution.py:183
  8.2 0.0 copy-start
  8.2 1.4 %collective-permute-start.5 = (bf16[2064,128]{1,0:T(8,128)(2,1)S(1)}, bf16[2064,128]{1,0:T(8,128)(2,1)S(1)}, u32[]{:S(2)}, u32[]{:S(2)}) collective-permute-start(bf16[2064,128]{1,0:T(8,128)(2,1)S(1)} %get-tuple-element.41), channel_id=1, source_target_pairs={{0,1},{1,2},{2,3},{3,4},{4,5},{5,6},{6,7},{7,8},{8,9},{9,10},{10,1... | collective-permute-start | bytes 1585160 | tf_op jit(solution)/shard_map/ppermute | solution.py:37
  9.7 3.4 %load_near_blocks.1.blocks_ref = bf16[16,4,256,256]{3,2,1,0:T(8,128)(2,1)S(1)} custom-call(bf16[16,4,256,256]{3,2,1,0:T(8,128)(2,1)} %blocks_ref), custom_call_target="tpu_custom_call" | custom-call | tf_op jit(solution)/shard_map/load_near_blocks/pallas_call | solution.py:280
  13.1 11.1 %collective-permute-done.high_ref = bf16[4096,128]{1,0:T(8,128)(2,1)S(1)} collective-permute-done((bf16[4096,128]{1,0:T(8,128)(2,1)}, bf16[4096,128]{1,0:T(8,128)(2,1)S(1)}, u32[]{:S(2)}, u32[]{:S(2)}) %collective-permute-start) | collective-permute-done | bytes 1048608 | tf_op jit(solution)/shard_map/ppermute | solution.py:37
  24.2 0.0 copy-done
  24.2 4.1 %near_own_and_high.1 = (f32[4096,128]{1,0:T(8,128)S(1)}, s32[160,128]{1,0:T(8,128)S(1)}, s32[8,128]{1,0:T(8,128)S(1)}) custom-call(s32[4,16]{1,0:T(4,128)S(1)} %bitcast.2, bf16[16,4,256,256]{3,2,1,0:T(8,128)(2,1)S(1)} %load_near_blocks.1.blocks_ref, bf16[4096,128]{1,0:T(8,128)(2,1)S(1)} %get-tuple-element.34.own_ref, ...), custom_call_target="tpu_custom_call" | custom-call | tf_op jit(solution)/shard_map/near_own_and_high/pallas_call | solution.py:349
  28.3 0.0 copy-start.1
  28.3 3.5 %collective-permute-done.1 = f16[48,128]{1,0:T(8,128)(2,1)S(1)} collective-permute-done((f16[48,128]{1,0:T(8,128)(2,1)S(1)}, f16[48,128]{1,0:T(8,128)(2,1)S(1)}, u32[]{:S(2)}, u32[]{:S(2)}) %collective-permute-start.1) | collective-permute-done | bytes 12320 | tf_op jit(solution)/shard_map/ppermute | solution.py:183
  31.8 0.5 collective-permute-done.2
  32.3 0.0 collective-permute-done.3
  32.4 1.3 %collective-permute-start.4 = (bf16[2048,128]{1,0:T(8,128)(2,1)S(1)}, bf16[2048,128]{1,0:T(8,128)(2,1)S(1)}, u32[]{:S(2)}, u32[]{:S(2)}) collective-permute-start(bf16[2048,128]{1,0:T(8,128)(2,1)S(1)} %get-tuple-element.40), channel_id=1, source_target_pairs={{0,1},{1,2},{2,3},{3,4},{4,5},{5,6},{6,7},{7,8},{8,9},{9,10},{10,1... | collective-permute-start | bytes 1572872 | tf_op jit(solution)/shard_map/ppermute | solution.py:37
  33.7 3.8 %collective-permute-start.6 = (f16[48,128]{1,0:T(8,128)(2,1)S(1)}, f16[48,128]{1,0:T(8,128)(2,1)S(1)}, u32[]{:S(2)}, u32[]{:S(2)}) collective-permute-start(f16[48,128]{1,0:T(8,128)(2,1)S(1)} %convert_element_type.26), channel_id=1, source_target_pairs={{0,28},{3,7},{4,0},{7,11},{8,4},{11,15},{12,8},{15,19},{16,12},{19... | collective-permute-start | bytes 36872 | tf_op jit(solution)/shard_map/ppermute | solution.py:202
  37.6 3.8 %collective-permute-done.6 = f16[48,128]{1,0:T(8,128)(2,1)S(1)} collective-permute-done((f16[48,128]{1,0:T(8,128)(2,1)S(1)}, f16[48,128]{1,0:T(8,128)(2,1)S(1)}, u32[]{:S(2)}, u32[]{:S(2)}) %collective-permute-start.6) | collective-permute-done | bytes 12320 | tf_op jit(solution)/shard_map/ppermute | solution.py:202
  41.4 0.0 copy-start.2
  41.4 0.0 copy-start.3
  41.4 0.6 sums_over_sub.1
  42.0 2.5 %collective-permute-start.7 = (f32[1,32,128]{2,1,0:T(8,128)S(1)}, f32[1,32,128]{2,1,0:T(8,128)S(1)}, u32[]{:S(2)}, u32[]{:S(2)}) collective-permute-start(f32[1,32,128]{2,1,0:T(8,128)S(1)} %get-tuple-element.48.first_ref), channel_id=1, source_target_pairs={{0,4},{4,0},{8,12},{12,8},{16,20},{20,16},{24,28},{28,24},{1,5},{5... | collective-permute-start | bytes 49160 | tf_op jit(solution)/shard_map/ppermute | solution.py:212
  44.5 0.8 %collective-permute-done.7.second_ref = f32[1,32,128]{2,1,0:T(8,128)S(1)} collective-permute-done((f32[1,32,128]{2,1,0:T(8,128)S(1)}, f32[1,32,128]{2,1,0:T(8,128)S(1)}, u32[]{:S(2)}, u32[]{:S(2)}) %collective-permute-start.7) | collective-permute-done | bytes 16416 | tf_op jit(solution)/shard_map/ppermute | solution.py:212
  45.3 0.7 %collective-permute-start.8 = (f32[2,32,128]{2,1,0:T(8,128)S(1)}, f32[2,32,128]{2,1,0:T(8,128)S(1)}, u32[]{:S(2)}, u32[]{:S(2)}) collective-permute-start(f32[2,32,128]{2,1,0:T(8,128)S(1)} %join_cols.3.first_ref), channel_id=1, source_target_pairs={{0,8},{4,12},{8,0},{12,4},{16,24},{20,28},{24,16},{28,20},{1,9},{5... | collective-permute-start | bytes 98312 | tf_op jit(solution)/shard_map/ppermute | solution.py:212
  46.0 2.4 %collective-permute-done.8.second_ref = f32[2,32,128]{2,1,0:T(8,128)S(1)} collective-permute-done((f32[2,32,128]{2,1,0:T(8,128)S(1)}, f32[2,32,128]{2,1,0:T(8,128)S(1)}, u32[]{:S(2)}, u32[]{:S(2)}) %collective-permute-start.8) | collective-permute-done | bytes 32800 | tf_op jit(solution)/shard_map/ppermute | solution.py:212
  48.4 0.2 collective-permute-start.9
  48.6 0.0 copy-done.1
  48.6 3.1 %far_field_of_leaves.1.field_ref = f32[512,128]{1,0:T(8,128)S(1)} custom-call(s32[8,16]{1,0:T(8,128)S(1)} %bitcast.4, s32[4,16]{1,0:T(4,128)S(1)} %bitcast.3, f32[16,8,32,32]{3,2,1,0:T(8,128)} %coupling_in.1, f32[560,128]{1,0:T(8,128)S(1)} %convert_element_type.23.low_ref, f32[512,128]{1,0:T(8,128)S(1)} %get-tuple-element.52.own_ref, ...), custom_call_target="tpu_custom_call" | custom-call | tf_op jit(solution)/shard_map/far_field_of_leaves/pallas_call | solution.py:259
  51.7 0.1 collective-permute-done.9.second_ref
  51.8 0.0 copy-done.2
  51.8 0.0 copy-done.3
  51.8 2.0 %fields_down.1.acc_in = f32[4096,128]{1,0:T(8,128)S(1)} custom-call(s32[1,4]{1,0:T(1,128)S(1)} %copy-done.2, s32[1,8]{1,0:T(1,128)S(1)} %copy-done.3, f32[4,32,128]{2,1,0:T(8,128)S(1)} %get-tuple-element.47.stack_ref, f32[8,32,128]{2,1,0:T(8,128)S(1)} %join_cols.5.cols_ref, f32[1,4,32,32]{3,2,1,0:T(8,128)S(1)} %get-tuple-element.49.coupling_ref, ...), custom_call_target="tpu_custom_call" | custom-call | tf_op jit(solution)/shard_map/fields_down/pallas_call | solution.py:398
  53.9 0.0 collective-permute-done.5.low_ref
  53.9 2.0 %near_low_first.1 = (f32[4096,128]{1,0:T(8,128)S(1)}, bf16[4096,128]{1,0:T(8,128)(2,1)}) custom-call(s32[160,128]{1,0:T(8,128)S(1)} %get-tuple-element.35.list_ref, s32[8,128]{1,0:T(8,128)S(1)} %get-tuple-element.36.found_ref, bf16[16,4,256,256]{3,2,1,0:T(8,128)(2,1)S(1)} %load_near_blocks.1.blocks_ref, ...), custom_call_target="tpu_custom_call", output_to_operand_aliasing={{0}: (4, {})} | custom-call | tf_op jit(solution)/shard_map/near_low_first/pallas_call | solution.py:467
  55.9 2.2 %collective-permute-done.4.low_ref = bf16[2048,128]{1,0:T(8,128)(2,1)S(1)} collective-permute-done((bf16[2048,128]{1,0:T(8,128)(2,1)S(1)}, bf16[2048,128]{1,0:T(8,128)(2,1)S(1)}, u32[]{:S(2)}, u32[]{:S(2)}) %collective-permute-start.4) | collective-permute-done | bytes 524320 | tf_op jit(solution)/shard_map/ppermute | solution.py:37
  58.1 1.8 %near_low_second.1 = bf16[4096,128]{1,0:T(8,128)(2,1)} custom-call(s32[160,128]{1,0:T(8,128)S(1)} %get-tuple-element.35.list_ref, s32[8,128]{1,0:T(8,128)S(1)} %get-tuple-element.36.found_ref, bf16[16,4,256,256]{3,2,1,0:T(8,128)(2,1)S(1)} %load_near_blocks.1.blocks_ref, ...), custom_call_target="tpu_custom_call", output_to_operand_aliasing={{}: (5, {})} | custom-call | tf_op jit(solution)/shard_map/near_low_second/pallas_call | solution.py:493
  (11 shorter events, 0.1 us)
Async XLA Ops:
  0.0 24.2 %collective-permute-start = (bf16[4096,128]{1,0:T(8,128)(2,1)}, bf16[4096,128]{1,0:T(8,128)(2,1)S(1)}, u32[]{:S(2)}, u32[]{:S(2)}) collective-permute-start(bf16[4096,128]{1,0:T(8,128)(2,1)} %refs_0_.1), channel_id=1, source_target_pairs={{1,0},{2,1},{3,2},{4,3},{5,4},{6,5},{7,6},{8,7},{9,8},{10,9},{11,1... | collective-permute-start | bytes 3145736 | tf_op jit(solution)/shard_map/ppermute | solution.py:37
  4.2 28.1 %collective-permute-start.2 = (f16[560,128]{1,0:T(8,128)(2,1)S(1)}, f16[560,128]{1,0:T(8,128)(2,1)S(1)}, u32[]{:S(2)}, u32[]{:S(2)}) collective-permute-start(f16[560,128]{1,0:T(8,128)(2,1)S(1)} %convert_element_type.21), channel_id=1, source_target_pairs={{0,1},{1,2},{2,3},{3,4},{4,5},{5,6},{6,7},{7,8},{8,9},{9,10},{10,1... | collective-permute-start | bytes 430088 | tf_op jit(solution)/shard_map/ppermute | solution.py:42
  4.3 28.1 %collective-permute-start.3 = (f16[560,128]{1,0:T(8,128)(2,1)S(1)}, f16[560,128]{1,0:T(8,128)(2,1)S(1)}, u32[]{:S(2)}, u32[]{:S(2)}) collective-permute-start(f16[560,128]{1,0:T(8,128)(2,1)S(1)} %convert_element_type.21), channel_id=1, source_target_pairs={{0,31},{1,0},{2,1},{3,2},{4,3},{5,4},{6,5},{7,6},{8,7},{9,8},{10,9... | collective-permute-start | bytes 430088 | tf_op jit(solution)/shard_map/ppermute | solution.py:42
  5.7 26.1 %collective-permute-start.1 = (f16[48,128]{1,0:T(8,128)(2,1)S(1)}, f16[48,128]{1,0:T(8,128)(2,1)S(1)}, u32[]{:S(2)}, u32[]{:S(2)}) collective-permute-start(f16[48,128]{1,0:T(8,128)(2,1)S(1)} %convert_element_type.22), channel_id=1, source_target_pairs={{0,2},{1,3},{2,0},{3,1},{4,6},{5,7},{6,4},{7,5},{8,10},{9,11},{10,... | collective-permute-start | bytes 36872 | tf_op jit(solution)/shard_map/ppermute | solution.py:183
  8.2 16.0 %copy-start = (s32[16,4]{0,1:T(4,128)S(1)}, s32[16,4]{0,1:T(4,128)}, u32[]{:S(2)}) copy-start(s32[16,4]{0,1:T(4,128)} %param.14) | copy-start | bytes 772
  8.2 45.6 %collective-permute-start.5 = (bf16[2064,128]{1,0:T(8,128)(2,1)S(1)}, bf16[2064,128]{1,0:T(8,128)(2,1)S(1)}, u32[]{:S(2)}, u32[]{:S(2)}) collective-permute-start(bf16[2064,128]{1,0:T(8,128)(2,1)S(1)} %get-tuple-element.41), channel_id=1, source_target_pairs={{0,1},{1,2},{2,3},{3,4},{4,5},{5,6},{6,7},{7,8},{8,9},{9,10},{10,1... | collective-permute-start | bytes 1585160 | tf_op jit(solution)/shard_map/ppermute | solution.py:37
  28.3 20.3 %copy-start.1 = (s32[16,8]{0,1:T(8,128)S(1)}, s32[16,8]{0,1:T(8,128)}, u32[]{:S(2)}) copy-start(s32[16,8]{0,1:T(8,128)} %param.18) | copy-start | bytes 1540
  32.4 25.8 %collective-permute-start.4 = (bf16[2048,128]{1,0:T(8,128)(2,1)S(1)}, bf16[2048,128]{1,0:T(8,128)(2,1)S(1)}, u32[]{:S(2)}, u32[]{:S(2)}) collective-permute-start(bf16[2048,128]{1,0:T(8,128)(2,1)S(1)} %get-tuple-element.40), channel_id=1, source_target_pairs={{0,1},{1,2},{2,3},{3,4},{4,5},{5,6},{6,7},{7,8},{8,9},{9,10},{10,1... | collective-permute-start | bytes 1572872 | tf_op jit(solution)/shard_map/ppermute | solution.py:37
  33.7 7.7 %collective-permute-start.6 = (f16[48,128]{1,0:T(8,128)(2,1)S(1)}, f16[48,128]{1,0:T(8,128)(2,1)S(1)}, u32[]{:S(2)}, u32[]{:S(2)}) collective-permute-start(f16[48,128]{1,0:T(8,128)(2,1)S(1)} %convert_element_type.26), channel_id=1, source_target_pairs={{0,28},{3,7},{4,0},{7,11},{8,4},{11,15},{12,8},{15,19},{16,12},{19... | collective-permute-start | bytes 36872 | tf_op jit(solution)/shard_map/ppermute | solution.py:202
  41.4 10.4 %copy-start.2 = (s32[1,4]{1,0:T(1,128)S(1)}, s32[1,4]{1,0:T(1,128)}, u32[]{:S(2)}) copy-start(s32[1,4]{1,0:T(1,128)} %partner_ref.1) | copy-start | bytes 52
  41.4 10.4 %copy-start.3 = (s32[1,8]{1,0:T(1,128)S(1)}, s32[1,8]{1,0:T(1,128)}, u32[]{:S(2)}) copy-start(s32[1,8]{1,0:T(1,128)} %top_partner_ref.1) | copy-start | bytes 100
  42.0 3.3 %collective-permute-start.7 = (f32[1,32,128]{2,1,0:T(8,128)S(1)}, f32[1,32,128]{2,1,0:T(8,128)S(1)}, u32[]{:S(2)}, u32[]{:S(2)}) collective-permute-start(f32[1,32,128]{2,1,0:T(8,128)S(1)} %get-tuple-element.48.first_ref), channel_id=1, source_target_pairs={{0,4},{4,0},{8,12},{12,8},{16,20},{20,16},{24,28},{28,24},{1,5},{5... | collective-permute-start | bytes 49160 | tf_op jit(solution)/shard_map/ppermute | solution.py:212
  45.3 3.1 %collective-permute-start.8 = (f32[2,32,128]{2,1,0:T(8,128)S(1)}, f32[2,32,128]{2,1,0:T(8,128)S(1)}, u32[]{:S(2)}, u32[]{:S(2)}) collective-permute-start(f32[2,32,128]{2,1,0:T(8,128)S(1)} %join_cols.3.first_ref), channel_id=1, source_target_pairs={{0,8},{4,12},{8,0},{12,4},{16,24},{20,28},{24,16},{28,20},{1,9},{5... | collective-permute-start | bytes 98312 | tf_op jit(solution)/shard_map/ppermute | solution.py:212
  48.4 3.4 %collective-permute-start.9 = (f32[4,32,128]{2,1,0:T(8,128)S(1)}, f32[4,32,128]{2,1,0:T(8,128)S(1)}, u32[]{:S(2)}, u32[]{:S(2)}) collective-permute-start(f32[4,32,128]{2,1,0:T(8,128)S(1)} %join_cols.4.first_ref), channel_id=1, source_target_pairs={{0,16},{4,20},{8,24},{12,28},{16,0},{20,4},{24,8},{28,12},{1,17},{... | collective-permute-start | bytes 196616 | tf_op jit(solution)/shard_map/ppermute | solution.py:212
